TPU v7x, 32 devices: a whole 2x2x4 slice. The times are simulated.
32 devices in a mesh: outer: 4 (over x, core), inner: 8 (over z, y).
Axes of the slice: x: 2, y: 2, z: 4, core: 2. Of those that a mesh axis runs over, the one named last changes fastest.
Arguments:
- features: bfloat16 [12288, 512], P(('outer', 'inner')), may hold values from -6 to 6
- adj_tiles: bfloat16 [576, 128, 128], P(('outer', 'inner')), may hold values from 0 to 0.0625
- tile_src: int32 [96, 6], P(('outer', 'inner')), may hold values from 0 to 11, as said below
- send_rows: int32 [256, 128], P(('outer', 'inner')), may hold values from 0 to 383
- send_count: int32 [32, 8], P(('outer', 'inner')), may hold values from 1 to 128, as said below
- hub_rows: int32 [128], P(('outer', 'inner')), may hold values from 0 to 383, as said below
- w_self: float32 [512, 512], replicated, may hold values from -0.25 to 0.25
- w_neigh: float32 [512, 512], replicated, may hold values from -0.25 to 0.25
- out_bias: float32 [512], replicated, may hold values from -3 to 3
- cotangent: bfloat16 [12288, 512], P(('outer', 'inner')), may hold values from -6 to 6
Outputs:
- hidden_out: bfloat16 [12288, 512], P(('outer', 'inner'))
- grad_features: bfloat16 [12288, 512], P(('outer', 'inner'))
- grad_w_self: float32 [512, 512], replicated
- grad_w_neigh: float32 [512, 512], replicated
- grad_bias: float32 [512], replicated
Inputs may be any that keep to these rules, and one draw needn't show every extreme that they name: `tile_src`: each partition's 3 * 6 tile slots name every one of its 12 source tiles at least once. `send_count`: on every partition one partner's count is exactly 128. `hub_rows`: the 4 hub rows of one partition are distinct.
All inputs are finite; a program needn't handle non-finite values.
Results may differ from a plain program's by a relative error of at most 0.0067.
Values may be sent and summed in bfloat16 or wider, within the bound.
No kernel may reach another device: no remote copies, remote signals or barrier semaphores. Data moves between devices by JAX's collectives and lax.ppermute only.
A program may use at most 128 MiB of HBM per device.

v0:
```python
import jax
import jax.numpy as jnp
from jax import lax
from jax.sharding import PartitionSpec as P


def body(
    features,
    adj_tiles,
    tile_src,
    send_rows,
    send_count,
    hub_rows,
    w_self,
    w_neigh,
    out_bias,
    cotangent,
):
    ndevice = lax.axis_size("outer") * lax.axis_size("inner")
    groupsize = lax.axis_size("inner")
    nrows, width = features.shape
    tilerows = adj_tiles.shape[1]
    nblocks, per_block = tile_src.shape
    nhubs = hub_rows.shape[0] * ndevice
    nbound = groupsize * tilerows
    ntiles = nblocks + groupsize + nhubs // tilerows
    self_low = w_self.astype(jnp.bfloat16)
    neigh_low = w_neigh.astype(jnp.bfloat16)
    slot_lane = jnp.arange(tilerows, dtype=jnp.int32)
    row_mask = slot_lane[None, :] < send_count[0][:, None]
    outgoing = jnp.where(row_mask[..., None], features[send_rows], jnp.zeros((), jnp.bfloat16))
    received = lax.all_to_all(outgoing, "inner", split_axis=0, concat_axis=0, tiled=True)
    hub_feats = lax.all_gather(features[hub_rows], ("outer", "inner"), axis=0, tiled=True)
    source = jnp.concatenate([features, received.reshape(nbound, width), hub_feats], 0)
    source = source.reshape(ntiles, tilerows, width)
    weights = adj_tiles.reshape(nblocks, per_block, tilerows, tilerows)
    aggregate = jnp.einsum(
        "btij,btjd->bid", weights, source[tile_src], preferred_element_type=jnp.float32
    )
    aggregate = aggregate.reshape(nrows, width).astype(jnp.bfloat16)
    pre_act = (
        jnp.dot(features, self_low, preferred_element_type=jnp.float32)
        + jnp.dot(aggregate, neigh_low, preferred_element_type=jnp.float32)
        + out_bias
    )
    sigmoid_pre = jax.nn.sigmoid(pre_act)
    hidden_out = (pre_act * sigmoid_pre).astype(jnp.bfloat16)
    grad_pre = (
        cotangent.astype(jnp.float32) * sigmoid_pre * (1.0 + pre_act * (1.0 - sigmoid_pre))
    ).astype(jnp.bfloat16)
    part_self = jnp.dot(features.T, grad_pre, preferred_element_type=jnp.float32)
    part_neigh = jnp.dot(aggregate.T, grad_pre, preferred_element_type=jnp.float32)
    part_bias = jnp.sum(grad_pre.astype(jnp.float32), 0)
    total_self, total_neigh, total_bias = lax.psum(
        (part_self, part_neigh, part_bias), ("outer", "inner")
    )
    factor = 1.0 / jnp.sqrt(jnp.float32(nrows * ndevice))
    grad_local = jnp.dot(grad_pre, self_low.T, preferred_element_type=jnp.float32)
    grad_agg = jnp.dot(grad_pre, neigh_low.T, preferred_element_type=jnp.float32).astype(
        jnp.bfloat16
    )
    contrib = jnp.einsum(
        "btij,bid->btjd",
        weights,
        grad_agg.reshape(nblocks, tilerows, width),
        preferred_element_type=jnp.float32,
    )
    contrib = contrib.reshape(nblocks * per_block, tilerows, width)
    grad_src = (
        jnp.zeros((ntiles, tilerows, width), jnp.float32).at[tile_src.reshape(-1)].add(contrib)
    )
    grad_src = grad_src.reshape(ntiles * tilerows, width)
    bound_grad = grad_src[nrows : nrows + nbound].reshape(groupsize, tilerows, width)
    returned = lax.all_to_all(bound_grad, "inner", split_axis=0, concat_axis=0, tiled=True)
    returned = jnp.where(row_mask[..., None], returned, jnp.zeros((), jnp.float32))
    hub_part = grad_src[nrows + nbound :]
    hub_mine = lax.psum_scatter(hub_part, ("outer", "inner"), scatter_dimension=0, tiled=True)
    grad_total = grad_local + grad_src[:nrows]
    grad_total = grad_total.at[send_rows.reshape(-1)].add(returned.reshape(nbound, width))
    grad_total = grad_total.at[hub_rows].add(hub_mine)
    return (
        hidden_out,
        grad_total.astype(jnp.bfloat16),
        total_self * factor,
        total_neigh * factor,
        total_bias * factor,
    )


def solution(mesh):
    return jax.shard_map(
        body,
        mesh=mesh,
        in_specs=(
            P(("outer", "inner"), None),
            P(("outer", "inner"), None, None),
            P(("outer", "inner"), None),
            P(("outer", "inner"), None),
            P(("outer", "inner"), None),
            P(("outer", "inner")),
            P(),
            P(),
            P(),
            P(("outer", "inner"), None),
        ),
        out_specs=(P(("outer", "inner"), None), P(("outer", "inner"), None), P(), P(), P()),
        check_vma=False,
    )
```

profile of v0, /device:TPU:0, one launch (start us, length us, event | category | flops | bytes accessed | tf_op | source)
XLA Modules:
  0.0 328.5 jit_solution(12967009982026884889)
XLA Ops:
  7.2 0.0 copy-start
  7.2 0.8 iota_compare_fusion
  8.0 0.7 fusion.10
  8.7 5.0 %gather_fusion = bf16[1024,512]{1,0:T(8,128)(2,1)S(1)} fusion(bf16[384,512]{1,0:T(8,128)(2,1)} %param.10, s32[1024]{0:T(1024)S(1)} %fusion.10), kind=kCustom, calls=%fused_computation | custom fusion | bytes 2101248 | tf_op jit(solution)/shard_map/gather | solution.py:31
  13.7 0.0 copy-start.11
  13.7 0.0 copy-start.1
  13.7 0.0 copy-start.8
  13.7 0.0 copy-start.2
  13.8 1.2 broadcast_select_fusion.1
  14.9 7.3 %all-to-all-start = ((bf16[8,128,512]{2,1,0:T(8,128)(2,1)}), bf16[8,128,512]{2,1,0:T(8,128)(2,1)S(1)}, u32[]{:S(2)}, u32[]{:S(2)}) async-start(bf16[8,128,512]{2,1,0:T(8,128)(2,1)} %broadcast_select_fusion.1), calls=%async_computation | async-start | bytes 2097152 | tf_op jit(solution)/shard_map/all_to_all | solution.py:32
  22.2 0.0 copy-done.11
  22.2 0.0 copy-done.1
  22.3 0.6 gather_fusion.1
  22.8 81.0 %all-gather.1 = bf16[32,4,512]{2,1,0:T(4,128)(2,1)S(1)} all-gather(bf16[1,4,512]{2,1,0:T(4,128)(2,1)S(1)} %bitcast.62), channel_id=2, replica_groups=mesh['outer'=4,'inner'=8] {'outer','inner'}, dimensions={0}, use_global_device_ids=true | all-gather | bytes 135168 | tf_op jit(solution)/shard_map/all_gather | solution.py:33
  103.9 0.0 copy-done.8
  103.9 0.1 reshape.126
  104.0 0.1 reshape.149
  104.1 0.0 copy-done.2
  104.1 1.3 fusion.5
  105.3 0.0 all-to-all-done
  105.3 0.0 copy-start.4
  105.3 1.0 copy-done.4
  106.3 1.3 pad_maximum_fusion
  107.6 2.3 gather_fusion.2
  109.9 0.0 copy-start.5
  109.9 0.0 copy-start.6
  109.9 0.0 copy-start.9
  109.9 0.0 copy-start.10
  109.9 0.0 copy-done
  110.0 2.3 fusion.1
  112.3 0.0 copy-done.5
  112.3 0.0 copy-done.6
  112.3 0.0 copy-done.9
  112.3 0.0 copy-done.10
  112.3 1.4 convert_reduce_fusion
  113.7 0.4 convolution_convert_fusion
  114.1 3.0 fusion.12
  117.1 6.1 %copy.21 = f32[18,128,512]{2,1,0:T(8,128)} copy(f32[18,128,512]{1,2,0:T(8,128)} %bitcast.51) | data formatting | bytes 9437184 | tf_op jit(solution)/shard_map/reshape | solution.py:68
  123.2 2.1 broadcast_in_dim.46
  125.2 13.2 %scatter_fusion = f32[12,128,512]{2,1,0:T(8,128)} fusion(f32[12,128,512]{2,1,0:T(8,128)} %broadcast_in_dim.46, s32[18]{0:T(128)S(1)} %fusion.11, f32[18,128,512]{2,1,0:T(8,128)} %copy.21), kind=kCustom, calls=%fused_computation.3 | custom fusion | flops 1179648 | bytes 14155848 | tf_op jit(solution)/shard_map/scatter-add | solution.py:70
  138.4 3.1 slice.28
  141.5 4.3 %all-to-all-start.1 = ((f32[8,128,512]{2,1,0:T(8,128)}), f32[8,128,512]{2,1,0:T(8,128)}, u32[]{:S(2)}, u32[]{:S(2)}) async-start(f32[8,128,512]{2,1,0:T(8,128)} %slice.28), calls=%async_computation.1 | async-start | bytes 4194304 | tf_op jit(solution)/shard_map/all_to_all | solution.py:74
  145.8 0.0 all-reduce.4.cloned.1.call-start
  145.9 1.7 slice_bitcast_fusion
  147.5 1.4 fusion.13
  149.0 0.0 copy-start.7
  149.0 1.4 convolution_bitcast_fusion
  150.4 0.0 copy-start.3
  150.4 0.0 all-reduce.4.cloned.1.call-update
  150.5 0.0 copy-done.7
  150.5 2.2 slice.27
  152.6 69.3 %psum.23 = f32[512]{0:T(512)S(1)} all-reduce(f32[512]{0:T(512)S(1)} %get-tuple-element.18), channel_id=1, replica_groups=mesh['outer'=4,'inner'=8] {'outer','inner'}, use_global_device_ids=true, to_apply=%region_7.8 | all-reduce | flops 512 | bytes 4096 | tf_op jit(solution)/shard_map/psum | solution.py:54
  221.9 0.6 broadcast_multiply_fusion.2
  222.5 0.0 copy-done.3
  222.5 1.5 convolution_add_fusion
  224.0 82.5 %all-reduce.4.cloned.1.call-done = (f32[128,512]{1,0:T(8,128)}, f32[512,512]{0,1:T(8,128)}, f32[512,512]{0,1:T(8,128)}) async-done(((f32[128,512]{1,0:T(8,128)}, f32[512,512]{0,1:T(8,128)}, f32[512,512]{0,1:T(8,128)}), (f32[128,512]{1,0:T(8,128)}, f32[512,512]{0,1:T(8,128)}, f32[512,512]{0,1:T(8,128)})) %all-reduce.4.cloned.1.call-update) | async-done | bytes 2359312
  306.5 1.8 broadcast_multiply_fusion
  308.3 1.3 copy.23
  309.6 1.3 copy.24
  310.9 0.0 all-to-all-done.1
  311.0 1.8 broadcast_select_fusion
  312.8 6.9 %scatter_fusion.1 = f32[384,512]{1,0:T(8,128)S(1)} fusion(f32[384,512]{1,0:T(8,128)S(1)} %convolution_add_fusion, s32[1024]{0:T(1024)S(1)} %bitcast.61, f32[1024,512]{1,0:T(8,128)S(1)} %bitcast.54), kind=kCustom, calls=%fused_computation.4 | custom fusion | flops 524288 | bytes 6295552 | tf_op jit(solution)/shard_map/scatter-add | solution.py:79
  319.7 1.1 scatter_custom_fusion.2
  320.8 0.8 convert_element_type.42
  (7 shorter events, 0.1 us)
Async XLA Ops:
  7.2 102.8 %copy-start = (bf16[18,128,128]{2,1,0:T(8,128)(2,1)S(1)}, bf16[18,128,128]{2,1,0:T(8,128)(2,1)}, u32[]{:S(2)}) copy-start(bf16[18,128,128]{2,1,0:T(8,128)(2,1)} %param.11) | copy-start | bytes 1769476
  13.7 8.5 %copy-start.11 = (s32[4]{0:T(128)S(1)}, s32[4]{0:T(128)}, u32[]{:S(2)}) copy-start(s32[4]{0:T(128)} %param.15) | copy-start | bytes 52
  13.7 8.5 %copy-start.1 = (bf16[384,512]{1,0:T(8,128)(2,1)S(1)}, bf16[384,512]{1,0:T(8,128)(2,1)}, u32[]{:S(2)}) copy-start(bf16[384,512]{1,0:T(8,128)(2,1)} %param.10) | copy-start | bytes 1179652
  13.7 90.1 %copy-start.8 = (s32[3,6]{1,0:T(4,128)S(1)}, s32[3,6]{1,0:T(4,128)}, u32[]{:S(2)}) copy-start(s32[3,6]{1,0:T(4,128)} %param.12) | copy-start | bytes 220
  13.7 90.3 %copy-start.2 = (f32[512,512]{1,0:T(8,128)S(1)}, f32[512,512]{1,0:T(8,128)}, u32[]{:S(2)}) copy-start(f32[512,512]{1,0:T(8,128)} %param.16) | copy-start | bytes 3145732
  14.9 90.4 %all-to-all-start = ((bf16[8,128,512]{2,1,0:T(8,128)(2,1)}), bf16[8,128,512]{2,1,0:T(8,128)(2,1)S(1)}, u32[]{:S(2)}, u32[]{:S(2)}) async-start(bf16[8,128,512]{2,1,0:T(8,128)(2,1)} %broadcast_select_fusion.1), calls=%async_computation | async-start | bytes 2097152 | tf_op jit(solution)/shard_map/all_to_all | solution.py:32
  105.3 1.0 copy-start.4
  109.9 2.3 copy-start.5
  109.9 2.3 copy-start.6
  109.9 2.3 copy-start.9
  109.9 2.3 copy-start.10
  141.5 169.5 %all-to-all-start.1 = ((f32[8,128,512]{2,1,0:T(8,128)}), f32[8,128,512]{2,1,0:T(8,128)}, u32[]{:S(2)}, u32[]{:S(2)}) async-start(f32[8,128,512]{2,1,0:T(8,128)} %slice.28), calls=%async_computation.1 | async-start | bytes 4194304 | tf_op jit(solution)/shard_map/all_to_all | solution.py:74
  145.8 160.7 %all-reduce.4.cloned.1.call-start = ((), (), s32[]{:S(2)}) async-start(), calls=%async_computation.2 | async-start | bytes 4718592
  149.0 1.5 copy-start.7
  150.4 72.1 %copy-start.3 = (f32[512,512]{1,0:T(8,128)S(1)}, f32[512,512]{1,0:T(8,128)}, u32[]{:S(2)}) copy-start(f32[512,512]{1,0:T(8,128)} %param.16) | copy-start | bytes 3145732
Sparse Core Ops, SparseCore 0:
  153.1 153.3 all-reduce.3
where the time goes:
time: 329 us; the launch traced here: 328 us
  blocking collectives  150 us (46%)
  waiting for transfers between devices  82.5 us (25%)
  other arithmetic  30.2 us (9%)
  local copies, waits for them, and re-layouts  26.7 us (8%)
  between operations  14.3 us (4%)
  matrix products  12.8 us (4%)
  starting transfers between devices  11.7 us (4%)
    unnamed x2, waiting for transfers between devices  82.5 us
    all_gather x1, blocking collectives, body(): lax.all_gather(features[hub_rows], ('outer', 'inner'), axis=0, tiled=True)  81 us
    psum x1, blocking collectives, body(): lax.psum((part_self, part_neigh, part_bias), ('outer', 'inner'))  69.3 us
    scatter-add x1, other arithmetic, body(): jnp.zeros((ntiles, tilerows, width), jnp.float32).at[tile_src.reshape(-1)]  13.2 us
    all_to_all x1, starting transfers between devices, body(): lax.all_to_all(outgoing, 'inner', split_axis=0, concat_axis=0, tiled=True)  7.28 us
    scatter-add x1, other arithmetic, body(): grad_total.at[send_rows.reshape(-1)].add(returned.reshape(nbound, width))  6.9 us
  transfers between devices with their start and end apart: 3, of which 1 were waited for; matrix products, arithmetic and copies ran while one was open for 5% of the time, Pallas kernels for 0%

commit v1 on v0

v1 whole, which is shorter than its diff:
```python
import functools

import jax
import jax.numpy as jnp
from jax import lax
from jax.experimental import pallas as pl
from jax.experimental.pallas import tpu as pltpu
from jax.sharding import PartitionSpec as P

BF = jnp.bfloat16
F32 = jnp.float32
ANY = pl.BlockSpec(memory_space=pl.ANY)
VM = pl.BlockSpec(memory_space=pltpu.VMEM)
SM = pl.BlockSpec(memory_space=pltpu.SMEM)
PARAMS = pltpu.CompilerParams(vmem_limit_bytes=48 * 1024 * 1024)
TN = (((0,), (0,)), ((), ()))
NT = (((1,), (1,)), ((), ()))


def dot(a, b, dims=(((1,), (0,)), ((), ()))):
    return lax.dot_general(a, b, dims, preferred_element_type=F32)


def tree_steps(n_outer, n_inner):
    steps = []
    for name, size in (("outer", n_outer), ("inner", n_inner)):
        bit = 1
        while bit < size:
            steps.append((name, bit))
            bit *= 2
    return steps


def tree_offsets(steps):
    count = len(steps)
    table = []
    for slot in range(2**count):
        flip = {"outer": 0, "inner": 0}
        for k, (name, bit) in enumerate(steps):
            if (slot >> (count - 1 - k)) & 1:
                flip[name] ^= bit
        table.append((flip["outer"], flip["inner"]))
    return table


def hub_order(steps, n_inner, hd, nhubs):
    me = lax.axis_index("outer") * n_inner + lax.axis_index("inner")
    column = lax.broadcasted_iota(jnp.int32, (1, nhubs), 1)
    slot = column // hd
    flip = jnp.zeros((1, nhubs), jnp.int32)
    for k, (name, bit) in enumerate(steps):
        weight = bit * n_inner if name == "outer" else bit
        flip = flip + ((slot >> (len(steps) - 1 - k)) & 1) * weight
    target = (flip ^ me) * hd + column % hd
    row = lax.broadcasted_iota(jnp.int32, (nhubs, nhubs), 0)
    return (row == target).astype(F32).astype(BF)


def load_rows(ref, at, n):
    if n % 8 == 0:
        return ref[pl.ds(pl.multiple_of(at, n), n), :]
    return jnp.concatenate([ref[pl.ds(at + r, 1), :] for r in range(n)], axis=0)


def store_rows(ref, at, value):
    n = value.shape[0]
    if n % 8 == 0:
        ref[pl.ds(pl.multiple_of(at, n), n), :] = value
    else:
        for r in range(n):
            ref[pl.ds(at + r, 1), :] = value[r : r + 1, :]


def exchange(x, name, bit):
    size = lax.axis_size(name)
    return lax.ppermute(x, name, [(s, s ^ bit) for s in range(size)])


def slot_onehot(rows_ref, count_ref, nrows):
    partners, slots = rows_ref.shape
    sub = lax.broadcasted_iota(jnp.int32, (nrows, slots), 0)
    lane = lax.broadcasted_iota(jnp.int32, (1, slots), 1)
    parts = []
    for q in range(partners):
        live = jnp.where(lane < count_ref[0, q], rows_ref[q : q + 1, :], -1)
        parts.append((sub == live).astype(F32).astype(BF))
    return jnp.concatenate(parts, axis=1)


def gather_kernel(hub_ref, count_ref, feat_ref, rows_ref, out_ref, hub_out_ref):
    nrows, width = feat_ref.shape
    partners, slots = rows_ref.shape
    nhub = hub_ref.shape[0]
    feat = feat_ref[...]
    pick = slot_onehot(rows_ref, count_ref, nrows)
    out_ref[...] = dot(pick, feat, TN).astype(BF).reshape(partners, slots, width)
    sub = lax.broadcasted_iota(jnp.int32, (16, nrows), 0)
    lane = lax.broadcasted_iota(jnp.int32, (16, nrows), 1)
    hot = jnp.zeros((16, nrows), F32)
    for h in range(nhub):
        hot = hot + ((sub == h) & (lane == hub_ref[h])).astype(F32)
    hub_out_ref[...] = dot(hot.astype(BF), feat)[:nhub]


def middle_kernel(
    steps,
    chunk,
    tile_src,
    feat_hbm,
    recv_hbm,
    hubx_hbm,
    adj_hbm,
    pre_hbm,
    wn_hbm,
    ws_hbm,
    cot_hbm,
    hidden_hbm,
    back_hbm,
    own_hbm,
    tree_hbm,
    src,
    hubx,
    hubf,
    adj,
    pre0,
    wn,
    ws,
    cot,
    agg,
    hidden,
    gsrc,
    back,
    own,
    wacc,
    tail,
    tree,
    sems,
    osems,
):
    o = lax.axis_index("outer")
    i = lax.axis_index("inner")
    n_inner = back.shape[0]
    offsets = tree_offsets(steps)
    nblocks, per_block = tile_src.shape
    tile = adj.shape[1]
    width = cot.shape[1]
    ntiles = src.shape[0]
    first_hub = nblocks + n_inner
    hd = hubx.shape[0] // len(offsets)
    pairs = [
        (hubx_hbm, hubx),
        (feat_hbm, src.at[pl.ds(0, nblocks)]),
        (recv_hbm, src.at[pl.ds(nblocks, n_inner)]),
        (adj_hbm, adj),
        (wn_hbm, wn),
        (pre_hbm, pre0),
        (cot_hbm, cot),
        (ws_hbm, ws),
    ]
    copies = [pltpu.make_async_copy(a, b, sems.at[k]) for k, (a, b) in enumerate(pairs)]
    for c in copies:
        c.start()
    outs = [
        pltpu.make_async_copy(hidden, hidden_hbm, osems.at[0]),
        pltpu.make_async_copy(back, back_hbm, osems.at[1]),
        pltpu.make_async_copy(own, own_hbm, osems.at[2]),
        pltpu.make_async_copy(tree, tree_hbm, osems.at[3]),
    ]
    devices = [(o ^ fo) * n_inner + (i ^ fi) for fo, fi in offsets]
    gsrc[...] = jnp.zeros(gsrc.shape, F32)
    copies[0].wait()
    order = hub_order(steps, n_inner, hd, hubx.shape[0])
    hubs = dot(order, hubx[...].astype(BF)).astype(BF)
    src[first_hub:] = hubs.reshape(ntiles - first_hub, tile, width)
    copies[1].wait()
    copies[2].wait()
    copies[3].wait()
    for b in range(nblocks):
        acc = jnp.zeros((tile, width), F32)
        for t in range(per_block):
            acc = acc + dot(adj[b * per_block + t], src[tile_src[b, t]])
        agg[b * tile : (b + 1) * tile, :] = acc.astype(BF)
    copies[4].wait()
    copies[5].wait()
    pre = pre0[...] + dot(agg[...], wn[...])
    copies[6].wait()
    sig = jax.nn.sigmoid(pre)
    hidden[...] = (pre * sig).astype(BF)
    outs[0].start()
    gp = (cot[...].astype(F32) * sig * (1.0 + pre * (1.0 - sig))).astype(BF)
    gagg = dot(gp, wn[...], NT).astype(BF)
    for b in range(nblocks):
        block = gagg[b * tile : (b + 1) * tile, :]
        for t in range(per_block):
            s = tile_src[b, t]
            gsrc[s] = gsrc[s] + dot(adj[b * per_block + t], block, TN)
    back[...] = gsrc[nblocks:first_hub].astype(BF)
    outs[1].start()
    feat = src[0:nblocks].reshape(nblocks * tile, width)
    wacc[0:width, :] = dot(feat, gp, TN)
    wacc[width : 2 * width, :] = dot(agg[...], gp, TN)
    hubf[...] = dot(order, gsrc[first_hub:].reshape(hubf.shape).astype(BF), TN)
    tail[...] = jnp.zeros(tail.shape, F32)
    tail[hd : hd + 1, :] = jnp.sum(gp.astype(F32), axis=0, keepdims=True)
    wrows = 2 * width // len(offsets)
    base = chunk - tail.shape[0]
    for j, d in enumerate(devices):
        mine = load_rows(wacc, d * wrows, wrows)
        if base == wrows:
            tree[j * chunk : j * chunk + wrows, :] = mine.astype(BF)
        else:
            tail[8 : 8 + wrows, :] = mine
        tail[0:hd, :] = hubf[j * hd : (j + 1) * hd, :]
        tree[j * chunk + base : (j + 1) * chunk, :] = tail[...].astype(BF)
    outs[3].start()
    copies[7].wait()
    own[...] = dot(gp, ws[...], NT) + gsrc[0:nblocks].reshape(own.shape)
    outs[2].start()
    for c in outs:
        c.wait()


def scatter_kernel(hub_ref, count_ref, rows_ref, ret_ref, own_ref, hub_grad_ref, out_ref, acc):
    nrows, width = own_ref.shape
    put = slot_onehot(rows_ref, count_ref, nrows)
    partners, slots = rows_ref.shape
    acc[...] = own_ref[...] + dot(put, ret_ref[...].reshape(partners * slots, width))
    for h in range(hub_ref.shape[0]):
        r = hub_ref[h]
        acc[pl.ds(r, 1), :] = acc[pl.ds(r, 1), :] + hub_grad_ref[h : h + 1, :]
    out_ref[...] = acc[...].astype(BF)


def finish_kernel(offsets, n_inner, factor, x_ref, self_ref, neigh_ref, full):
    o = lax.axis_index("outer")
    i = lax.axis_index("inner")
    wrows = x_ref.shape[0] // len(offsets)
    width = self_ref.shape[0]
    x = x_ref[...].astype(F32) * factor
    for j, (fo, fi) in enumerate(offsets):
        d = (o ^ fo) * n_inner + (i ^ fi)
        store_rows(full, d * wrows, x[j * wrows : (j + 1) * wrows, :])
    self_ref[...] = full[0:width, :]
    neigh_ref[...] = full[width : 2 * width, :]


def cost(flops, nbytes):
    return pl.CostEstimate(flops=flops, bytes_accessed=nbytes, transcendentals=0)


def body(
    features,
    adj_tiles,
    tile_src,
    send_rows,
    send_count,
    hub_rows,
    w_self,
    w_neigh,
    out_bias,
    cotangent,
):
    n_outer, n_inner = lax.axis_size("outer"), lax.axis_size("inner")
    ndevice = n_outer * n_inner
    nrows, width = features.shape
    tile = adj_tiles.shape[1]
    nblocks, per_block = tile_src.shape
    hd = hub_rows.shape[0]
    nhubs = hd * ndevice
    ntiles = nblocks + n_inner + nhubs // tile
    steps = tree_steps(n_outer, n_inner)
    offsets = tree_offsets(steps)
    wrows = 2 * width // ndevice
    chunk = wrows + 16 if wrows % 16 == 0 else 16
    base = chunk - 16

    outgoing, hub_own = pl.pallas_call(
        gather_kernel,
        out_shape=(
            jax.ShapeDtypeStruct((n_inner, tile, width), BF),
            jax.ShapeDtypeStruct((hd, width), F32),
        ),
        in_specs=[SM, SM, VM, VM],
        out_specs=(VM, VM),
        compiler_params=PARAMS,
        cost_estimate=cost(4 * 10**8, 3 * 10**6),
        name="gather_rows",
    )(hub_rows, send_count, features, send_rows)
    received = lax.all_to_all(outgoing, "inner", split_axis=0, concat_axis=0, tiled=True)
    hubx = hub_own
    for name, bit in reversed(steps):
        hubx = jnp.concatenate([hubx, exchange(hubx, name, bit)], 0)
    self_low = w_self.astype(BF)
    neigh_low = w_neigh.astype(BF)
    pre0 = jnp.dot(features, self_low, preferred_element_type=F32) + out_bias

    hidden_out, back, own, tree = pl.pallas_call(
        functools.partial(middle_kernel, steps, chunk),
        out_shape=(
            jax.ShapeDtypeStruct((nrows, width), BF),
            jax.ShapeDtypeStruct((n_inner, tile, width), BF),
            jax.ShapeDtypeStruct((nrows, width), F32),
            jax.ShapeDtypeStruct((ndevice * chunk, width), BF),
        ),
        in_specs=[SM] + [ANY] * 8,
        out_specs=(ANY,) * 4,
        scratch_shapes=[
            pltpu.VMEM((ntiles, tile, width), BF),
            pltpu.VMEM((nhubs, width), F32),
            pltpu.VMEM((nhubs, width), F32),
            pltpu.VMEM(adj_tiles.shape, BF),
            pltpu.VMEM((nrows, width), F32),
            pltpu.VMEM((width, width), BF),
            pltpu.VMEM((width, width), BF),
            pltpu.VMEM((nrows, width), BF),
            pltpu.VMEM((nrows, width), BF),
            pltpu.VMEM((nrows, width), BF),
            pltpu.VMEM((ntiles, tile, width), F32),
            pltpu.VMEM((n_inner, tile, width), BF),
            pltpu.VMEM((nrows, width), F32),
            pltpu.VMEM((2 * width, width), F32),
            pltpu.VMEM((16, width), F32),
            pltpu.VMEM((ndevice * chunk, width), BF),
            pltpu.SemaphoreType.DMA((8,)),
            pltpu.SemaphoreType.DMA((4,)),
        ],
        compiler_params=PARAMS,
        cost_estimate=cost(2 * 10**9, 9 * 10**6),
        name="middle",
    )(
        tile_src,
        features.reshape(nblocks, tile, width),
        received,
        hubx,
        adj_tiles,
        pre0,
        neigh_low,
        self_low,
        cotangent,
    )
    returned = lax.all_to_all(back, "inner", split_axis=0, concat_axis=0, tiled=True)
    part = tree
    for k, (name, bit) in enumerate(steps):
        half = part.shape[0] // 2
        got = exchange(part[half:], name, bit)
        part = part[:half].astype(F32) + got.astype(F32)
        if k + 1 < len(steps):
            part = part.astype(BF)
    if wrows % 16 == 0:
        mine = part[:wrows]
    else:
        mine = part[8 : 8 + wrows]
    hub_grad = part[base : base + hd]
    total_bias = part[base + hd]
    gathered = mine.astype(BF)
    for name, bit in reversed(steps):
        gathered = jnp.concatenate([gathered, exchange(gathered, name, bit)], 0)

    grad_features = pl.pallas_call(
        scatter_kernel,
        out_shape=jax.ShapeDtypeStruct((nrows, width), BF),
        in_specs=[SM, SM, VM, VM, VM, VM],
        out_specs=VM,
        scratch_shapes=[pltpu.VMEM((nrows, width), F32)],
        compiler_params=PARAMS,
        cost_estimate=cost(4 * 10**8, 3 * 10**6),
        name="scatter_rows",
    )(hub_rows, send_count, send_rows, returned, own, hub_grad)
    factor = 1.0 / float(nrows * ndevice) ** 0.5
    total_self, total_neigh = pl.pallas_call(
        functools.partial(finish_kernel, offsets, n_inner, factor),
        out_shape=(jax.ShapeDtypeStruct((width, width), F32),) * 2,
        in_specs=[VM],
        out_specs=(VM, VM),
        scratch_shapes=[pltpu.VMEM((2 * width, width), F32)],
        compiler_params=PARAMS,
        cost_estimate=cost(10**6, 3 * 10**6),
        name="finish",
    )(gathered)
    return hidden_out, grad_features, total_self, total_neigh, total_bias * factor


def solution(mesh):
    both = ("outer", "inner")
    return jax.shard_map(
        body,
        mesh=mesh,
        in_specs=(
            P(both, None),
            P(both, None, None),
            P(both, None),
            P(both, None),
            P(both, None),
            P(both),
            P(),
            P(),
            P(),
            P(both, None),
        ),
        out_specs=(P(both, None), P(both, None), P(), P(), P()),
        check_vma=False,
    )
```

time: 329 us -> 140 us (0.43)
  blocking collectives: 150 us -> 0 us
  other arithmetic: 30.2 us -> 2.4 us
  local copies, waits for them, and re-layouts: 26.7 us -> 9.82 us
  starting transfers between devices: 11.7 us -> 28 us
  between operations: 14.3 us -> 0.91 us
  Pallas kernels: 0 us -> 12.6 us
  matrix products: 12.8 us -> 0.37 us
    ppermute x0 -> x15, waiting for transfers between devices: none -> 85.7 us  [exchange(): return lax.ppermute(x, name, [(s, s ^ bit) for s in range(size)])]
    unnamed x2 -> x0, waiting for transfers between devices: 82.5 us -> none
    all_gather x1 -> x0, blocking collectives: 81 us -> none  [body(): lax.all_gather(features[hub_rows], ('outer', 'inner'), axis=0, tiled=True)]
    psum x1 -> x0, blocking collectives: 69.3 us -> none  [body(): lax.psum((part_self, part_neigh, part_bias), ('outer', 'inner'))]
    scatter-add x3 -> x0, other arithmetic: 21.2 us -> none  [the longest x1 13.2 us: body(): jnp.zeros((ntiles, tilerows, width), jnp.float32).at[tile_src.reshape(-1)]]
    ppermute x0 -> x15, starting transfers between devices: none -> 15.5 us  [exchange(): return lax.ppermute(x, name, [(s, s ^ bit) for s in range(size)])]
    pallas_call x0 -> x4, Pallas kernels: none -> 12.6 us  [the longest x1 6.71 us: body(): pl.pallas_call(functools.partial(middle_kernel, steps, chunk), out_shape=...]
    dot_general x8 -> x1, matrix products: 12.8 us -> 0.37 us  [body(): pre0 = jnp.dot(features, self_low, preferred_element_type=F32) + out_bias]
  transfers between devices with their start and end apart: 3 -> 17, of which waited for: 1 -> 12; matrix products, arithmetic and copies ran while one was open for 5% -> 4% of each run, Pallas kernels for 0% -> 1%
where the time goes in v1:
time: 140 us
  waiting for transfers between devices  85.7 us (61%)
  starting transfers between devices  28 us (20%)
  Pallas kernels  12.6 us (9%)
  local copies, waits for them, and re-layouts  9.82 us (7%)
  other arithmetic  2.4 us (2%)
    ppermute x15, waiting for transfers between devices, exchange(): return lax.ppermute(x, name, [(s, s ^ bit) for s in range(size)])  85.7 us
    ppermute x15, starting transfers between devices, exchange(): return lax.ppermute(x, name, [(s, s ^ bit) for s in range(size)])  15.5 us
    unnamed x33, local copies, waits for them, and re-layouts  7.63 us
    all_to_all x1, starting transfers between devices, body(): lax.all_to_all(outgoing, 'inner', split_axis=0, concat_axis=0, tiled=True)  7.42 us
    pallas_call x1, Pallas kernels, body(): pl.pallas_call(functools.partial(middle_kernel, steps, chunk), out_shape=...  6.71 us
    all_to_all x1, starting transfers between devices, body(): lax.all_to_all(back, 'inner', split_axis=0, concat_axis=0, tiled=True)  5.04 us
  transfers between devices with their start and end apart: 17, of which 12 were waited for; matrix products, arithmetic and copies ran while one was open for 4% of the time, Pallas kernels for 1%

profile of v1, /device:TPU:0, one launch (start us, length us, event | category | flops | bytes accessed | tf_op | source)
XLA Modules:
  0.0 139.8 jit_solution(18437436456582285928)
XLA Ops:
  0.6 0.0 copy-start
  0.6 1.0 copy-done
  1.6 0.7 copy-done.2
  2.3 0.7 copy-done.4
  3.0 0.7 copy-done.6
  3.6 2.3 %gather_rows.1 = (bf16[8,128,512]{2,1,0:T(8,128)(2,1)}, f32[4,512]{1,0:T(4,128)S(1)}) custom-call(s32[4]{0:T(128)S(1)} %copy-done.4, s32[1,8]{1,0:T(1,128)S(1)} %copy-done.6, bf16[384,512]{1,0:T(8,128)(2,1)S(1)} %copy-done, s32[8,128]{1,0:T(8,128)S(1)} %copy-done.2), custom_call_target="tpu_custom_call" | custom-call | flops 400000000 | bytes 3000000 | tf_op jit(solution)/shard_map/gather_rows/pallas_call | solution.py:277
  5.9 7.4 %all-to-all-start = ((bf16[8,128,512]{2,1,0:T(8,128)(2,1)}), bf16[8,128,512]{2,1,0:T(8,128)(2,1)}, u32[]{:S(2)}, u32[]{:S(2)}) async-start(bf16[8,128,512]{2,1,0:T(8,128)(2,1)} %get-tuple-element.13), calls=%async_computation | async-start | bytes 2097152 | tf_op jit(solution)/shard_map/all_to_all | solution.py:289
  13.3 2.9 %collective-permute-start = (f32[4,512]{1,0:T(4,128)S(1)}, f32[4,512]{1,0:T(4,128)S(1)}, u32[]{:S(2)}, u32[]{:S(2)}) collective-permute-start(f32[4,512]{1,0:T(4,128)S(1)} %get-tuple-element.14), channel_id=1, source_target_pairs={{0,4},{1,5},{2,6},{3,7},{4,0},{5,1},{6,2},{7,3},{8,12},{9,13},{10,... | collective-permute-start | bytes 24584 | tf_op jit(solution)/shard_map/ppermute | solution.py:76
  16.2 23.2 %collective-permute-done = f32[4,512]{1,0:T(4,128)S(1)} collective-permute-done((f32[4,512]{1,0:T(4,128)S(1)}, f32[4,512]{1,0:T(4,128)S(1)}, u32[]{:S(2)}, u32[]{:S(2)}) %collective-permute-start) | collective-permute-done | bytes 8224 | tf_op jit(solution)/shard_map/ppermute | solution.py:76
  39.5 0.1 collective-permute-start.1
  39.5 3.7 %collective-permute-done.1 = f32[8,512]{1,0:T(8,128)S(1)} collective-permute-done((f32[8,512]{1,0:T(8,128)S(1)}, f32[8,512]{1,0:T(8,128)S(1)}, u32[]{:S(2)}, u32[]{:S(2)}) %collective-permute-start.1) | collective-permute-done | bytes 16416 | tf_op jit(solution)/shard_map/ppermute | solution.py:76
  43.3 1.5 %collective-permute-start.2 = (f32[16,512]{1,0:T(8,128)S(1)}, f32[16,512]{1,0:T(8,128)S(1)}, u32[]{:S(2)}, u32[]{:S(2)}) collective-permute-start(f32[16,512]{1,0:T(8,128)S(1)} %pad_maximum_fusion.4), channel_id=1, source_target_pairs={{0,1},{1,0},{2,3},{3,2},{4,5},{5,4},{6,7},{7,6},{8,9},{9,8},{10,11... | collective-permute-start | bytes 98312 | tf_op jit(solution)/shard_map/ppermute | solution.py:76
  44.8 2.5 %collective-permute-done.2 = f32[16,512]{1,0:T(8,128)S(1)} collective-permute-done((f32[16,512]{1,0:T(8,128)S(1)}, f32[16,512]{1,0:T(8,128)S(1)}, u32[]{:S(2)}, u32[]{:S(2)}) %collective-permute-start.2) | collective-permute-done | bytes 32800 | tf_op jit(solution)/shard_map/ppermute | solution.py:76
  47.3 1.6 %collective-permute-start.3 = (f32[32,512]{1,0:T(8,128)S(1)}, f32[32,512]{1,0:T(8,128)S(1)}, u32[]{:S(2)}, u32[]{:S(2)}) collective-permute-start(f32[32,512]{1,0:T(8,128)S(1)} %pad_maximum_fusion.2), channel_id=1, source_target_pairs={{0,16},{8,24},{16,0},{24,8},{1,17},{9,25},{17,1},{25,9},{2,18},{10... | collective-permute-start | bytes 196616 | tf_op jit(solution)/shard_map/ppermute | solution.py:76
  48.8 0.0 copy-done.12
  48.8 0.1 convert_element_type.49.ws_hbm
  48.9 2.7 %collective-permute-done.3 = f32[32,512]{1,0:T(8,128)S(1)} collective-permute-done((f32[32,512]{1,0:T(8,128)S(1)}, f32[32,512]{1,0:T(8,128)S(1)}, u32[]{:S(2)}, u32[]{:S(2)}) %collective-permute-start.3) | collective-permute-done | bytes 65568 | tf_op jit(solution)/shard_map/ppermute | solution.py:76
  51.6 0.0 copy-start.10
  51.6 0.1 collective-permute-start.4
  51.7 0.4 convolution_add_fusion.pre_hbm
  52.1 1.3 convert_element_type.50.wn_hbm
  53.4 0.0 collective-permute-done.4
  53.5 0.0 all-to-all-done.recv_hbm
  53.5 0.0 copy-start.8
  53.5 1.1 copy-done.8
  54.5 1.0 copy-done.9
  55.5 6.7 %middle.1 = (bf16[384,512]{1,0:T(8,128)(2,1)}, bf16[8,128,512]{2,1,0:T(8,128)(2,1)}, f32[384,512]{1,0:T(8,128)S(1)}, bf16[1536,512]{1,0:T(8,128)(2,1)}) custom-call(s32[3,6]{1,0:T(4,128)S(1)} %copy-done.10, bf16[3,128,512]{2,1,0:T(8,128)(2,1)S(1)} %bitcast.4, bf16[8,128,512]{2,1,0:T(8,128)(2,1)} %all-to-all-done.recv_hbm, ...), custom_call_target="tpu_custom_call" | custom-call | flops 2000000000 | bytes 9000000 | tf_op jit(solution)/shard_map/middle/pallas_call | solution.py:297
  62.3 1.3 slice.41
  63.6 0.5 collective-permute-start.5
  64.1 1.9 %collective-permute-done.5 = bf16[768,512]{1,0:T(8,128)(2,1)S(1)} collective-permute-done((bf16[768,512]{1,0:T(8,128)(2,1)S(1)}, bf16[768,512]{1,0:T(8,128)(2,1)S(1)}, u32[]{:S(2)}, u32[]{:S(2)}) %collective-permute-start.5) | collective-permute-done | bytes 786464 | tf_op jit(solution)/shard_map/ppermute | solution.py:76
  66.0 0.2 add_convert_fusion
  66.3 1.6 %collective-permute-start.6 = (bf16[384,512]{1,0:T(8,128)(2,1)S(1)}, bf16[384,512]{1,0:T(8,128)(2,1)S(1)}, u32[]{:S(2)}, u32[]{:S(2)}) collective-permute-start(bf16[384,512]{1,0:T(8,128)(2,1)S(1)} %slice.54), channel_id=1, source_target_pairs={{0,16},{8,24},{16,0},{24,8},{1,17},{9,25},{17,1},{25,9},{2,18},{10... | collective-permute-start | bytes 1179656 | tf_op jit(solution)/shard_map/ppermute | solution.py:76
  67.8 9.9 %collective-permute-done.6 = bf16[384,512]{1,0:T(8,128)(2,1)S(1)} collective-permute-done((bf16[384,512]{1,0:T(8,128)(2,1)S(1)}, bf16[384,512]{1,0:T(8,128)(2,1)S(1)}, u32[]{:S(2)}, u32[]{:S(2)}) %collective-permute-start.6) | collective-permute-done | bytes 393248 | tf_op jit(solution)/shard_map/ppermute | solution.py:76
  77.7 0.1 add_convert_fusion.1
  77.9 1.5 %collective-permute-start.7 = (bf16[192,512]{1,0:T(8,128)(2,1)S(1)}, bf16[192,512]{1,0:T(8,128)(2,1)S(1)}, u32[]{:S(2)}, u32[]{:S(2)}) collective-permute-start(bf16[192,512]{1,0:T(8,128)(2,1)S(1)} %slice.56), channel_id=1, source_target_pairs={{0,1},{1,0},{2,3},{3,2},{4,5},{5,4},{6,7},{7,6},{8,9},{9,8},{10,11... | collective-permute-start | bytes 589832 | tf_op jit(solution)/shard_map/ppermute | solution.py:76
  79.3 4.9 %collective-permute-done.7 = bf16[192,512]{1,0:T(8,128)(2,1)S(1)} collective-permute-done((bf16[192,512]{1,0:T(8,128)(2,1)S(1)}, bf16[192,512]{1,0:T(8,128)(2,1)S(1)}, u32[]{:S(2)}, u32[]{:S(2)}) %collective-permute-start.7) | collective-permute-done | bytes 196640 | tf_op jit(solution)/shard_map/ppermute | solution.py:76
  84.3 0.1 add_convert_fusion.2
  84.4 0.1 collective-permute-start.8
  84.4 4.6 %collective-permute-done.8 = bf16[96,512]{1,0:T(8,128)(2,1)S(1)} collective-permute-done((bf16[96,512]{1,0:T(8,128)(2,1)S(1)}, bf16[96,512]{1,0:T(8,128)(2,1)S(1)}, u32[]{:S(2)}, u32[]{:S(2)}) %collective-permute-start.8) | collective-permute-done | bytes 98336 | tf_op jit(solution)/shard_map/ppermute | solution.py:76
  89.1 0.1 collective-permute-start.9
  89.2 5.0 %all-to-all-start.1 = ((bf16[8,128,512]{2,1,0:T(8,128)(2,1)}), bf16[8,128,512]{2,1,0:T(8,128)(2,1)S(1)}, u32[]{:S(2)}, u32[]{:S(2)}) async-start(bf16[8,128,512]{2,1,0:T(8,128)(2,1)} %get-tuple-element.16), calls=%async_computation.1 | async-start | bytes 2097152 | tf_op jit(solution)/shard_map/all_to_all | solution.py:341
  94.2 0.0 copy-start.5
  94.2 0.0 copy-start.7
  94.2 0.0 collective-permute-done.9
  94.3 0.6 constant_dynamic-update-slice_fusion.4
  94.9 2.9 %collective-permute-start.10 = (bf16[32,512]{1,0:T(8,128)(2,1)S(1)}, bf16[32,512]{1,0:T(8,128)(2,1)S(1)}, u32[]{:S(2)}, u32[]{:S(2)}) collective-permute-start(bf16[32,512]{1,0:T(8,128)(2,1)S(1)} %get-tuple-element.22), channel_id=1, source_target_pairs={{0,4},{1,5},{2,6},{3,7},{4,0},{5,1},{6,2},{7,3},{8,12},{9,13},{10,... | collective-permute-start | bytes 98312 | tf_op jit(solution)/shard_map/ppermute | solution.py:76
  97.8 21.2 %collective-permute-done.10 = bf16[32,512]{1,0:T(8,128)(2,1)S(1)} collective-permute-done((bf16[32,512]{1,0:T(8,128)(2,1)S(1)}, bf16[32,512]{1,0:T(8,128)(2,1)S(1)}, u32[]{:S(2)}, u32[]{:S(2)}) %collective-permute-start.10) | collective-permute-done | bytes 32800 | tf_op jit(solution)/shard_map/ppermute | solution.py:76
  119.0 0.0 collective-permute-start.11
  119.0 4.3 %collective-permute-done.11 = bf16[64,512]{1,0:T(8,128)(2,1)S(1)} collective-permute-done((bf16[64,512]{1,0:T(8,128)(2,1)S(1)}, bf16[64,512]{1,0:T(8,128)(2,1)S(1)}, u32[]{:S(2)}, u32[]{:S(2)}) %collective-permute-start.11) | collective-permute-done | bytes 65568 | tf_op jit(solution)/shard_map/ppermute | solution.py:76
  123.3 1.3 collective-permute-start.12
  124.5 3.8 %collective-permute-done.12 = bf16[128,512]{1,0:T(8,128)(2,1)S(1)} collective-permute-done((bf16[128,512]{1,0:T(8,128)(2,1)S(1)}, bf16[128,512]{1,0:T(8,128)(2,1)S(1)}, u32[]{:S(2)}, u32[]{:S(2)}) %collective-permute-start.12) | collective-permute-done | bytes 131104 | tf_op jit(solution)/shard_map/ppermute | solution.py:76
  128.3 1.5 %collective-permute-start.13 = (bf16[256,512]{1,0:T(8,128)(2,1)S(1)}, bf16[256,512]{1,0:T(8,128)(2,1)S(1)}, u32[]{:S(2)}, u32[]{:S(2)}) collective-permute-start(bf16[256,512]{1,0:T(8,128)(2,1)S(1)} %pad_maximum_fusion), channel_id=1, source_target_pairs={{0,16},{8,24},{16,0},{24,8},{1,17},{9,25},{17,1},{25,9},{2,18},{10... | collective-permute-start | bytes 786440 | tf_op jit(solution)/shard_map/ppermute | solution.py:76
  129.9 0.6 constant_dynamic-update-slice_fusion.3
  130.5 0.6 constant_dynamic-update-slice_fusion.2
  131.1 0.7 constant_dynamic-update-slice_fusion.1
  131.8 3.0 %collective-permute-done.13 = bf16[256,512]{1,0:T(8,128)(2,1)S(1)} collective-permute-done((bf16[256,512]{1,0:T(8,128)(2,1)S(1)}, bf16[256,512]{1,0:T(8,128)(2,1)S(1)}, u32[]{:S(2)}, u32[]{:S(2)}) %collective-permute-start.13) | collective-permute-done | bytes 262176 | tf_op jit(solution)/shard_map/ppermute | solution.py:76
  134.8 0.7 constant_dynamic-update-slice_fusion
  135.5 0.0 collective-permute-start.14
  135.5 0.6 slice_multiply_fusion
  136.1 0.0 all-to-all-done.1.ret_ref
  136.1 0.0 copy-done.3
  136.1 1.9 %scatter_rows.1 = bf16[384,512]{1,0:T(8,128)(2,1)} custom-call(s32[4]{0:T(128)S(1)} %copy-done.5, s32[1,8]{1,0:T(1,128)S(1)} %copy-done.7, s32[8,128]{1,0:T(8,128)S(1)} %copy-done.3, bf16[8,128,512]{2,1,0:T(8,128)(2,1)S(1)} %all-to-all-done.1.ret_ref, f32[384,512]{1,0:T(8,128)S(1)} %get-tuple-element.17.own_ref, f32[4,512]{1,0:T(4,128)S(1)} %slice.61.hub_grad_ref), custom_call_target="tpu_custom_call" | custom-call | flops 400000000 | bytes 3000000 | tf_op jit(solution)/shard_map/scatter_rows/pallas_call | solution.py:359
  138.0 0.0 collective-permute-done.14
  138.1 1.7 %finish.1 = (f32[512,512]{1,0:T(8,128)}, f32[512,512]{1,0:T(8,128)}) custom-call(bf16[1024,512]{1,0:T(8,128)(2,1)S(1)} %constant_dynamic-update-slice_fusion.5.x_ref), custom_call_target="tpu_custom_call" | custom-call | flops 1000000 | bytes 3000000 | tf_op jit(solution)/shard_map/finish/pallas_call | solution.py:370
  (32 shorter events, 0.3 us)
Async XLA Ops:
  0.6 1.0 copy-start
  1.6 0.7 copy-start.2
  2.3 0.7 copy-start.4
  3.0 0.7 copy-start.6
  3.6 45.2 %copy-start.12 = (f32[512,512]{1,0:T(8,128)S(1)}, f32[512,512]{1,0:T(8,128)}, u32[]{:S(2)}) copy-start(f32[512,512]{1,0:T(8,128)} %param.16) | copy-start | bytes 3145732
  5.9 45.8 %copy-start.1 = (bf16[384,512]{1,0:T(8,128)(2,1)S(1)}, bf16[384,512]{1,0:T(8,128)(2,1)}, u32[]{:S(2)}) copy-start(bf16[384,512]{1,0:T(8,128)(2,1)} %feat_ref.1) | copy-start | bytes 1179652
  5.9 45.8 %copy-start.13 = (f32[512]{0:T(512)S(1)}, f32[512]{0:T(512)}, u32[]{:S(2)}) copy-start(f32[512]{0:T(512)} %param.18) | copy-start | bytes 6148
  5.9 47.6 %all-to-all-start = ((bf16[8,128,512]{2,1,0:T(8,128)(2,1)}), bf16[8,128,512]{2,1,0:T(8,128)(2,1)}, u32[]{:S(2)}, u32[]{:S(2)}) async-start(bf16[8,128,512]{2,1,0:T(8,128)(2,1)} %get-tuple-element.13), calls=%async_computation | async-start | bytes 2097152 | tf_op jit(solution)/shard_map/all_to_all | solution.py:289
  13.3 26.1 %collective-permute-start = (f32[4,512]{1,0:T(4,128)S(1)}, f32[4,512]{1,0:T(4,128)S(1)}, u32[]{:S(2)}, u32[]{:S(2)}) collective-permute-start(f32[4,512]{1,0:T(4,128)S(1)} %get-tuple-element.14), channel_id=1, source_target_pairs={{0,4},{1,5},{2,6},{3,7},{4,0},{5,1},{6,2},{7,3},{8,12},{9,13},{10,... | collective-permute-start | bytes 24584 | tf_op jit(solution)/shard_map/ppermute | solution.py:76
  39.5 3.8 %collective-permute-start.1 = (f32[8,512]{1,0:T(8,128)S(1)}, f32[8,512]{1,0:T(8,128)S(1)}, u32[]{:S(2)}, u32[]{:S(2)}) collective-permute-start(f32[8,512]{1,0:T(8,128)S(1)} %pad_maximum_fusion.5), channel_id=1, source_target_pairs={{0,2},{1,3},{2,0},{3,1},{4,6},{5,7},{6,4},{7,5},{8,10},{9,11},{10,... | collective-permute-start | bytes 49160 | tf_op jit(solution)/shard_map/ppermute | solution.py:76
  43.3 4.0 %collective-permute-start.2 = (f32[16,512]{1,0:T(8,128)S(1)}, f32[16,512]{1,0:T(8,128)S(1)}, u32[]{:S(2)}, u32[]{:S(2)}) collective-permute-start(f32[16,512]{1,0:T(8,128)S(1)} %pad_maximum_fusion.4), channel_id=1, source_target_pairs={{0,1},{1,0},{2,3},{3,2},{4,5},{5,4},{6,7},{7,6},{8,9},{9,8},{10,11... | collective-permute-start | bytes 98312 | tf_op jit(solution)/shard_map/ppermute | solution.py:76
  47.3 4.3 %collective-permute-start.3 = (f32[32,512]{1,0:T(8,128)S(1)}, f32[32,512]{1,0:T(8,128)S(1)}, u32[]{:S(2)}, u32[]{:S(2)}) collective-permute-start(f32[32,512]{1,0:T(8,128)S(1)} %pad_maximum_fusion.2), channel_id=1, source_target_pairs={{0,16},{8,24},{16,0},{24,8},{1,17},{9,25},{17,1},{25,9},{2,18},{10... | collective-permute-start | bytes 196616 | tf_op jit(solution)/shard_map/ppermute | solution.py:76
  51.6 1.8 %copy-start.10 = (s32[3,6]{1,0:T(4,128)S(1)}, s32[3,6]{1,0:T(4,128)}, u32[]{:S(2)}) copy-start(s32[3,6]{1,0:T(4,128)} %tile_src.1) | copy-start | bytes 220
  51.6 1.8 %collective-permute-start.4 = (f32[64,512]{1,0:T(8,128)S(1)}, f32[64,512]{1,0:T(8,128)S(1)}, u32[]{:S(2)}, u32[]{:S(2)}) collective-permute-start(f32[64,512]{1,0:T(8,128)S(1)} %concatenate.41), channel_id=1, source_target_pairs={{0,8},{8,0},{16,24},{24,16},{1,9},{9,1},{17,25},{25,17},{2,10},{10... | collective-permute-start | bytes 393224 | tf_op jit(solution)/shard_map/ppermute | solution.py:76
  53.5 1.1 copy-start.8
  54.5 1.0 copy-start.9
  62.3 3.8 %copy-start.11 = (bf16[1536,512]{1,0:T(8,128)(2,1)S(1)}, bf16[1536,512]{1,0:T(8,128)(2,1)}, u32[]{:S(2)}) copy-start(bf16[1536,512]{1,0:T(8,128)(2,1)} %get-tuple-element.18) | copy-start | bytes 4718596
  63.6 2.5 %collective-permute-start.5 = (bf16[768,512]{1,0:T(8,128)(2,1)S(1)}, bf16[768,512]{1,0:T(8,128)(2,1)S(1)}, u32[]{:S(2)}, u32[]{:S(2)}) collective-permute-start(bf16[768,512]{1,0:T(8,128)(2,1)S(1)} %slice.41), channel_id=1, source_target_pairs={{0,8},{8,0},{16,24},{24,16},{1,9},{9,1},{17,25},{25,17},{2,10},{10... | collective-permute-start | bytes 2359304 | tf_op jit(solution)/shard_map/ppermute | solution.py:76
  66.3 11.5 %collective-permute-start.6 = (bf16[384,512]{1,0:T(8,128)(2,1)S(1)}, bf16[384,512]{1,0:T(8,128)(2,1)S(1)}, u32[]{:S(2)}, u32[]{:S(2)}) collective-permute-start(bf16[384,512]{1,0:T(8,128)(2,1)S(1)} %slice.54), channel_id=1, source_target_pairs={{0,16},{8,24},{16,0},{24,8},{1,17},{9,25},{17,1},{25,9},{2,18},{10... | collective-permute-start | bytes 1179656 | tf_op jit(solution)/shard_map/ppermute | solution.py:76
  77.9 6.4 %collective-permute-start.7 = (bf16[192,512]{1,0:T(8,128)(2,1)S(1)}, bf16[192,512]{1,0:T(8,128)(2,1)S(1)}, u32[]{:S(2)}, u32[]{:S(2)}) collective-permute-start(bf16[192,512]{1,0:T(8,128)(2,1)S(1)} %slice.56), channel_id=1, source_target_pairs={{0,1},{1,0},{2,3},{3,2},{4,5},{5,4},{6,7},{7,6},{8,9},{9,8},{10,11... | collective-permute-start | bytes 589832 | tf_op jit(solution)/shard_map/ppermute | solution.py:76
  84.4 4.7 %collective-permute-start.8 = (bf16[96,512]{1,0:T(8,128)(2,1)S(1)}, bf16[96,512]{1,0:T(8,128)(2,1)S(1)}, u32[]{:S(2)}, u32[]{:S(2)}) collective-permute-start(bf16[96,512]{1,0:T(8,128)(2,1)S(1)} %slice.58), channel_id=1, source_target_pairs={{0,2},{1,3},{2,0},{3,1},{4,6},{5,7},{6,4},{7,5},{8,10},{9,11},{10,... | collective-permute-start | bytes 294920 | tf_op jit(solution)/shard_map/ppermute | solution.py:76
  89.1 5.2 %collective-permute-start.9 = (bf16[48,512]{1,0:T(8,128)(2,1)S(1)}, bf16[48,512]{1,0:T(8,128)(2,1)S(1)}, u32[]{:S(2)}, u32[]{:S(2)}) collective-permute-start(bf16[48,512]{1,0:T(8,128)(2,1)S(1)} %slice.60), channel_id=1, source_target_pairs={{0,4},{1,5},{2,6},{3,7},{4,0},{5,1},{6,2},{7,3},{8,12},{9,13},{10,... | collective-permute-start | bytes 147464 | tf_op jit(solution)/shard_map/ppermute | solution.py:76
  89.2 46.9 %all-to-all-start.1 = ((bf16[8,128,512]{2,1,0:T(8,128)(2,1)}), bf16[8,128,512]{2,1,0:T(8,128)(2,1)S(1)}, u32[]{:S(2)}, u32[]{:S(2)}) async-start(bf16[8,128,512]{2,1,0:T(8,128)(2,1)} %get-tuple-element.16), calls=%async_computation.1 | async-start | bytes 2097152 | tf_op jit(solution)/shard_map/all_to_all | solution.py:341
  94.2 41.9 %copy-start.3 = (s32[8,128]{1,0:T(8,128)S(1)}, s32[8,128]{1,0:T(8,128)}, u32[]{:S(2)}) copy-start(s32[8,128]{1,0:T(8,128)} %rows_ref.3) | copy-start | bytes 12292
  94.2 41.9 %copy-start.5 = (s32[4]{0:T(128)S(1)}, s32[4]{0:T(128)}, u32[]{:S(2)}) copy-start(s32[4]{0:T(128)} %hub_ref.3) | copy-start | bytes 52
  94.2 41.9 %copy-start.7 = (s32[1,8]{1,0:T(1,128)S(1)}, s32[1,8]{1,0:T(1,128)}, u32[]{:S(2)}) copy-start(s32[1,8]{1,0:T(1,128)} %count_ref.3) | copy-start | bytes 100
  94.9 24.1 %collective-permute-start.10 = (bf16[32,512]{1,0:T(8,128)(2,1)S(1)}, bf16[32,512]{1,0:T(8,128)(2,1)S(1)}, u32[]{:S(2)}, u32[]{:S(2)}) collective-permute-start(bf16[32,512]{1,0:T(8,128)(2,1)S(1)} %get-tuple-element.22), channel_id=1, source_target_pairs={{0,4},{1,5},{2,6},{3,7},{4,0},{5,1},{6,2},{7,3},{8,12},{9,13},{10,... | collective-permute-start | bytes 98312 | tf_op jit(solution)/shard_map/ppermute | solution.py:76
  119.0 4.3 %collective-permute-start.11 = (bf16[64,512]{1,0:T(8,128)(2,1)S(1)}, bf16[64,512]{1,0:T(8,128)(2,1)S(1)}, u32[]{:S(2)}, u32[]{:S(2)}) collective-permute-start(bf16[64,512]{1,0:T(8,128)(2,1)S(1)} %pad_maximum_fusion.3), channel_id=1, source_target_pairs={{0,2},{1,3},{2,0},{3,1},{4,6},{5,7},{6,4},{7,5},{8,10},{9,11},{10,... | collective-permute-start | bytes 196616 | tf_op jit(solution)/shard_map/ppermute | solution.py:76
  123.3 5.0 %collective-permute-start.12 = (bf16[128,512]{1,0:T(8,128)(2,1)S(1)}, bf16[128,512]{1,0:T(8,128)(2,1)S(1)}, u32[]{:S(2)}, u32[]{:S(2)}) collective-permute-start(bf16[128,512]{1,0:T(8,128)(2,1)S(1)} %pad_maximum_fusion.1), channel_id=1, source_target_pairs={{0,1},{1,0},{2,3},{3,2},{4,5},{5,4},{6,7},{7,6},{8,9},{9,8},{10,11... | collective-permute-start | bytes 393224 | tf_op jit(solution)/shard_map/ppermute | solution.py:76
  128.3 6.4 %collective-permute-start.13 = (bf16[256,512]{1,0:T(8,128)(2,1)S(1)}, bf16[256,512]{1,0:T(8,128)(2,1)S(1)}, u32[]{:S(2)}, u32[]{:S(2)}) collective-permute-start(bf16[256,512]{1,0:T(8,128)(2,1)S(1)} %pad_maximum_fusion), channel_id=1, source_target_pairs={{0,16},{8,24},{16,0},{24,8},{1,17},{9,25},{17,1},{25,9},{2,18},{10... | collective-permute-start | bytes 786440 | tf_op jit(solution)/shard_map/ppermute | solution.py:76
  135.5 2.5 %collective-permute-start.14 = (bf16[512,512]{1,0:T(8,128)(2,1)}, bf16[512,512]{1,0:T(8,128)(2,1)S(1)}, u32[]{:S(2)}, u32[]{:S(2)}) collective-permute-start(bf16[512,512]{1,0:T(8,128)(2,1)} %get-tuple-element.23), channel_id=1, source_target_pairs={{0,8},{8,0},{16,24},{24,16},{1,9},{9,1},{17,25},{25,17},{2,10},{10... | collective-permute-start | bytes 1572872 | tf_op jit(solution)/shard_map/ppermute | solution.py:76

commit v2 on v1

v2 whole, which is shorter than its diff:
```python
import functools
import math

import jax
import jax.numpy as jnp
from jax import lax
from jax.experimental import pallas as pl
from jax.experimental.pallas import tpu as pltpu
from jax.sharding import PartitionSpec as P

BF = jnp.bfloat16
F32 = jnp.float32
ANY = pl.BlockSpec(memory_space=pl.ANY)
VM = pl.BlockSpec(memory_space=pltpu.VMEM)
SM = pl.BlockSpec(memory_space=pltpu.SMEM)
MIB = 1024 * 1024
HBM = pl.BlockSpec(memory_space=pltpu.HBM)
TN = (((0,), (0,)), ((), ()))
NT = (((1,), (1,)), ((), ()))


def dot(a, b, dims=(((1,), (0,)), ((), ()))):
    return lax.dot_general(a, b, dims, preferred_element_type=F32)


def tree_steps(n_outer, n_inner):
    steps = []
    for name, size in (("outer", n_outer), ("inner", n_inner)):
        bit = 1
        while bit < size:
            steps.append((name, bit))
            bit *= 2
    return steps


def tree_offsets(steps):
    count = len(steps)
    table = []
    for slot in range(2**count):
        flip = {"outer": 0, "inner": 0}
        for k, (name, bit) in enumerate(steps):
            if (slot >> (count - 1 - k)) & 1:
                flip[name] ^= bit
        table.append((flip["outer"], flip["inner"]))
    return table


def hub_order(steps, n_inner, hd, nhubs):
    me = lax.axis_index("outer") * n_inner + lax.axis_index("inner")
    column = lax.broadcasted_iota(jnp.int32, (1, nhubs), 1)
    slot = column // hd
    flip = jnp.zeros((1, nhubs), jnp.int32)
    for k, (name, bit) in enumerate(steps):
        weight = bit * n_inner if name == "outer" else bit
        flip = flip + ((slot >> (len(steps) - 1 - k)) & 1) * weight
    target = (flip ^ me) * hd + column % hd
    row = lax.broadcasted_iota(jnp.int32, (nhubs, nhubs), 0)
    return (row == target).astype(F32).astype(BF)


def load_rows(ref, at, n):
    if n % 8 == 0:
        return ref[pl.ds(pl.multiple_of(at, n), n), :]
    return jnp.concatenate([ref[pl.ds(at + r, 1), :] for r in range(n)], axis=0)


def store_rows(ref, at, value):
    n = value.shape[0]
    if n % 8 == 0:
        ref[pl.ds(pl.multiple_of(at, n), n), :] = value
    else:
        for r in range(n):
            ref[pl.ds(at + r, 1), :] = value[r : r + 1, :]


def exchange(x, name, bit):
    size = lax.axis_size(name)
    return lax.ppermute(x, name, [(s, s ^ bit) for s in range(size)])


def direct_bits(steps):
    high, low = steps[-2][1], steps[-1][1]
    return [(high if c & 2 else 0) ^ (low if c & 1 else 0) for c in range(1, 4)]


def slot_onehot(rows_ref, count_ref, nrows, partners):
    slots = rows_ref.shape[1]
    sub = lax.broadcasted_iota(jnp.int32, (nrows, slots), 0)
    lane = lax.broadcasted_iota(jnp.int32, (1, slots), 1)
    parts = []
    for q in partners:
        live = jnp.where(lane < count_ref[0, q], rows_ref[pl.ds(q, 1), :], -1)
        parts.append((sub == live).astype(F32).astype(BF))
    return jnp.concatenate(parts, axis=1)


def gather_kernel(hub_ref, count_ref, feat_ref, rows_ref, out_ref, hub_out_ref):
    nrows, width = feat_ref.shape
    partners, slots = rows_ref.shape
    nhub = hub_ref.shape[0]
    feat = feat_ref[...]
    pick = slot_onehot(rows_ref, count_ref, nrows, range(partners))
    out_ref[...] = dot(pick, feat, TN).astype(BF).reshape(partners, slots, width)
    sub = lax.broadcasted_iota(jnp.int32, (16, nrows), 0)
    lane = lax.broadcasted_iota(jnp.int32, (16, nrows), 1)
    hot = jnp.zeros((16, nrows), F32)
    for h in range(nhub):
        hot = hot + ((sub == h) & (lane == hub_ref[h])).astype(F32)
    hub_out_ref[...] = dot(hot.astype(BF), feat)[:nhub].astype(BF)


def middle_kernel(
    steps,
    hub_steps,
    chunk,
    tile_src,
    feat_hbm,
    recv_hbm,
    hubx_hbm,
    adj_hbm,
    pre_hbm,
    wn_hbm,
    ws_hbm,
    cot_hbm,
    hidden_hbm,
    own_hbm,
    keep_hbm,
    give_hbm,
    *rest,
):
    n_inner = recv_hbm.shape[0]
    back_hbm, rest = rest[:n_inner], rest[n_inner:]
    (src, hubx, hubf, adj, pre0, wn, ws, cot, agg, hidden, gsrc, back, own, wacc, tail, tree, sems, osems) = rest
    o = lax.axis_index("outer")
    i = lax.axis_index("inner")
    offsets = tree_offsets(steps)
    nblocks, per_block = tile_src.shape
    tile = adj.shape[1]
    width = cot.shape[1]
    ntiles = src.shape[0]
    first_hub = nblocks + n_inner
    hd = hubx.shape[0] // len(offsets)
    pairs = [
        (hubx_hbm, hubx),
        (feat_hbm, src.at[pl.ds(0, nblocks)]),
        (recv_hbm, src.at[pl.ds(nblocks, n_inner)]),
        (adj_hbm, adj),
        (wn_hbm, wn),
        (pre_hbm, pre0),
        (cot_hbm, cot),
        (ws_hbm, ws),
    ]
    copies = [pltpu.make_async_copy(a, b, sems.at[k]) for k, (a, b) in enumerate(pairs)]
    for c in copies:
        c.start()
    half = keep_hbm.shape[0]
    outs = [
        pltpu.make_async_copy(hidden, hidden_hbm, osems.at[0]),
        pltpu.make_async_copy(own, own_hbm, osems.at[1]),
        pltpu.make_async_copy(tree.at[pl.ds(0, half)], keep_hbm, osems.at[2]),
        pltpu.make_async_copy(tree.at[pl.ds(half, half)], give_hbm, osems.at[3]),
    ]
    backs = [pltpu.make_async_copy(back.at[d], back_hbm[d], osems.at[4 + d]) for d in range(n_inner)]
    devices = [(o ^ fo) * n_inner + (i ^ fi) for fo, fi in offsets]
    gsrc[...] = jnp.zeros(gsrc.shape, F32)
    copies[0].wait()
    order = hub_order(hub_steps, n_inner, hd, hubx.shape[0])
    hubs = dot(order, hubx[...]).astype(BF)
    src[first_hub:] = hubs.reshape(ntiles - first_hub, tile, width)
    copies[1].wait()
    copies[2].wait()
    copies[3].wait()
    for b in range(nblocks):
        acc = jnp.zeros((tile, width), F32)
        for t in range(per_block):
            acc = acc + dot(adj[b * per_block + t], src[tile_src[b, t]])
        agg[b * tile : (b + 1) * tile, :] = acc.astype(BF)
    copies[4].wait()
    copies[5].wait()
    pre = pre0[...] + dot(agg[...], wn[...])
    copies[6].wait()
    sig = jax.nn.sigmoid(pre)
    hidden[...] = (pre * sig).astype(BF)
    outs[0].start()
    gp = (cot[...].astype(F32) * sig * (1.0 + pre * (1.0 - sig))).astype(BF)
    gagg = dot(gp, wn[...], NT).astype(BF)
    for b in range(nblocks):
        block = gagg[b * tile : (b + 1) * tile, :]
        for t in range(per_block):
            s = tile_src[b, t]
            gsrc[s] = gsrc[s] + dot(adj[b * per_block + t], block, TN)
    for d in range(n_inner):
        back[d] = gsrc[nblocks + (i ^ d)].astype(BF)
        backs[d].start()
    feat = src[0:nblocks].reshape(nblocks * tile, width)
    wacc[0:width, :] = dot(feat, gp, TN)
    wacc[width : 2 * width, :] = dot(agg[...], gp, TN)
    order = hub_order(steps, n_inner, hd, hubx.shape[0])
    hubf[...] = dot(order, gsrc[first_hub:].reshape(hubf.shape).astype(BF), TN)
    tail[...] = jnp.zeros(tail.shape, F32)
    tail[hd : hd + 1, :] = jnp.sum(gp.astype(F32), axis=0, keepdims=True)
    wrows = 2 * width // len(offsets)
    base = chunk - tail.shape[0]
    for j in reversed(range(len(devices))):
        d = devices[j]
        mine = load_rows(wacc, d * wrows, wrows)
        if base == wrows:
            tree[j * chunk : j * chunk + wrows, :] = mine.astype(BF)
        else:
            tail[8 : 8 + wrows, :] = mine
        tail[0:hd, :] = hubf[j * hd : (j + 1) * hd, :]
        tree[j * chunk + base : (j + 1) * chunk, :] = tail[...].astype(BF)
        if j * 2 == len(devices):
            outs[3].start()
    outs[2].start()
    copies[7].wait()
    own[...] = dot(gp, ws[...], NT) + gsrc[0:nblocks].reshape(own.shape)
    outs[1].start()
    for c in outs + backs:
        c.wait()


def scatter_kernel(base, hub_ref, count_ref, rows_ref, own_ref, part_ref, *rest):
    returned, (out_ref, acc) = rest[:-2], rest[-2:]
    nrows, width = own_ref.shape
    i = lax.axis_index("inner")
    acc[...] = own_ref[...]
    for d in range(0, len(returned), 2):
        put = slot_onehot(rows_ref, count_ref, nrows, (i ^ d, i ^ (d + 1)))
        acc[...] += dot(put, jnp.concatenate([returned[d][...], returned[d + 1][...]], axis=0))
    for h in range(hub_ref.shape[0]):
        r = hub_ref[h]
        acc[pl.ds(r, 1), :] = acc[pl.ds(r, 1), :] + part_ref[base + h : base + h + 1, :]
    out_ref[...] = acc[...].astype(BF)


def finish_kernel(steps, n_inner, factor, bias_row, x_ref, y_ref, part_ref, self_ref, neigh_ref, bias_ref, full):
    offsets = tree_offsets(steps)
    o = lax.axis_index("outer")
    i = lax.axis_index("inner")
    wrows = 2 * x_ref.shape[0] // len(offsets)
    width = self_ref.shape[0]
    for j, (fo, fi) in enumerate(offsets):
        d = (o ^ fo) * n_inner + (i ^ fi)
        ref, at = (x_ref, j) if 2 * j < len(offsets) else (y_ref, j - len(offsets) // 2)
        store_rows(full, d * wrows, ref[at * wrows : (at + 1) * wrows, :].astype(F32) * factor)
    self_ref[...] = full[0:width, :]
    neigh_ref[...] = full[width : 2 * width, :]
    bias_ref[...] = part_ref[bias_row : bias_row + 1, :] * factor


def params(mib):
    return pltpu.CompilerParams(vmem_limit_bytes=mib * MIB)


def nbytes(scratch):
    return sum(s.dtype.itemsize * math.prod(s.shape) for s in scratch)


def cost(flops, nbytes):
    return pl.CostEstimate(flops=flops, bytes_accessed=nbytes, transcendentals=0)


def body(
    features,
    adj_tiles,
    tile_src,
    send_rows,
    send_count,
    hub_rows,
    w_self,
    w_neigh,
    out_bias,
    cotangent,
):
    n_outer, n_inner = lax.axis_size("outer"), lax.axis_size("inner")
    ndevice = n_outer * n_inner
    nrows, width = features.shape
    tile = adj_tiles.shape[1]
    nblocks, per_block = tile_src.shape
    hd = hub_rows.shape[0]
    nhubs = hd * ndevice
    ntiles = nblocks + n_inner + nhubs // tile
    steps = tree_steps(n_outer, n_inner)
    offsets = tree_offsets(steps)
    wrows = 2 * width // ndevice
    chunk = wrows + 16 if wrows % 16 == 0 else 16
    base = chunk - 16

    outgoing, hub_own = pl.pallas_call(
        gather_kernel,
        out_shape=(
            jax.ShapeDtypeStruct((n_inner, tile, width), BF),
            jax.ShapeDtypeStruct((hd, width), BF),
        ),
        in_specs=[SM, SM, VM, VM],
        out_specs=(VM, VM),
        compiler_params=params(60),
        cost_estimate=cost(4 * 10**8, 3 * 10**6),
        name="gather_rows",
    )(hub_rows, send_count, features, send_rows)
    received = lax.all_to_all(outgoing, "inner", split_axis=0, concat_axis=0, tiled=True)
    hubx = hub_own
    for name, bit in steps[:-2]:
        hubx = lax.optimization_barrier(jnp.concatenate([hubx, exchange(hubx, name, bit)], 0))
    hubx = jnp.concatenate([hubx] + [exchange(hubx, "inner", bit) for bit in direct_bits(steps)], 0)
    hub_steps = steps[-2:] + steps[:-2][::-1]
    self_low = w_self.astype(BF)
    neigh_low = w_neigh.astype(BF)
    pre0 = jnp.dot(features, self_low, preferred_element_type=F32) + out_bias

    half = ndevice * chunk // 2
    scratch = [
        pltpu.VMEM((ntiles, tile, width), BF),
        pltpu.VMEM((nhubs, width), BF),
        pltpu.VMEM((nhubs, width), F32),
        pltpu.VMEM(adj_tiles.shape, BF),
        pltpu.VMEM((nrows, width), F32),
        pltpu.VMEM((width, width), BF),
        pltpu.VMEM((width, width), BF),
        pltpu.VMEM((nrows, width), BF),
        pltpu.VMEM((nrows, width), BF),
        pltpu.VMEM((nrows, width), BF),
        pltpu.VMEM((ntiles, tile, width), F32),
        pltpu.VMEM((n_inner, tile, width), BF),
        pltpu.VMEM((nrows, width), F32),
        pltpu.VMEM((2 * width, width), F32),
        pltpu.VMEM((16, width), F32),
        pltpu.VMEM((ndevice * chunk, width), BF),
    ]
    hidden_out, own, keep, give, *back = pl.pallas_call(
        functools.partial(middle_kernel, steps, hub_steps, chunk),
        out_shape=(
            jax.ShapeDtypeStruct((nrows, width), BF),
            jax.ShapeDtypeStruct((nrows, width), F32),
            jax.ShapeDtypeStruct((half, width), BF),
            jax.ShapeDtypeStruct((half, width), BF),
        )
        + (jax.ShapeDtypeStruct((tile, width), BF),) * n_inner,
        in_specs=[SM, HBM, ANY, ANY, HBM, ANY, ANY, ANY, HBM],
        out_specs=(ANY,) * (4 + n_inner),
        scratch_shapes=scratch
        + [
            pltpu.SemaphoreType.DMA((8,)),
            pltpu.SemaphoreType.DMA((4 + n_inner,)),
        ],
        compiler_params=params(nbytes(scratch) // MIB + 12),
        cost_estimate=cost(2 * 10**9, 9 * 10**6),
        name="middle",
    )(
        tile_src,
        features.reshape(nblocks, tile, width),
        received,
        hubx,
        adj_tiles,
        pre0,
        neigh_low,
        self_low,
        cotangent,
    )
    returned = [back[0]] + [None] * (n_inner - 1)
    far = n_inner // 2

    def start(ds, held):
        for d, value in zip(ds, held):
            returned[d] = exchange(value, "inner", d)

    def after(value, ds):
        value, held = lax.optimization_barrier((value, [returned[d] for d in ds]))
        for d, block in zip(ds, held):
            returned[d] = block
        return value

    first, second = list(range(far, n_inner - 2)), [n_inner - 2]
    third, fourth = [n_inner - 1], list(range(1, far))
    start(first + second, [back[d] for d in first + second])
    got = exchange(give, *steps[0])
    part = keep.astype(F32) + got.astype(F32)
    for k, (name, bit) in enumerate(steps[1:-2]):
        rows = part.shape[0] // 2
        send = part[rows:].astype(BF)
        if k == len(steps) - 4:
            send = after(send, first)
        part = part[:rows] + exchange(send, name, bit).astype(F32)
    quarter = part.shape[0] // 4
    pieces = [part[c * quarter : (c + 1) * quarter].astype(BF) for c in range(1, 4)]
    pieces = after(pieces, second)
    part = part[:quarter]
    for bit, piece in zip(direct_bits(steps), pieces):
        part = part + exchange(piece, "inner", bit).astype(F32)
    at = 0 if wrows % 16 == 0 else 8
    mine = part[at : at + wrows].astype(BF)
    parts = [mine] + [exchange(mine, "inner", bit) for bit in direct_bits(steps)]
    gathered = jnp.concatenate(parts, 0)
    gathered, held = lax.optimization_barrier((gathered, [back[d] for d in third + fourth]))
    start(third + fourth, held)
    for k, (name, bit) in enumerate(reversed(steps[1:-2])):
        if k == 1:
            gathered = after(gathered, third)
        gathered = lax.optimization_barrier(jnp.concatenate([gathered, exchange(gathered, name, bit)], 0))
    gathered = after(gathered, fourth)
    other = exchange(gathered, *steps[0])

    grad_features = pl.pallas_call(
        functools.partial(scatter_kernel, base),
        out_shape=jax.ShapeDtypeStruct((nrows, width), BF),
        in_specs=[SM, SM] + [VM] * (3 + n_inner),
        out_specs=VM,
        scratch_shapes=[pltpu.VMEM((nrows, width), F32)],
        compiler_params=params(24),
        cost_estimate=cost(4 * 10**8, 3 * 10**6),
        name="scatter_rows",
    )(hub_rows, send_count, send_rows, own, part, *returned)
    factor = 1.0 / float(nrows * ndevice) ** 0.5
    total_self, total_neigh, total_bias = pl.pallas_call(
        functools.partial(finish_kernel, steps, n_inner, factor, base + hd),
        out_shape=(jax.ShapeDtypeStruct((width, width), F32),) * 2 + (jax.ShapeDtypeStruct((1, width), F32),),
        in_specs=[VM] * 3,
        out_specs=(VM,) * 3,
        scratch_shapes=[pltpu.VMEM((2 * width, width), F32)],
        compiler_params=params(24),
        cost_estimate=cost(10**6, 3 * 10**6),
        name="finish",
    )(gathered, other, part)
    return hidden_out, grad_features, total_self, total_neigh, total_bias.reshape(width)


def solution(mesh):
    both = ("outer", "inner")
    return jax.shard_map(
        body,
        mesh=mesh,
        in_specs=(
            P(both, None),
            P(both, None, None),
            P(both, None),
            P(both, None),
            P(both, None),
            P(both),
            P(),
            P(),
            P(),
            P(both, None),
        ),
        out_specs=(P(both, None), P(both, None), P(), P(), P()),
        check_vma=False,
    )
```

time: 140 us -> 113 us (0.81)
  waiting for transfers between devices: 85.7 us -> 56.3 us
  starting transfers between devices: 28 us -> 38.5 us
  local copies, waits for them, and re-layouts: 9.82 us -> 2.19 us
  other arithmetic: 2.4 us -> 0.63 us
    ppermute x15 -> x25, waiting for transfers between devices: 85.7 us -> 56.3 us  [exchange(): return lax.ppermute(x, name, [(s, s ^ bit) for s in range(size)])]
    ppermute x15 -> x25, starting transfers between devices: 15.5 us -> 31.1 us  [exchange(): return lax.ppermute(x, name, [(s, s ^ bit) for s in range(size)])]
    unnamed x33 -> x22, local copies, waits for them, and re-layouts: 7.63 us -> 2.1 us
    all_to_all x1 -> x0, starting transfers between devices: 5.04 us -> none  [body(): lax.all_to_all(back, 'inner', split_axis=0, concat_axis=0, tiled=True)]
  transfers between devices with their start and end apart: 17 -> 26, of which waited for: 12 -> 20; matrix products, arithmetic and copies ran while one was open for 4% -> 1% of each run, Pallas kernels for 1% -> 2%
where the time goes in v2:
time: 113 us
  waiting for transfers between devices  56.3 us (50%)
  starting transfers between devices  38.5 us (34%)
  Pallas kernels  13.8 us (12%)
  local copies, waits for them, and re-layouts  2.19 us (2%)
    ppermute x25, waiting for transfers between devices, exchange(): return lax.ppermute(x, name, [(s, s ^ bit) for s in range(size)])  56.3 us
    ppermute x25, starting transfers between devices, exchange(): return lax.ppermute(x, name, [(s, s ^ bit) for s in range(size)])  31.1 us
    pallas_call x1, Pallas kernels, body(): pl.pallas_call(functools.partial(middle_kernel, steps, hub_steps, chunk),...  7.52 us
    all_to_all x1, starting transfers between devices, body(): lax.all_to_all(outgoing, 'inner', split_axis=0, concat_axis=0, tiled=True)  7.43 us
    pallas_call x1, Pallas kernels, body(): pl.pallas_call(gather_kernel, out_shape=(jax.ShapeDtypeStruct((n_inner, t...  2.82 us
  transfers between devices with their start and end apart: 26, of which 20 were waited for; matrix products, arithmetic and copies ran while one was open for 1% of the time, Pallas kernels for 2%

profile of v2, /device:TPU:0, one launch (start us, length us, event | category | flops | bytes accessed | tf_op | source)
XLA Modules:
  0.0 112.7 jit_solution(11266644858044157140)
XLA Ops:
  0.6 2.8 %gather_rows.1 = (bf16[8,128,512]{2,1,0:T(8,128)(2,1)}, bf16[4,512]{1,0:T(4,128)(2,1)}) custom-call(s32[4]{0:T(128)} %hub_ref.3, s32[1,8]{1,0:T(1,128)} %count_ref.3, bf16[384,512]{1,0:T(8,128)(2,1)} %feat_ref.1, s32[8,128]{1,0:T(8,128)} %rows_ref.3), custom_call_target="tpu_custom_call" | custom-call | flops 400000000 | bytes 3000000 | tf_op jit(solution)/shard_map/gather_rows/pallas_call | solution.py:290
  3.5 7.4 %all-to-all-start = ((bf16[8,128,512]{2,1,0:T(8,128)(2,1)}), bf16[8,128,512]{2,1,0:T(8,128)(2,1)S(1)}, u32[]{:S(2)}, u32[]{:S(2)}) async-start(bf16[8,128,512]{2,1,0:T(8,128)(2,1)} %get-tuple-element.40), calls=%async_computation | async-start | bytes 2097152 | tf_op jit(solution)/shard_map/all_to_all | solution.py:302
  10.9 0.1 collective-permute-start
  11.0 1.2 %collective-permute-done = bf16[4,512]{1,0:T(4,128)(2,1)S(1)} collective-permute-done((bf16[4,512]{1,0:T(4,128)(2,1)S(1)}, bf16[4,512]{1,0:T(4,128)(2,1)S(1)}, u32[]{:S(2)}, u32[]{:S(2)}) %collective-permute-start) | collective-permute-done | bytes 4128 | tf_op jit(solution)/shard_map/ppermute | solution.py:78
  12.1 1.6 %collective-permute-start.1 = (bf16[8,512]{1,0:T(8,128)(2,1)S(1)}, bf16[8,512]{1,0:T(8,128)(2,1)S(1)}, u32[]{:S(2)}, u32[]{:S(2)}) collective-permute-start(bf16[8,512]{1,0:T(8,128)(2,1)S(1)} %pad_maximum_fusion.6), channel_id=1, source_target_pairs={{0,16},{8,24},{16,0},{24,8},{1,17},{9,25},{17,1},{25,9},{2,18},{10... | collective-permute-start | bytes 24584 | tf_op jit(solution)/shard_map/ppermute | solution.py:78
  13.7 2.2 %collective-permute-done.1 = bf16[8,512]{1,0:T(8,128)(2,1)S(1)} collective-permute-done((bf16[8,512]{1,0:T(8,128)(2,1)S(1)}, bf16[8,512]{1,0:T(8,128)(2,1)S(1)}, u32[]{:S(2)}, u32[]{:S(2)}) %collective-permute-start.1) | collective-permute-done | bytes 8224 | tf_op jit(solution)/shard_map/ppermute | solution.py:78
  15.9 2.0 %collective-permute-start.2 = (bf16[16,512]{1,0:T(8,128)(2,1)S(1)}, bf16[16,512]{1,0:T(8,128)(2,1)S(1)}, u32[]{:S(2)}, u32[]{:S(2)}) collective-permute-start(bf16[16,512]{1,0:T(8,128)(2,1)S(1)} %pad_maximum_fusion.5), channel_id=1, source_target_pairs={{0,1},{1,0},{2,3},{3,2},{4,5},{5,4},{6,7},{7,6},{8,9},{9,8},{10,11... | collective-permute-start | bytes 49160 | tf_op jit(solution)/shard_map/ppermute | solution.py:78
  17.8 0.1 convert_element_type.33.ws_hbm
  17.9 2.0 %collective-permute-done.2 = bf16[16,512]{1,0:T(8,128)(2,1)S(1)} collective-permute-done((bf16[16,512]{1,0:T(8,128)(2,1)S(1)}, bf16[16,512]{1,0:T(8,128)(2,1)S(1)}, u32[]{:S(2)}, u32[]{:S(2)}) %collective-permute-start.2) | collective-permute-done | bytes 16416 | tf_op jit(solution)/shard_map/ppermute | solution.py:78
  19.9 3.6 %collective-permute-start.5 = (bf16[32,512]{1,0:T(8,128)(2,1)S(1)}, bf16[32,512]{1,0:T(8,128)(2,1)S(1)}, u32[]{:S(2)}, u32[]{:S(2)}) collective-permute-start(bf16[32,512]{1,0:T(8,128)(2,1)S(1)} %pad_maximum_fusion.4), channel_id=1, source_target_pairs={{0,6},{1,7},{2,4},{3,5},{4,2},{5,3},{6,0},{7,1},{8,14},{9,15},{10,... | collective-permute-start | bytes 98312 | tf_op jit(solution)/shard_map/ppermute | solution.py:78
  23.5 0.0 collective-permute-start.4
  23.5 0.7 collective-permute-start.3
  24.3 0.4 convolution_add_fusion.pre_hbm
  24.7 0.1 convert_element_type.34.wn_hbm
  24.8 8.6 %collective-permute-done.5 = bf16[32,512]{1,0:T(8,128)(2,1)S(1)} collective-permute-done((bf16[32,512]{1,0:T(8,128)(2,1)S(1)}, bf16[32,512]{1,0:T(8,128)(2,1)S(1)}, u32[]{:S(2)}, u32[]{:S(2)}) %collective-permute-start.5) | collective-permute-done | bytes 32800 | tf_op jit(solution)/shard_map/ppermute | solution.py:78
  33.4 0.0 collective-permute-done.4
  33.4 6.1 %collective-permute-done.3 = bf16[32,512]{1,0:T(8,128)(2,1)S(1)} collective-permute-done((bf16[32,512]{1,0:T(8,128)(2,1)S(1)}, bf16[32,512]{1,0:T(8,128)(2,1)S(1)}, u32[]{:S(2)}, u32[]{:S(2)}) %collective-permute-start.3) | collective-permute-done | bytes 32800 | tf_op jit(solution)/shard_map/ppermute | solution.py:78
  39.5 0.0 copy-start.4
  39.5 1.1 copy-done.4
  40.6 1.0 copy-done.5
  41.6 7.5 %middle.1 = (bf16[384,512]{1,0:T(8,128)(2,1)}, f32[384,512]{1,0:T(8,128)S(1)}, bf16[768,512]{1,0:T(8,128)(2,1)S(1)}, bf16[768,512]{1,0:T(8,128)(2,1)S(1)}, bf16[...) custom-call(s32[3,6]{1,0:T(4,128)S(1)} %copy-done.6, ...), custom_call_target="tpu_custom_call" | custom-call | flops 2000000000 | bytes 9000000 | tf_op jit(solution)/shard_map/middle/pallas_call | solution.py:331
  49.1 0.1 collective-permute-start.6
  49.2 2.3 %collective-permute-done.6 = bf16[768,512]{1,0:T(8,128)(2,1)S(1)} collective-permute-done((bf16[768,512]{1,0:T(8,128)(2,1)S(1)}, bf16[768,512]{1,0:T(8,128)(2,1)S(1)}, u32[]{:S(2)}, u32[]{:S(2)}) %collective-permute-start.6) | collective-permute-done | bytes 786464 | tf_op jit(solution)/shard_map/ppermute | solution.py:78
  51.5 0.2 convert_add_fusion
  51.7 0.1 slice.61
  51.7 1.6 %collective-permute-start.7 = (bf16[384,512]{1,0:T(8,128)(2,1)S(1)}, bf16[384,512]{1,0:T(8,128)(2,1)S(1)}, u32[]{:S(2)}, u32[]{:S(2)}) collective-permute-start(bf16[384,512]{1,0:T(8,128)(2,1)S(1)} %slice.61), channel_id=1, source_target_pairs={{0,16},{8,24},{16,0},{24,8},{1,17},{9,25},{17,1},{25,9},{2,18},{10... | collective-permute-start | bytes 1179656 | tf_op jit(solution)/shard_map/ppermute | solution.py:78
  53.3 0.0 collective-permute-start.8
  53.3 3.8 %collective-permute-start.9 = (bf16[128,512]{1,0:T(8,128)(2,1)S(1)}, bf16[128,512]{1,0:T(8,128)(2,1)S(1)}, u32[]{:S(2)}, u32[]{:S(2)}) collective-permute-start(bf16[128,512]{1,0:T(8,128)(2,1)S(1)} %get-tuple-element.47), channel_id=1, source_target_pairs={{0,5},{1,4},{2,7},{3,6},{4,1},{5,0},{6,3},{7,2},{8,13},{9,12},{10,... | collective-permute-start | bytes 393224 | tf_op jit(solution)/shard_map/ppermute | solution.py:78
  57.1 5.9 %collective-permute-done.7 = bf16[384,512]{1,0:T(8,128)(2,1)S(1)} collective-permute-done((bf16[384,512]{1,0:T(8,128)(2,1)S(1)}, bf16[384,512]{1,0:T(8,128)(2,1)S(1)}, u32[]{:S(2)}, u32[]{:S(2)}) %collective-permute-start.7) | collective-permute-done | bytes 393248 | tf_op jit(solution)/shard_map/ppermute | solution.py:78
  63.0 0.1 slice_add_fusion
  63.1 1.7 %collective-permute-done.8.rest_4_ = bf16[128,512]{1,0:T(8,128)(2,1)S(1)} collective-permute-done((bf16[128,512]{1,0:T(8,128)(2,1)S(1)}, bf16[128,512]{1,0:T(8,128)(2,1)S(1)}, u32[]{:S(2)}, u32[]{:S(2)}) %collective-permute-start.8) | collective-permute-done | bytes 131104 | tf_op jit(solution)/shard_map/ppermute | solution.py:78
  64.8 3.6 %collective-permute-done.9.rest_5_ = bf16[128,512]{1,0:T(8,128)(2,1)S(1)} collective-permute-done((bf16[128,512]{1,0:T(8,128)(2,1)S(1)}, bf16[128,512]{1,0:T(8,128)(2,1)S(1)}, u32[]{:S(2)}, u32[]{:S(2)}) %collective-permute-start.9) | collective-permute-done | bytes 131104 | tf_op jit(solution)/shard_map/ppermute | solution.py:78
  68.4 0.6 collective-permute-start.10
  69.0 1.5 %collective-permute-start.11 = (bf16[128,512]{1,0:T(8,128)(2,1)S(1)}, bf16[128,512]{1,0:T(8,128)(2,1)S(1)}, u32[]{:S(2)}, u32[]{:S(2)}) collective-permute-start(bf16[128,512]{1,0:T(8,128)(2,1)S(1)} %get-tuple-element.49), channel_id=1, source_target_pairs={{0,6},{1,7},{2,4},{3,5},{4,2},{5,3},{6,0},{7,1},{8,14},{9,15},{10,... | collective-permute-start | bytes 393224 | tf_op jit(solution)/shard_map/ppermute | solution.py:78
  70.5 4.7 %collective-permute-done.10 = bf16[192,512]{1,0:T(8,128)(2,1)S(1)} collective-permute-done((bf16[192,512]{1,0:T(8,128)(2,1)S(1)}, bf16[192,512]{1,0:T(8,128)(2,1)S(1)}, u32[]{:S(2)}, u32[]{:S(2)}) %collective-permute-start.10) | collective-permute-done | bytes 196640 | tf_op jit(solution)/shard_map/ppermute | solution.py:78
  75.2 0.1 fusion.2
  75.3 0.0 copy-start.1
  75.3 0.0 copy-start.2
  75.3 0.0 copy-start.3
  75.3 0.6 collective-permute-done.11.rest_6_
  76.0 2.0 %collective-permute-start.13 = (bf16[48,512]{1,0:T(8,128)(2,1)S(1)}, bf16[48,512]{1,0:T(8,128)(2,1)S(1)}, u32[]{:S(2)}, u32[]{:S(2)}) collective-permute-start(bf16[48,512]{1,0:T(8,128)(2,1)S(1)} %get-tuple-element.51), channel_id=1, source_target_pairs={{0,2},{1,3},{2,0},{3,1},{4,6},{5,7},{6,4},{7,5},{8,10},{9,11},{10,... | collective-permute-start | bytes 147464 | tf_op jit(solution)/shard_map/ppermute | solution.py:78
  78.0 2.4 %collective-permute-start.14 = (bf16[48,512]{1,0:T(8,128)(2,1)S(1)}, bf16[48,512]{1,0:T(8,128)(2,1)S(1)}, u32[]{:S(2)}, u32[]{:S(2)}) collective-permute-start(bf16[48,512]{1,0:T(8,128)(2,1)S(1)} %get-tuple-element.52), channel_id=1, source_target_pairs={{0,6},{1,7},{2,4},{3,5},{4,2},{5,3},{6,0},{7,1},{8,14},{9,15},{10,... | collective-permute-start | bytes 147464 | tf_op jit(solution)/shard_map/ppermute | solution.py:78
  80.3 1.1 %collective-permute-done.12 = bf16[48,512]{1,0:T(8,128)(2,1)S(1)} collective-permute-done((bf16[48,512]{1,0:T(8,128)(2,1)S(1)}, bf16[48,512]{1,0:T(8,128)(2,1)S(1)}, u32[]{:S(2)}, u32[]{:S(2)}) %collective-permute-start.12) | collective-permute-done | bytes 49184 | tf_op jit(solution)/shard_map/ppermute | solution.py:78
  81.5 2.4 %collective-permute-done.14 = bf16[48,512]{1,0:T(8,128)(2,1)S(1)} collective-permute-done((bf16[48,512]{1,0:T(8,128)(2,1)S(1)}, bf16[48,512]{1,0:T(8,128)(2,1)S(1)}, u32[]{:S(2)}, u32[]{:S(2)}) %collective-permute-start.14) | collective-permute-done | bytes 49184 | tf_op jit(solution)/shard_map/ppermute | solution.py:78
  83.9 2.4 %collective-permute-start.17 = (bf16[32,512]{1,0:T(8,128)(2,1)S(1)}, bf16[32,512]{1,0:T(8,128)(2,1)S(1)}, u32[]{:S(2)}, u32[]{:S(2)}) collective-permute-start(bf16[32,512]{1,0:T(8,128)(2,1)S(1)} %slice.63), channel_id=1, source_target_pairs={{0,6},{1,7},{2,4},{3,5},{4,2},{5,3},{6,0},{7,1},{8,14},{9,15},{10,... | collective-permute-start | bytes 98312 | tf_op jit(solution)/shard_map/ppermute | solution.py:78
  86.3 0.0 collective-permute-start.16
  86.3 2.0 %collective-permute-start.15 = (bf16[32,512]{1,0:T(8,128)(2,1)S(1)}, bf16[32,512]{1,0:T(8,128)(2,1)S(1)}, u32[]{:S(2)}, u32[]{:S(2)}) collective-permute-start(bf16[32,512]{1,0:T(8,128)(2,1)S(1)} %slice.63), channel_id=1, source_target_pairs={{0,4},{1,5},{2,6},{3,7},{4,0},{5,1},{6,2},{7,3},{8,12},{9,13},{10,... | collective-permute-start | bytes 98312 | tf_op jit(solution)/shard_map/ppermute | solution.py:78
  88.3 1.3 %collective-permute-done.17 = bf16[32,512]{1,0:T(8,128)(2,1)S(1)} collective-permute-done((bf16[32,512]{1,0:T(8,128)(2,1)S(1)}, bf16[32,512]{1,0:T(8,128)(2,1)S(1)}, u32[]{:S(2)}, u32[]{:S(2)}) %collective-permute-start.17) | collective-permute-done | bytes 32800 | tf_op jit(solution)/shard_map/ppermute | solution.py:78
  89.7 0.6 collective-permute-done.16
  90.3 0.9 collective-permute-done.15
  91.2 1.5 %collective-permute-start.18 = (bf16[128,512]{1,0:T(8,128)(2,1)S(1)}, bf16[128,512]{1,0:T(8,128)(2,1)S(1)}, u32[]{:S(2)}, u32[]{:S(2)}) collective-permute-start(bf16[128,512]{1,0:T(8,128)(2,1)S(1)} %pad_maximum_fusion.3), channel_id=1, source_target_pairs={{0,1},{1,0},{2,3},{3,2},{4,5},{5,4},{6,7},{7,6},{8,9},{9,8},{10,11... | collective-permute-start | bytes 393224 | tf_op jit(solution)/shard_map/ppermute | solution.py:78
  92.7 1.5 %collective-permute-start.19 = (bf16[128,512]{1,0:T(8,128)(2,1)S(1)}, bf16[128,512]{1,0:T(8,128)(2,1)S(1)}, u32[]{:S(2)}, u32[]{:S(2)}) collective-permute-start(bf16[128,512]{1,0:T(8,128)(2,1)S(1)} %get-tuple-element.59), channel_id=1, source_target_pairs={{0,7},{1,6},{2,5},{3,4},{4,3},{5,2},{6,1},{7,0},{8,15},{9,14},{10,... | collective-permute-start | bytes 393224 | tf_op jit(solution)/shard_map/ppermute | solution.py:78
  94.2 2.2 %collective-permute-done.18 = bf16[128,512]{1,0:T(8,128)(2,1)S(1)} collective-permute-done((bf16[128,512]{1,0:T(8,128)(2,1)S(1)}, bf16[128,512]{1,0:T(8,128)(2,1)S(1)}, u32[]{:S(2)}, u32[]{:S(2)}) %collective-permute-start.18) | collective-permute-done | bytes 131104 | tf_op jit(solution)/shard_map/ppermute | solution.py:78
  96.4 4.4 %collective-permute-done.19.rest_7_ = bf16[128,512]{1,0:T(8,128)(2,1)S(1)} collective-permute-done((bf16[128,512]{1,0:T(8,128)(2,1)S(1)}, bf16[128,512]{1,0:T(8,128)(2,1)S(1)}, u32[]{:S(2)}, u32[]{:S(2)}) %collective-permute-start.19) | collective-permute-done | bytes 131104 | tf_op jit(solution)/shard_map/ppermute | solution.py:78
  100.8 0.3 collective-permute-start.20
  101.1 0.6 collective-permute-start.21
  101.7 1.6 %collective-permute-start.22 = (bf16[128,512]{1,0:T(8,128)(2,1)S(1)}, bf16[128,512]{1,0:T(8,128)(2,1)S(1)}, u32[]{:S(2)}, u32[]{:S(2)}) collective-permute-start(bf16[128,512]{1,0:T(8,128)(2,1)S(1)} %get-tuple-element.62), channel_id=1, source_target_pairs={{0,2},{1,3},{2,0},{3,1},{4,6},{5,7},{6,4},{7,5},{8,10},{9,11},{10,... | collective-permute-start | bytes 393224 | tf_op jit(solution)/shard_map/ppermute | solution.py:78
  103.3 1.3 %collective-permute-start.23 = (bf16[128,512]{1,0:T(8,128)(2,1)S(1)}, bf16[128,512]{1,0:T(8,128)(2,1)S(1)}, u32[]{:S(2)}, u32[]{:S(2)}) collective-permute-start(bf16[128,512]{1,0:T(8,128)(2,1)S(1)} %get-tuple-element.63), channel_id=1, source_target_pairs={{0,3},{1,2},{2,1},{3,0},{4,7},{5,6},{6,5},{7,4},{8,11},{9,10},{10,... | collective-permute-start | bytes 393224 | tf_op jit(solution)/shard_map/ppermute | solution.py:78
  104.6 2.6 %collective-permute-done.20 = bf16[256,512]{1,0:T(8,128)(2,1)S(1)} collective-permute-done((bf16[256,512]{1,0:T(8,128)(2,1)S(1)}, bf16[256,512]{1,0:T(8,128)(2,1)S(1)}, u32[]{:S(2)}, u32[]{:S(2)}) %collective-permute-start.20) | collective-permute-done | bytes 262176 | tf_op jit(solution)/shard_map/ppermute | solution.py:78
  107.2 0.0 collective-permute-done.21.rest_1_
  107.2 0.0 collective-permute-done.22.rest_2_
  107.2 1.9 %collective-permute-done.23.rest_3_ = bf16[128,512]{1,0:T(8,128)(2,1)S(1)} collective-permute-done((bf16[128,512]{1,0:T(8,128)(2,1)S(1)}, bf16[128,512]{1,0:T(8,128)(2,1)S(1)}, u32[]{:S(2)}, u32[]{:S(2)}) %collective-permute-start.23) | collective-permute-done | bytes 131104 | tf_op jit(solution)/shard_map/ppermute | solution.py:78
  109.2 1.9 %scatter_rows.1 = bf16[384,512]{1,0:T(8,128)(2,1)} custom-call(s32[4]{0:T(128)S(1)} %copy-done.2, s32[1,8]{1,0:T(1,128)S(1)} %copy-done.3, s32[8,128]{1,0:T(8,128)S(1)} %copy-done.1, f32[384,512]{1,0:T(8,128)S(1)} %get-tuple-element.43.own_ref, f32[48,512]{1,0:T(8,128)S(1)} %fusion.1.part_ref, bf16[128,512]{1,0:T(8,128)(2,1)S(1)} %get-tuple-element.53.rest_0_, ...), custom_call_target="tpu_custom_call" | custom-call | flops 400000000 | bytes 3000000 | tf_op jit(solution)/shard_map/scatter_rows/pallas_call | solution.py:404
  111.1 1.6 %finish.1 = (f32[512,512]{1,0:T(8,128)}, f32[512,512]{1,0:T(8,128)}, f32[1,512]{1,0:T(1,128)}) custom-call(bf16[512,512]{1,0:T(8,128)(2,1)S(1)} %pad_maximum_fusion.x_ref, bf16[512,512]{1,0:T(8,128)(2,1)S(1)} %collective-permute-done.24.y_ref, f32[48,512]{1,0:T(8,128)S(1)} %fusion.1.part_ref), custom_call_target="tpu_custom_call" | custom-call | flops 1000000 | bytes 3000000 | tf_op jit(solution)/shard_map/finish/pallas_call | solution.py:415
  (32 shorter events, 0.2 us)
Async XLA Ops:
  0.6 17.2 %copy-start.7 = (f32[512,512]{1,0:T(8,128)S(1)}, f32[512,512]{1,0:T(8,128)}, u32[]{:S(2)}) copy-start(f32[512,512]{1,0:T(8,128)} %param.16) | copy-start | bytes 3145732
  3.5 7.4 %copy-start.9 = (bf16[4,512]{1,0:T(4,128)(2,1)S(1)}, bf16[4,512]{1,0:T(4,128)(2,1)}, u32[]{:S(2)}) copy-start(bf16[4,512]{1,0:T(4,128)(2,1)} %get-tuple-element.41) | copy-start | bytes 12292
  3.5 20.8 %copy-start = (bf16[384,512]{1,0:T(8,128)(2,1)S(1)}, bf16[384,512]{1,0:T(8,128)(2,1)}, u32[]{:S(2)}) copy-start(bf16[384,512]{1,0:T(8,128)(2,1)} %feat_ref.1) | copy-start | bytes 1179652
  3.5 20.8 %copy-start.10 = (f32[512]{0:T(512)S(1)}, f32[512]{0:T(512)}, u32[]{:S(2)}) copy-start(f32[512]{0:T(512)} %param.18) | copy-start | bytes 6148
  3.5 36.0 %all-to-all-start = ((bf16[8,128,512]{2,1,0:T(8,128)(2,1)}), bf16[8,128,512]{2,1,0:T(8,128)(2,1)S(1)}, u32[]{:S(2)}, u32[]{:S(2)}) async-start(bf16[8,128,512]{2,1,0:T(8,128)(2,1)} %get-tuple-element.40), calls=%async_computation | async-start | bytes 2097152 | tf_op jit(solution)/shard_map/all_to_all | solution.py:302
  10.9 1.2 %collective-permute-start = (bf16[4,512]{1,0:T(4,128)(2,1)S(1)}, bf16[4,512]{1,0:T(4,128)(2,1)S(1)}, u32[]{:S(2)}, u32[]{:S(2)}) collective-permute-start(bf16[4,512]{1,0:T(4,128)(2,1)S(1)} %copy-done.9), channel_id=1, source_target_pairs={{0,8},{8,0},{16,24},{24,16},{1,9},{9,1},{17,25},{25,17},{2,10},{10... | collective-permute-start | bytes 12296 | tf_op jit(solution)/shard_map/ppermute | solution.py:78
  12.1 3.7 %collective-permute-start.1 = (bf16[8,512]{1,0:T(8,128)(2,1)S(1)}, bf16[8,512]{1,0:T(8,128)(2,1)S(1)}, u32[]{:S(2)}, u32[]{:S(2)}) collective-permute-start(bf16[8,512]{1,0:T(8,128)(2,1)S(1)} %pad_maximum_fusion.6), channel_id=1, source_target_pairs={{0,16},{8,24},{16,0},{24,8},{1,17},{9,25},{17,1},{25,9},{2,18},{10... | collective-permute-start | bytes 24584 | tf_op jit(solution)/shard_map/ppermute | solution.py:78
  15.9 8.8 %copy-start.8 = (f32[512,512]{1,0:T(8,128)S(1)}, f32[512,512]{1,0:T(8,128)}, u32[]{:S(2)}) copy-start(f32[512,512]{1,0:T(8,128)} %param.17) | copy-start | bytes 3145732
  15.9 4.0 %collective-permute-start.2 = (bf16[16,512]{1,0:T(8,128)(2,1)S(1)}, bf16[16,512]{1,0:T(8,128)(2,1)S(1)}, u32[]{:S(2)}, u32[]{:S(2)}) collective-permute-start(bf16[16,512]{1,0:T(8,128)(2,1)S(1)} %pad_maximum_fusion.5), channel_id=1, source_target_pairs={{0,1},{1,0},{2,3},{3,2},{4,5},{5,4},{6,7},{7,6},{8,9},{9,8},{10,11... | collective-permute-start | bytes 49160 | tf_op jit(solution)/shard_map/ppermute | solution.py:78
  19.9 19.6 %copy-start.6 = (s32[3,6]{1,0:T(4,128)S(1)}, s32[3,6]{1,0:T(4,128)}, u32[]{:S(2)}) copy-start(s32[3,6]{1,0:T(4,128)} %tile_src.1) | copy-start | bytes 220
  19.9 13.5 %collective-permute-start.5 = (bf16[32,512]{1,0:T(8,128)(2,1)S(1)}, bf16[32,512]{1,0:T(8,128)(2,1)S(1)}, u32[]{:S(2)}, u32[]{:S(2)}) collective-permute-start(bf16[32,512]{1,0:T(8,128)(2,1)S(1)} %pad_maximum_fusion.4), channel_id=1, source_target_pairs={{0,6},{1,7},{2,4},{3,5},{4,2},{5,3},{6,0},{7,1},{8,14},{9,15},{10,... | collective-permute-start | bytes 98312 | tf_op jit(solution)/shard_map/ppermute | solution.py:78
  23.5 9.8 %collective-permute-start.4 = (bf16[32,512]{1,0:T(8,128)(2,1)S(1)}, bf16[32,512]{1,0:T(8,128)(2,1)S(1)}, u32[]{:S(2)}, u32[]{:S(2)}) collective-permute-start(bf16[32,512]{1,0:T(8,128)(2,1)S(1)} %pad_maximum_fusion.4), channel_id=1, source_target_pairs={{0,2},{1,3},{2,0},{3,1},{4,6},{5,7},{6,4},{7,5},{8,10},{9,11},{10,... | collective-permute-start | bytes 98312 | tf_op jit(solution)/shard_map/ppermute | solution.py:78
  23.5 15.9 %collective-permute-start.3 = (bf16[32,512]{1,0:T(8,128)(2,1)S(1)}, bf16[32,512]{1,0:T(8,128)(2,1)S(1)}, u32[]{:S(2)}, u32[]{:S(2)}) collective-permute-start(bf16[32,512]{1,0:T(8,128)(2,1)S(1)} %pad_maximum_fusion.4), channel_id=1, source_target_pairs={{0,4},{1,5},{2,6},{3,7},{4,0},{5,1},{6,2},{7,3},{8,12},{9,13},{10,... | collective-permute-start | bytes 98312 | tf_op jit(solution)/shard_map/ppermute | solution.py:78
  39.5 1.1 copy-start.4
  40.6 1.0 copy-start.5
  49.1 2.4 %collective-permute-start.6 = (bf16[768,512]{1,0:T(8,128)(2,1)S(1)}, bf16[768,512]{1,0:T(8,128)(2,1)S(1)}, u32[]{:S(2)}, u32[]{:S(2)}) collective-permute-start(bf16[768,512]{1,0:T(8,128)(2,1)S(1)} %get-tuple-element.45), channel_id=1, source_target_pairs={{0,8},{8,0},{16,24},{24,16},{1,9},{9,1},{17,25},{25,17},{2,10},{10... | collective-permute-start | bytes 2359304 | tf_op jit(solution)/shard_map/ppermute | solution.py:78
  51.7 11.2 %collective-permute-start.7 = (bf16[384,512]{1,0:T(8,128)(2,1)S(1)}, bf16[384,512]{1,0:T(8,128)(2,1)S(1)}, u32[]{:S(2)}, u32[]{:S(2)}) collective-permute-start(bf16[384,512]{1,0:T(8,128)(2,1)S(1)} %slice.61), channel_id=1, source_target_pairs={{0,16},{8,24},{16,0},{24,8},{1,17},{9,25},{17,1},{25,9},{2,18},{10... | collective-permute-start | bytes 1179656 | tf_op jit(solution)/shard_map/ppermute | solution.py:78
  53.3 11.5 %collective-permute-start.8 = (bf16[128,512]{1,0:T(8,128)(2,1)S(1)}, bf16[128,512]{1,0:T(8,128)(2,1)S(1)}, u32[]{:S(2)}, u32[]{:S(2)}) collective-permute-start(bf16[128,512]{1,0:T(8,128)(2,1)S(1)} %get-tuple-element.46), channel_id=1, source_target_pairs={{0,4},{1,5},{2,6},{3,7},{4,0},{5,1},{6,2},{7,3},{8,12},{9,13},{10,... | collective-permute-start | bytes 393224 | tf_op jit(solution)/shard_map/ppermute | solution.py:78
  53.3 15.1 %collective-permute-start.9 = (bf16[128,512]{1,0:T(8,128)(2,1)S(1)}, bf16[128,512]{1,0:T(8,128)(2,1)S(1)}, u32[]{:S(2)}, u32[]{:S(2)}) collective-permute-start(bf16[128,512]{1,0:T(8,128)(2,1)S(1)} %get-tuple-element.47), channel_id=1, source_target_pairs={{0,5},{1,4},{2,7},{3,6},{4,1},{5,0},{6,3},{7,2},{8,13},{9,12},{10,... | collective-permute-start | bytes 393224 | tf_op jit(solution)/shard_map/ppermute | solution.py:78
  68.4 6.8 %collective-permute-start.10 = (bf16[192,512]{1,0:T(8,128)(2,1)S(1)}, bf16[192,512]{1,0:T(8,128)(2,1)S(1)}, u32[]{:S(2)}, u32[]{:S(2)}) collective-permute-start(bf16[192,512]{1,0:T(8,128)(2,1)S(1)} %slice.62), channel_id=1, source_target_pairs={{0,1},{1,0},{2,3},{3,2},{4,5},{5,4},{6,7},{7,6},{8,9},{9,8},{10,11... | collective-permute-start | bytes 589832 | tf_op jit(solution)/shard_map/ppermute | solution.py:78
  69.0 6.9 %collective-permute-start.11 = (bf16[128,512]{1,0:T(8,128)(2,1)S(1)}, bf16[128,512]{1,0:T(8,128)(2,1)S(1)}, u32[]{:S(2)}, u32[]{:S(2)}) collective-permute-start(bf16[128,512]{1,0:T(8,128)(2,1)S(1)} %get-tuple-element.49), channel_id=1, source_target_pairs={{0,6},{1,7},{2,4},{3,5},{4,2},{5,3},{6,0},{7,1},{8,14},{9,15},{10,... | collective-permute-start | bytes 393224 | tf_op jit(solution)/shard_map/ppermute | solution.py:78
  75.3 33.9 %copy-start.1 = (s32[8,128]{1,0:T(8,128)S(1)}, s32[8,128]{1,0:T(8,128)}, u32[]{:S(2)}) copy-start(s32[8,128]{1,0:T(8,128)} %rows_ref.3) | copy-start | bytes 12292
  75.3 33.9 %copy-start.2 = (s32[4]{0:T(128)S(1)}, s32[4]{0:T(128)}, u32[]{:S(2)}) copy-start(s32[4]{0:T(128)} %hub_ref.3) | copy-start | bytes 52
  75.3 33.9 %copy-start.3 = (s32[1,8]{1,0:T(1,128)S(1)}, s32[1,8]{1,0:T(1,128)}, u32[]{:S(2)}) copy-start(s32[1,8]{1,0:T(1,128)} %count_ref.3) | copy-start | bytes 100
  76.0 5.5 %collective-permute-start.12 = (bf16[48,512]{1,0:T(8,128)(2,1)S(1)}, bf16[48,512]{1,0:T(8,128)(2,1)S(1)}, u32[]{:S(2)}, u32[]{:S(2)}) collective-permute-start(bf16[48,512]{1,0:T(8,128)(2,1)S(1)} %get-tuple-element.50), channel_id=1, source_target_pairs={{0,4},{1,5},{2,6},{3,7},{4,0},{5,1},{6,2},{7,3},{8,12},{9,13},{10,... | collective-permute-start | bytes 147464 | tf_op jit(solution)/shard_map/ppermute | solution.py:78
  76.0 5.5 %collective-permute-start.13 = (bf16[48,512]{1,0:T(8,128)(2,1)S(1)}, bf16[48,512]{1,0:T(8,128)(2,1)S(1)}, u32[]{:S(2)}, u32[]{:S(2)}) collective-permute-start(bf16[48,512]{1,0:T(8,128)(2,1)S(1)} %get-tuple-element.51), channel_id=1, source_target_pairs={{0,2},{1,3},{2,0},{3,1},{4,6},{5,7},{6,4},{7,5},{8,10},{9,11},{10,... | collective-permute-start | bytes 147464 | tf_op jit(solution)/shard_map/ppermute | solution.py:78
  78.0 5.9 %collective-permute-start.14 = (bf16[48,512]{1,0:T(8,128)(2,1)S(1)}, bf16[48,512]{1,0:T(8,128)(2,1)S(1)}, u32[]{:S(2)}, u32[]{:S(2)}) collective-permute-start(bf16[48,512]{1,0:T(8,128)(2,1)S(1)} %get-tuple-element.52), channel_id=1, source_target_pairs={{0,6},{1,7},{2,4},{3,5},{4,2},{5,3},{6,0},{7,1},{8,14},{9,15},{10,... | collective-permute-start | bytes 147464 | tf_op jit(solution)/shard_map/ppermute | solution.py:78
  83.9 5.8 %collective-permute-start.17 = (bf16[32,512]{1,0:T(8,128)(2,1)S(1)}, bf16[32,512]{1,0:T(8,128)(2,1)S(1)}, u32[]{:S(2)}, u32[]{:S(2)}) collective-permute-start(bf16[32,512]{1,0:T(8,128)(2,1)S(1)} %slice.63), channel_id=1, source_target_pairs={{0,6},{1,7},{2,4},{3,5},{4,2},{5,3},{6,0},{7,1},{8,14},{9,15},{10,... | collective-permute-start | bytes 98312 | tf_op jit(solution)/shard_map/ppermute | solution.py:78
  86.3 3.9 %collective-permute-start.16 = (bf16[32,512]{1,0:T(8,128)(2,1)S(1)}, bf16[32,512]{1,0:T(8,128)(2,1)S(1)}, u32[]{:S(2)}, u32[]{:S(2)}) collective-permute-start(bf16[32,512]{1,0:T(8,128)(2,1)S(1)} %slice.63), channel_id=1, source_target_pairs={{0,2},{1,3},{2,0},{3,1},{4,6},{5,7},{6,4},{7,5},{8,10},{9,11},{10,... | collective-permute-start | bytes 98312 | tf_op jit(solution)/shard_map/ppermute | solution.py:78
  86.3 4.8 %collective-permute-start.15 = (bf16[32,512]{1,0:T(8,128)(2,1)S(1)}, bf16[32,512]{1,0:T(8,128)(2,1)S(1)}, u32[]{:S(2)}, u32[]{:S(2)}) collective-permute-start(bf16[32,512]{1,0:T(8,128)(2,1)S(1)} %slice.63), channel_id=1, source_target_pairs={{0,4},{1,5},{2,6},{3,7},{4,0},{5,1},{6,2},{7,3},{8,12},{9,13},{10,... | collective-permute-start | bytes 98312 | tf_op jit(solution)/shard_map/ppermute | solution.py:78
  91.2 5.2 %collective-permute-start.18 = (bf16[128,512]{1,0:T(8,128)(2,1)S(1)}, bf16[128,512]{1,0:T(8,128)(2,1)S(1)}, u32[]{:S(2)}, u32[]{:S(2)}) collective-permute-start(bf16[128,512]{1,0:T(8,128)(2,1)S(1)} %pad_maximum_fusion.3), channel_id=1, source_target_pairs={{0,1},{1,0},{2,3},{3,2},{4,5},{5,4},{6,7},{7,6},{8,9},{9,8},{10,11... | collective-permute-start | bytes 393224 | tf_op jit(solution)/shard_map/ppermute | solution.py:78
  92.7 8.1 %collective-permute-start.19 = (bf16[128,512]{1,0:T(8,128)(2,1)S(1)}, bf16[128,512]{1,0:T(8,128)(2,1)S(1)}, u32[]{:S(2)}, u32[]{:S(2)}) collective-permute-start(bf16[128,512]{1,0:T(8,128)(2,1)S(1)} %get-tuple-element.59), channel_id=1, source_target_pairs={{0,7},{1,6},{2,5},{3,4},{4,3},{5,2},{6,1},{7,0},{8,15},{9,14},{10,... | collective-permute-start | bytes 393224 | tf_op jit(solution)/shard_map/ppermute | solution.py:78
  100.8 6.4 %collective-permute-start.20 = (bf16[256,512]{1,0:T(8,128)(2,1)S(1)}, bf16[256,512]{1,0:T(8,128)(2,1)S(1)}, u32[]{:S(2)}, u32[]{:S(2)}) collective-permute-start(bf16[256,512]{1,0:T(8,128)(2,1)S(1)} %pad_maximum_fusion.1), channel_id=1, source_target_pairs={{0,16},{8,24},{16,0},{24,8},{1,17},{9,25},{17,1},{25,9},{2,18},{10... | collective-permute-start | bytes 786440 | tf_op jit(solution)/shard_map/ppermute | solution.py:78
  101.1 6.1 %collective-permute-start.21 = (bf16[128,512]{1,0:T(8,128)(2,1)S(1)}, bf16[128,512]{1,0:T(8,128)(2,1)S(1)}, u32[]{:S(2)}, u32[]{:S(2)}) collective-permute-start(bf16[128,512]{1,0:T(8,128)(2,1)S(1)} %get-tuple-element.61), channel_id=1, source_target_pairs={{0,1},{1,0},{2,3},{3,2},{4,5},{5,4},{6,7},{7,6},{8,9},{9,8},{10,11... | collective-permute-start | bytes 393224 | tf_op jit(solution)/shard_map/ppermute | solution.py:78
  101.7 5.6 %collective-permute-start.22 = (bf16[128,512]{1,0:T(8,128)(2,1)S(1)}, bf16[128,512]{1,0:T(8,128)(2,1)S(1)}, u32[]{:S(2)}, u32[]{:S(2)}) collective-permute-start(bf16[128,512]{1,0:T(8,128)(2,1)S(1)} %get-tuple-element.62), channel_id=1, source_target_pairs={{0,2},{1,3},{2,0},{3,1},{4,6},{5,7},{6,4},{7,5},{8,10},{9,11},{10,... | collective-permute-start | bytes 393224 | tf_op jit(solution)/shard_map/ppermute | solution.py:78
  103.3 5.9 %collective-permute-start.23 = (bf16[128,512]{1,0:T(8,128)(2,1)S(1)}, bf16[128,512]{1,0:T(8,128)(2,1)S(1)}, u32[]{:S(2)}, u32[]{:S(2)}) collective-permute-start(bf16[128,512]{1,0:T(8,128)(2,1)S(1)} %get-tuple-element.63), channel_id=1, source_target_pairs={{0,3},{1,2},{2,1},{3,0},{4,7},{5,6},{6,5},{7,4},{8,11},{9,10},{10,... | collective-permute-start | bytes 393224 | tf_op jit(solution)/shard_map/ppermute | solution.py:78
  109.2 1.9 %collective-permute-start.24 = (bf16[512,512]{1,0:T(8,128)(2,1)S(1)}, bf16[512,512]{1,0:T(8,128)(2,1)S(1)}, u32[]{:S(2)}, u32[]{:S(2)}) collective-permute-start(bf16[512,512]{1,0:T(8,128)(2,1)S(1)} %pad_maximum_fusion.x_ref), channel_id=1, source_target_pairs={{0,8},{8,0},{16,24},{24,16},{1,9},{9,1},{17,25},{25,17},{2,10},{10... | collective-permute-start | bytes 1572872 | tf_op jit(solution)/shard_map/ppermute | solution.py:78

commit v3 on v0

v3 whole, which is shorter than its diff:
```python
import functools
import math

import jax
import jax.numpy as jnp
from jax import lax
from jax.experimental import pallas as pl
from jax.experimental.pallas import tpu as pltpu
from jax.sharding import PartitionSpec as P

BF = jnp.bfloat16
F32 = jnp.float32
VM = pl.BlockSpec(memory_space=pltpu.VMEM)
SM = pl.BlockSpec(memory_space=pltpu.SMEM)
MIB = 1024 * 1024
TN = (((0,), (0,)), ((), ()))
NT = (((1,), (1,)), ((), ()))


def dot(a, b, dims=(((1,), (0,)), ((), ()))):
    return lax.dot_general(a, b, dims, preferred_element_type=F32)


def tree_groups(n_outer, n_inner):
    steps = []
    bit = 1
    while bit < n_outer:
        steps.append((bit, 0))
        bit *= 2
    bit = 1
    while bit < n_inner:
        steps.append((0, bit))
        bit *= 2
    middle = steps[1:-2]
    return [steps[:1]] + [middle[k : k + 2] for k in range(0, len(middle), 2)] + [steps[-2:]]


def flips(steps):
    count = len(steps)
    table = []
    for slot in range(2**count):
        fo = fi = 0
        for k, (bo, bi) in enumerate(steps):
            if (slot >> (count - 1 - k)) & 1:
                fo, fi = fo ^ bo, fi ^ bi
        table.append((fo, fi))
    return table


def hub_order(steps, n_inner, hd, nhubs):
    me = lax.axis_index("outer") * n_inner + lax.axis_index("inner")
    column = lax.broadcasted_iota(jnp.int32, (1, nhubs), 1)
    slot = column // hd
    flip = jnp.zeros((1, nhubs), jnp.int32)
    for k, (bo, bi) in enumerate(steps):
        flip = flip + ((slot >> (len(steps) - 1 - k)) & 1) * (bo * n_inner + bi)
    target = (flip ^ me) * hd + column % hd
    row = lax.broadcasted_iota(jnp.int32, (nhubs, nhubs), 0)
    return (row == target).astype(F32).astype(BF)


def load_rows(ref, at, n):
    if n % 8 == 0:
        return ref[pl.ds(pl.multiple_of(at, n), n), :]
    return jnp.concatenate([ref[pl.ds(at + r, 1), :] for r in range(n)], axis=0)


def store_rows(ref, at, value):
    n = value.shape[0]
    if n % 8 == 0:
        ref[pl.ds(pl.multiple_of(at, n), n), :] = value
    else:
        for r in range(n):
            ref[pl.ds(at + r, 1), :] = value[r : r + 1, :]


def exchange(x, flip):
    n_outer, n_inner = lax.axis_size("outer"), lax.axis_size("inner")
    mask = flip[0] * n_inner + flip[1]
    return lax.ppermute(x, ("outer", "inner"), [(s, s ^ mask) for s in range(n_outer * n_inner)])


def spread(x, group):
    parts = [x] + [exchange(x, flip) for flip in flips(group)[1:]]
    return lax.optimization_barrier(jnp.concatenate(parts, 0))


def slot_onehot(rows_ref, count_ref, nrows, partners):
    slots = rows_ref.shape[1]
    sub = lax.broadcasted_iota(jnp.int32, (nrows, slots), 0)
    lane = lax.broadcasted_iota(jnp.int32, (1, slots), 1)
    parts = []
    for q in partners:
        live = jnp.where(lane < count_ref[0, q], rows_ref[pl.ds(q, 1), :], -1)
        parts.append((sub == live).astype(F32).astype(BF))
    return jnp.concatenate(parts, axis=1)


def gather_kernel(hub_ref, count_ref, feat_ref, rows_ref, hub_out_ref, *outs):
    nrows = feat_ref.shape[0]
    slots = rows_ref.shape[1]
    nhub = hub_ref.shape[0]
    i = lax.axis_index("inner")
    feat = feat_ref[...]
    sub = lax.broadcasted_iota(jnp.int32, (16, nrows), 0)
    lane = lax.broadcasted_iota(jnp.int32, (16, nrows), 1)
    hot = jnp.zeros((16, nrows), F32)
    for h in range(nhub):
        hot = hot + ((sub == h) & (lane == hub_ref[h])).astype(F32)
    hub_out_ref[...] = dot(hot.astype(BF), feat)[:nhub].astype(BF)
    pick = slot_onehot(rows_ref, count_ref, nrows, [i ^ d for d in range(len(outs))])
    rows = dot(pick, feat, TN).astype(BF)
    for d, out in enumerate(outs):
        out[...] = rows[d * slots : (d + 1) * slots, :]


def prepare_kernel(feat_ref, adj_ref, wn_ref, cot_ref, feat_t, adj_cat, adj_t, wn_low, wn_t, cot_wide):
    feat_t[...] = feat_ref[...].T
    nblocks, tile, _ = adj_cat.shape
    per_block = adj_ref.shape[0] // nblocks
    for b in range(nblocks):
        for t in range(per_block):
            block = adj_ref[b * per_block + t]
            adj_cat[b, :, t * tile : (t + 1) * tile] = block
            adj_t[b, t * tile : (t + 1) * tile, :] = block.T
    low = wn_ref[...].astype(BF)
    wn_low[...] = low
    wn_t[...] = low.T
    cot_wide[...] = cot_ref[...].astype(F32)


def middle_kernel(
    steps,
    hub_steps,
    tile_src,
    feat,
    feat_t,
    hubx,
    adj_cat,
    adj_t,
    pre0,
    wn,
    wn_t,
    cot,
    *rest,
):
    n_inner = (len(rest) - 11) // 2
    recv, (pre_out, gp_out, gown, keep, give), rest = rest[:n_inner], rest[n_inner : n_inner + 5], rest[n_inner + 5 :]
    back, (src, agg, gsrc, wacc, wperm, hubf) = rest[:n_inner], rest[n_inner:]
    o = lax.axis_index("outer")
    i = lax.axis_index("inner")
    table = flips(steps)
    nblocks, per_block = tile_src.shape
    tile = adj_cat.shape[1]
    nrows, width = cot.shape
    ntiles = src.shape[0]
    first_hub = nblocks + n_inner
    nhubs = hubx.shape[0]
    hd = nhubs // len(table)
    src[0:nblocks] = feat[...]
    for d in range(n_inner):
        src[nblocks + (i ^ d)] = recv[d][...]
    order = hub_order(hub_steps, n_inner, hd, nhubs)
    src[first_hub:] = dot(order, hubx[...]).astype(BF).reshape(ntiles - first_hub, tile, width)
    for b in range(nblocks):
        acc = jnp.zeros((tile, width), F32)
        for t in range(0, per_block, 2):
            ts = range(t, min(t + 2, per_block))
            rhs = [src[tile_src[b, u]] for u in ts]
            rhs = rhs[0] if len(rhs) == 1 else jnp.concatenate(rhs, axis=0)
            acc = acc + dot(adj_cat[b, :, t * tile : (t + len(ts)) * tile], rhs)
        agg[b * tile : (b + 1) * tile, :] = acc.astype(BF)
    pre = pre0[...] + dot(agg[...], wn[...])
    pre_out[...] = pre
    sig = jax.nn.sigmoid(pre)
    gp = (cot[...] * sig * (1.0 + pre * (1.0 - sig))).astype(BF)
    gp_out[...] = gp
    gagg = dot(gp, wn_t[...]).astype(BF)
    gsrc[...] = jnp.zeros(gsrc.shape, F32)
    for b in range(nblocks):
        for t in range(0, per_block, 3):
            last = min(t + 3, per_block)
            some = dot(adj_t[b, t * tile : last * tile, :], gagg[b * tile : (b + 1) * tile, :])
            for u in range(t, last):
                s = tile_src[b, u]
                gsrc[s] = gsrc[s] + some[(u - t) * tile : (u - t + 1) * tile, :]
    for d in range(n_inner):
        back[d][...] = gsrc[nblocks + (i ^ d)].astype(BF)
    gown[...] = gsrc[0:nblocks].reshape(nrows, width)
    wacc[0:width, :] = dot(feat_t[...], gp)
    wacc[width : 2 * width, :] = dot(agg[...], gp, TN)
    order = hub_order(steps, n_inner, hd, nhubs)
    hubf[...] = dot(order, gsrc[first_hub:].reshape(nhubs, width).astype(BF), TN).astype(BF)
    bias = jnp.sum(gp.astype(F32), axis=0, keepdims=True)
    tail = jnp.where(lax.broadcasted_iota(jnp.int32, (16, width), 0) == 0, bias, 0.0).astype(BF)
    wrows = 2 * width // len(table)
    devices = [(o ^ fo) * n_inner + (i ^ fi) for fo, fi in table]
    for k, out in enumerate((keep, give)):
        for j in range(len(table) // 2):
            rows = load_rows(wacc, devices[k * len(table) // 2 + j] * wrows, wrows)
            if wrows % 16 == 0:
                out[j * wrows : (j + 1) * wrows, :] = rows.astype(BF)
            else:
                wperm[j * wrows : (j + 1) * wrows, :] = rows
        if wrows % 16:
            out[0:width, :] = wperm[...].astype(BF)
        out[width : width + nhubs // 2, :] = hubf[k * nhubs // 2 : (k + 1) * nhubs // 2, :]
        out[width + nhubs // 2 :, :] = tail


def add_returned(acc, rows_ref, count_ref, blocks, returned):
    i = lax.axis_index("inner")
    for k in range(0, len(blocks), 2):
        some = range(k, min(k + 2, len(blocks)))
        put = slot_onehot(rows_ref, count_ref, acc.shape[0], [i ^ blocks[u] for u in some])
        values = [returned[u][...] for u in some]
        acc[...] += dot(put, values[0] if len(values) == 1 else jnp.concatenate(values, axis=0))


def first_scatter_kernel(blocks, count_ref, rows_ref, gown_ref, gp_ref, ws_ref, *rest):
    returned, out_ref = rest[:-1], rest[-1]
    out_ref[...] = gown_ref[...] + dot(gp_ref[...], ws_ref[...], NT)
    add_returned(out_ref, rows_ref, count_ref, blocks, returned)


def last_scatter_kernel(blocks, hub_ref, count_ref, rows_ref, own_ref, hub_grad_ref, *rest):
    returned, (out_ref, acc) = rest[:-2], rest[-2:]
    acc[...] = own_ref[...]
    add_returned(acc, rows_ref, count_ref, blocks, returned)
    for h in range(hub_ref.shape[0]):
        r = hub_ref[h]
        acc[pl.ds(r, 1), :] = acc[pl.ds(r, 1), :] + hub_grad_ref[h : h + 1, :]
    out_ref[...] = acc[...].astype(BF)


def finish_kernel(steps, n_inner, factor, x_ref, y_ref, bias_in, self_ref, neigh_ref, bias_ref, full):
    table = flips(steps)
    o = lax.axis_index("outer")
    i = lax.axis_index("inner")
    wrows = 2 * x_ref.shape[0] // len(table)
    width = self_ref.shape[0]
    for j, (fo, fi) in enumerate(table):
        d = (o ^ fo) * n_inner + (i ^ fi)
        ref, at = (x_ref, j) if 2 * j < len(table) else (y_ref, j - len(table) // 2)
        store_rows(full, d * wrows, ref[at * wrows : (at + 1) * wrows, :].astype(F32) * factor)
    self_ref[...] = full[0:width, :]
    neigh_ref[...] = full[width : 2 * width, :]
    bias_ref[...] = bias_in[0:1, :] * factor


def params(mib):
    return pltpu.CompilerParams(vmem_limit_bytes=mib * MIB)


def nbytes(scratch):
    return sum(s.dtype.itemsize * math.prod(s.shape) for s in scratch)


def cost(flops, nbytes):
    return pl.CostEstimate(flops=flops, bytes_accessed=nbytes, transcendentals=0)


def body(
    features,
    adj_tiles,
    tile_src,
    send_rows,
    send_count,
    hub_rows,
    w_self,
    w_neigh,
    out_bias,
    cotangent,
):
    n_outer, n_inner = lax.axis_size("outer"), lax.axis_size("inner")
    ndevice = n_outer * n_inner
    nrows, width = features.shape
    tile = adj_tiles.shape[1]
    nblocks, per_block = tile_src.shape
    hd = hub_rows.shape[0]
    nhubs = hd * ndevice
    ntiles = nblocks + n_inner + nhubs // tile
    groups = tree_groups(n_outer, n_inner)
    steps = sum(groups, [])
    hub_steps = sum(groups[::-1], [])
    wrows = 2 * width // ndevice

    def shape(*dims, dtype=BF):
        return jax.ShapeDtypeStruct(dims, dtype)

    hub_own, *outgoing = pl.pallas_call(
        gather_kernel,
        out_shape=(shape(hd, width),) + (shape(tile, width),) * n_inner,
        in_specs=[SM, SM, VM, VM],
        out_specs=(VM,) * (1 + n_inner),
        compiler_params=params(60),
        cost_estimate=cost(4 * 10**8, 3 * 10**6),
        name="gather_rows",
    )(hub_rows, send_count, features, send_rows)
    received = [outgoing[0]] + [None] * (n_inner - 1)
    for d in range(1, n_inner):
        received[d] = exchange(outgoing[d], (0, d))
    far = n_inner // 2
    hubx = hub_own
    for group in groups[:-1]:
        hubx = spread(hubx, group)
    ahead = range(far, far + far // 2)
    hubx, held = lax.optimization_barrier((hubx, [received[d] for d in ahead]))
    for d, value in zip(ahead, held):
        received[d] = value
    hubx = spread(hubx, groups[-1])
    feat_t, adj_cat, adj_t, neigh_low, neigh_t, cot_wide = pl.pallas_call(
        prepare_kernel,
        out_shape=(
            shape(width, nrows),
            shape(nblocks, tile, per_block * tile),
            shape(nblocks, per_block * tile, tile),
            shape(width, width),
            shape(width, width),
            shape(nrows, width, dtype=F32),
        ),
        in_specs=[VM] * 4,
        out_specs=(VM,) * 6,
        compiler_params=params(8 + 4 * nbytes([adj_tiles]) // MIB),
        cost_estimate=cost(10**6, 7 * 10**6),
        name="prepare",
    )(features, adj_tiles, w_neigh, cotangent)
    self_low = w_self.astype(BF)
    pre0 = jnp.dot(features, self_low, preferred_element_type=F32) + out_bias

    half = width + nhubs // 2 + 16
    scratch = [
        pltpu.VMEM((ntiles, tile, width), BF),
        pltpu.VMEM((nrows, width), BF),
        pltpu.VMEM((ntiles, tile, width), F32),
        pltpu.VMEM((2 * width, width), F32),
        pltpu.VMEM((width, width) if wrows % 16 else (8, 128), F32),
        pltpu.VMEM((nhubs, width), BF),
    ]
    out_shape = (
        shape(nrows, width, dtype=F32),
        shape(nrows, width),
        shape(nrows, width, dtype=F32),
        shape(half, width),
        shape(half, width),
    ) + (shape(tile, width),) * n_inner
    operands = (
        features.reshape(nblocks, tile, width),
        feat_t,
        hubx,
        adj_cat,
        adj_t,
        pre0,
        neigh_low,
        neigh_t,
        cot_wide,
        *received,
    )
    pre, gp, gown, keep, give, *back = pl.pallas_call(
        functools.partial(middle_kernel, steps, hub_steps),
        out_shape=out_shape,
        in_specs=[SM] + [VM] * len(operands),
        out_specs=(VM,) * len(out_shape),
        scratch_shapes=scratch,
        compiler_params=params(nbytes([*scratch, *operands, *out_shape]) // MIB + 8),
        cost_estimate=cost(2 * 10**9, 9 * 10**6),
        name="middle",
    )(tile_src, *operands)
    hidden_out = (pre * jax.nn.sigmoid(pre)).astype(BF)

    returned = [back[0]] + [None] * (n_inner - 1)
    odd = list(range(far + 1, n_inner, 2))
    first = list(range(far, n_inner, 2))
    second = [1] + odd[: far // 4]
    third = [3] + odd[far // 4 :]
    fourth = [d for d in range(2, far) if d != 3]

    def start(ds, after=None):
        held = [back[d] for d in ds]
        if after is not None:
            after, held = lax.optimization_barrier((after, held))
        for d, value in zip(ds, held):
            returned[d] = exchange(value, (0, d))
        return after

    def wait(value, ds):
        value, held = lax.optimization_barrier((value, [returned[d] for d in ds]))
        for d, block in zip(ds, held):
            returned[d] = block
        return value

    def reduce(parts, group, pending=()):
        ways = 2 ** len(group)
        seg = [p.shape[0] // ways for p in parts[:2]]
        sends = []
        for c in range(1, ways):
            rows = [p[c * n : (c + 1) * n] for p, n in zip(parts, seg)]
            sends.append(jnp.concatenate(rows + [parts[2]], 0).astype(BF))
        if pending:
            sends = wait(sends, pending)
        w, hub, bias = parts[0][: seg[0]], parts[1][: seg[1]], parts[2]
        for flip, send in zip(flips(group)[1:], sends):
            got = exchange(send, flip).astype(F32)
            w, hub, bias = w + got[: seg[0]], hub + got[seg[0] : seg[0] + seg[1]], bias + got[seg[0] + seg[1] :]
        return w, hub, bias

    start(first)
    got = exchange(give, flips(groups[0])[1])
    part = keep.astype(F32) + got.astype(F32)
    parts = (part[:width], part[width : width + nhubs // 2], part[width + nhubs // 2 : width + nhubs // 2 + 8])
    for group in groups[1:-1]:
        parts = reduce(parts, group)
    parts = start(second, parts)
    part, hub_grad, bias_sum = reduce(parts, groups[-1])
    mine = wait(part.astype(BF), first)
    mine, hidden_out = lax.optimization_barrier((mine, hidden_out))
    mine = start(third, mine)
    gathered = spread(mine, groups[-1])
    gathered = start(fourth, gathered)
    gathered = wait(gathered, second)
    for group in groups[1:-1][::-1]:
        gathered = spread(gathered, group)
    gathered = wait(gathered, third + fourth)

    blocks = [0] + first + second
    own = pl.pallas_call(
        functools.partial(first_scatter_kernel, blocks),
        out_shape=shape(nrows, width, dtype=F32),
        in_specs=[SM] + [VM] * (4 + len(blocks)),
        out_specs=VM,
        compiler_params=params(16),
        cost_estimate=cost(4 * 10**8, 3 * 10**6),
        name="scatter_first",
    )(send_count, send_rows, gown, gp, self_low, *[returned[d] for d in blocks])
    gathered, own = lax.optimization_barrier((gathered, own))
    other = exchange(gathered, flips(groups[0])[1])
    blocks = third + fourth
    grad_features = pl.pallas_call(
        functools.partial(last_scatter_kernel, blocks),
        out_shape=shape(nrows, width),
        in_specs=[SM, SM] + [VM] * (3 + len(blocks)),
        out_specs=VM,
        scratch_shapes=[pltpu.VMEM((nrows, width), F32)],
        compiler_params=params(16),
        cost_estimate=cost(2 * 10**8, 2 * 10**6),
        name="scatter_last",
    )(hub_rows, send_count, send_rows, own, hub_grad, *[returned[d] for d in blocks])
    factor = 1.0 / float(nrows * ndevice) ** 0.5
    total_self, total_neigh, total_bias = pl.pallas_call(
        functools.partial(finish_kernel, steps, n_inner, factor),
        out_shape=(shape(width, width, dtype=F32),) * 2 + (shape(1, width, dtype=F32),),
        in_specs=[VM] * 3,
        out_specs=(VM,) * 3,
        scratch_shapes=[pltpu.VMEM((2 * width, width), F32)],
        compiler_params=params(16),
        cost_estimate=cost(10**6, 3 * 10**6),
        name="finish",
    )(gathered, other, bias_sum)
    return hidden_out, grad_features, total_self, total_neigh, total_bias.reshape(width)


def solution(mesh):
    both = ("outer", "inner")
    return jax.shard_map(
        body,
        mesh=mesh,
        in_specs=(
            P(both, None),
            P(both, None, None),
            P(both, None),
            P(both, None),
            P(both, None),
            P(both),
            P(),
            P(),
            P(),
            P(both, None),
        ),
        out_specs=(P(both, None), P(both, None), P(), P(), P()),
        check_vma=False,
    )
```

time: 329 us -> 98.9 us (0.30)
  blocking collectives: 150 us -> 0 us
  waiting for transfers between devices: 82.5 us -> 39 us
  starting transfers between devices: 11.7 us -> 44.5 us
  other arithmetic: 30.2 us -> 2.33 us
  local copies, waits for them, and re-layouts: 26.7 us -> 0.13 us
  between operations: 14.3 us -> 1.11 us
  matrix products: 12.8 us -> 0.37 us
  Pallas kernels: 0 us -> 11.2 us
    unnamed x2 -> x0, waiting for transfers between devices: 82.5 us -> none
    all_gather x1 -> x0, blocking collectives: 81 us -> none  [body(): lax.all_gather(features[hub_rows], ('outer', 'inner'), axis=0, tiled=True)]
    psum x1 -> x0, blocking collectives: 69.3 us -> none  [body(): lax.psum((part_self, part_neigh, part_bias), ('outer', 'inner'))]
    ppermute x0 -> x35, starting transfers between devices: none -> 44.5 us  [exchange(): lax.ppermute(x, ('outer', 'inner'), [(s, s ^ mask) for s in range(n_outer...]
    ppermute x0 -> x35, waiting for transfers between devices: none -> 39 us  [exchange(): lax.ppermute(x, ('outer', 'inner'), [(s, s ^ mask) for s in range(n_outer...]
    scatter-add x3 -> x0, other arithmetic: 21.2 us -> none  [the longest x1 13.2 us: body(): jnp.zeros((ntiles, tilerows, width), jnp.float32).at[tile_src.reshape(-1)]]
    dot_general x8 -> x1, matrix products: 12.8 us -> 0.37 us  [body(): pre0 = jnp.dot(features, self_low, preferred_element_type=F32) + out_bias]
    all_to_all x2 -> x0, starting transfers between devices: 11.6 us -> none  [the longest x1 7.28 us: body(): lax.all_to_all(outgoing, 'inner', split_axis=0, concat_axis=0, tiled=True)]
  transfers between devices with their start and end apart: 3 -> 35, of which waited for: 1 -> 19; matrix products, arithmetic and copies ran while one was open for 5% -> 3% of each run, Pallas kernels for 0% -> 3%
where the time goes in v3:
time: 98.9 us; the launch traced here: 98.7 us
  starting transfers between devices  44.5 us (45%)
  waiting for transfers between devices  39 us (39%)
  Pallas kernels  11.2 us (11%)
  other arithmetic  2.33 us (2%)
  between operations  1.11 us (1%)
    ppermute x35, starting transfers between devices, exchange(): lax.ppermute(x, ('outer', 'inner'), [(s, s ^ mask) for s in range(n_outer...  44.5 us
    ppermute x35, waiting for transfers between devices, exchange(): lax.ppermute(x, ('outer', 'inner'), [(s, s ^ mask) for s in range(n_outer...  39 us
    pallas_call x1, Pallas kernels, body(): pl.pallas_call(functools.partial(middle_kernel, steps, hub_steps), out_sh...  3.63 us
    pallas_call x1, Pallas kernels, body(): pl.pallas_call(gather_kernel, out_shape=(shape(hd, width),) + (shape(tile...  2.61 us
  transfers between devices with their start and end apart: 35, of which 19 were waited for; matrix products, arithmetic and copies ran while one was open for 3% of the time, Pallas kernels for 3%

profile of v3, /device:TPU:0, one launch (start us, length us, event | category | flops | bytes accessed | tf_op | source)
XLA Modules:
  0.0 98.7 jit_solution(3045941540484957153)
XLA Ops:
  0.7 2.6 %gather_rows.1 = (bf16[4,512]{1,0:T(4,128)(2,1)}, bf16[128,512]{1,0:T(8,128)(2,1)}, bf16[128,512]{1,0:T(8,128)(2,1)}, bf16[128,512]{1,0:T(8,128)(2,1)}, bf16[128...) custom-call(s32[4]{0:T(128)} %hub_ref.3, ...), custom_call_target="tpu_custom_call" | custom-call | flops 400000000 | bytes 3000000 | tf_op jit(solution)/shard_map/gather_rows/pallas_call | solution.py:291
  3.3 0.5 collective-permute-start
  3.8 3.7 %collective-permute-start.4 = (bf16[128,512]{1,0:T(8,128)(2,1)}, bf16[128,512]{1,0:T(8,128)(2,1)S(1)}, u32[]{:S(2)}, u32[]{:S(2)}) collective-permute-start(bf16[128,512]{1,0:T(8,128)(2,1)} %get-tuple-element.65), channel_id=1, source_target_pairs={{0,4},{1,5},{2,6},{3,7},{4,0},{5,1},{6,2},{7,3},{8,12},{9,13},{10,... | collective-permute-start | bytes 393224 | tf_op jit(solution)/shard_map/ppermute | solution.py:80
  7.5 1.3 %collective-permute-start.5 = (bf16[128,512]{1,0:T(8,128)(2,1)}, bf16[128,512]{1,0:T(8,128)(2,1)S(1)}, u32[]{:S(2)}, u32[]{:S(2)}) collective-permute-start(bf16[128,512]{1,0:T(8,128)(2,1)} %get-tuple-element.66), channel_id=1, source_target_pairs={{0,5},{1,4},{2,7},{3,6},{4,1},{5,0},{6,3},{7,2},{8,13},{9,12},{10,... | collective-permute-start | bytes 393224 | tf_op jit(solution)/shard_map/ppermute | solution.py:80
  8.8 0.7 pad_maximum_fusion.10
  9.5 1.4 %collective-permute-start.3 = (bf16[8,512]{1,0:T(8,128)(2,1)S(1)}, bf16[8,512]{1,0:T(8,128)(2,1)S(1)}, u32[]{:S(2)}, u32[]{:S(2)}) collective-permute-start(bf16[8,512]{1,0:T(8,128)(2,1)S(1)} %pad_maximum_fusion.10), channel_id=1, source_target_pairs={{0,17},{1,16},{2,19},{3,18},{4,21},{5,20},{6,23},{7,22},{8,25},{9,... | collective-permute-start | bytes 24584 | tf_op jit(solution)/shard_map/ppermute | solution.py:80
  10.9 0.3 collective-permute-start.2
  11.2 1.8 %collective-permute-start.1 = (bf16[8,512]{1,0:T(8,128)(2,1)S(1)}, bf16[8,512]{1,0:T(8,128)(2,1)S(1)}, u32[]{:S(2)}, u32[]{:S(2)}) collective-permute-start(bf16[8,512]{1,0:T(8,128)(2,1)S(1)} %pad_maximum_fusion.10), channel_id=1, source_target_pairs={{0,1},{1,0},{2,3},{3,2},{4,5},{5,4},{6,7},{7,6},{8,9},{9,8},{10,11... | collective-permute-start | bytes 24584 | tf_op jit(solution)/shard_map/ppermute | solution.py:80
  12.9 1.1 %collective-permute-done.3 = bf16[8,512]{1,0:T(8,128)(2,1)S(1)} collective-permute-done((bf16[8,512]{1,0:T(8,128)(2,1)S(1)}, bf16[8,512]{1,0:T(8,128)(2,1)S(1)}, u32[]{:S(2)}, u32[]{:S(2)}) %collective-permute-start.3) | collective-permute-done | bytes 8224 | tf_op jit(solution)/shard_map/ppermute | solution.py:80
  14.0 0.5 collective-permute-done.2
  14.5 0.3 collective-permute-done.1
  14.8 2.8 %collective-permute-done.4.rest_4_ = bf16[128,512]{1,0:T(8,128)(2,1)S(1)} collective-permute-done((bf16[128,512]{1,0:T(8,128)(2,1)}, bf16[128,512]{1,0:T(8,128)(2,1)S(1)}, u32[]{:S(2)}, u32[]{:S(2)}) %collective-permute-start.4) | collective-permute-done | bytes 131104 | tf_op jit(solution)/shard_map/ppermute | solution.py:80
  17.7 3.6 %collective-permute-done.5.rest_5_ = bf16[128,512]{1,0:T(8,128)(2,1)S(1)} collective-permute-done((bf16[128,512]{1,0:T(8,128)(2,1)}, bf16[128,512]{1,0:T(8,128)(2,1)S(1)}, u32[]{:S(2)}, u32[]{:S(2)}) %collective-permute-start.5) | collective-permute-done | bytes 131104 | tf_op jit(solution)/shard_map/ppermute | solution.py:80
  21.2 3.5 %collective-permute-start.8 = (bf16[32,512]{1,0:T(8,128)(2,1)S(1)}, bf16[32,512]{1,0:T(8,128)(2,1)S(1)}, u32[]{:S(2)}, u32[]{:S(2)}) collective-permute-start(bf16[32,512]{1,0:T(8,128)(2,1)S(1)} %pad_maximum_fusion.9), channel_id=1, source_target_pairs={{0,6},{1,7},{2,4},{3,5},{4,2},{5,3},{6,0},{7,1},{8,14},{9,15},{10,... | collective-permute-start | bytes 98312 | tf_op jit(solution)/shard_map/ppermute | solution.py:80
  24.7 0.9 collective-permute-start.6
  25.6 0.4 collective-permute-start.9
  26.1 1.2 %collective-permute-start.10 = (bf16[128,512]{1,0:T(8,128)(2,1)}, bf16[128,512]{1,0:T(8,128)(2,1)S(1)}, u32[]{:S(2)}, u32[]{:S(2)}) collective-permute-start(bf16[128,512]{1,0:T(8,128)(2,1)} %get-tuple-element.75), channel_id=1, source_target_pairs={{0,2},{1,3},{2,0},{3,1},{4,6},{5,7},{6,4},{7,5},{8,10},{9,11},{10,... | collective-permute-start | bytes 393224 | tf_op jit(solution)/shard_map/ppermute | solution.py:80
  27.3 0.1 convert_element_type.39.ws_ref
  27.3 0.0 copy-start.2
  27.4 1.9 %collective-permute-start.11 = (bf16[128,512]{1,0:T(8,128)(2,1)S(1)}, bf16[128,512]{1,0:T(8,128)(2,1)S(1)}, u32[]{:S(2)}, u32[]{:S(2)}) collective-permute-start(bf16[128,512]{1,0:T(8,128)(2,1)S(1)} %copy-done.13), channel_id=1, source_target_pairs={{0,3},{1,2},{2,1},{3,0},{4,7},{5,6},{6,5},{7,4},{8,11},{9,10},{10,... | collective-permute-start | bytes 393224 | tf_op jit(solution)/shard_map/ppermute | solution.py:80
  29.3 3.5 %collective-permute-start.12 = (bf16[128,512]{1,0:T(8,128)(2,1)S(1)}, bf16[128,512]{1,0:T(8,128)(2,1)S(1)}, u32[]{:S(2)}, u32[]{:S(2)}) collective-permute-start(bf16[128,512]{1,0:T(8,128)(2,1)S(1)} %copy-done.12), channel_id=1, source_target_pairs={{0,6},{1,7},{2,4},{3,5},{4,2},{5,3},{6,0},{7,1},{8,14},{9,15},{10,... | collective-permute-start | bytes 393224 | tf_op jit(solution)/shard_map/ppermute | solution.py:80
  32.8 0.2 collective-permute-start.13
  33.0 0.4 convolution_add_fusion.pre0
  33.4 0.5 prepare.1
  34.0 0.7 collective-permute-done.11.rest_3_
  34.7 5.1 %collective-permute-done.12.rest_6_ = bf16[128,512]{1,0:T(8,128)(2,1)S(1)} collective-permute-done((bf16[128,512]{1,0:T(8,128)(2,1)S(1)}, bf16[128,512]{1,0:T(8,128)(2,1)S(1)}, u32[]{:S(2)}, u32[]{:S(2)}) %collective-permute-start.12) | collective-permute-done | bytes 131104 | tf_op jit(solution)/shard_map/ppermute | solution.py:80
  39.9 2.4 %collective-permute-done.13.rest_7_ = bf16[128,512]{1,0:T(8,128)(2,1)S(1)} collective-permute-done((bf16[128,512]{1,0:T(8,128)(2,1)S(1)}, bf16[128,512]{1,0:T(8,128)(2,1)S(1)}, u32[]{:S(2)}, u32[]{:S(2)}) %collective-permute-start.13) | collective-permute-done | bytes 131104 | tf_op jit(solution)/shard_map/ppermute | solution.py:80
  42.3 3.6 %middle.1 = (f32[384,512]{1,0:T(8,128)S(1)}, bf16[384,512]{1,0:T(8,128)(2,1)S(1)}, f32[384,512]{1,0:T(8,128)S(1)}, bf16[592,512]{1,0:T(8,128)(2,1)S(1)}, bf16[59...) custom-call(s32[3,6]{1,0:T(4,128)S(1)} %copy-done.7, ...), custom_call_target="tpu_custom_call" | custom-call | flops 2000000000 | bytes 9000000 | tf_op jit(solution)/shard_map/middle/pallas_call | solution.py:359
  45.9 0.1 collective-permute-start.14
  46.0 2.0 %collective-permute-done.14 = bf16[592,512]{1,0:T(8,128)(2,1)S(1)} collective-permute-done((bf16[592,512]{1,0:T(8,128)(2,1)S(1)}, bf16[592,512]{1,0:T(8,128)(2,1)S(1)}, u32[]{:S(2)}, u32[]{:S(2)}) %collective-permute-start.14) | collective-permute-done | bytes 606240 | tf_op jit(solution)/shard_map/ppermute | solution.py:80
  48.0 0.2 convert_add_fusion
  48.3 1.5 %collective-permute-start.17 = (bf16[152,512]{1,0:T(8,128)(2,1)S(1)}, bf16[152,512]{1,0:T(8,128)(2,1)S(1)}, u32[]{:S(2)}, u32[]{:S(2)}) collective-permute-start(bf16[152,512]{1,0:T(8,128)(2,1)S(1)} %pad_maximum_fusion.3), channel_id=1, source_target_pairs={{0,17},{1,16},{2,19},{3,18},{4,21},{5,20},{6,23},{7,22},{8,25},{9,... | collective-permute-start | bytes 466952 | tf_op jit(solution)/shard_map/ppermute | solution.py:80
  49.8 1.6 %collective-permute-start.15 = (bf16[152,512]{1,0:T(8,128)(2,1)S(1)}, bf16[152,512]{1,0:T(8,128)(2,1)S(1)}, u32[]{:S(2)}, u32[]{:S(2)}) collective-permute-start(bf16[152,512]{1,0:T(8,128)(2,1)S(1)} %get-tuple-element.137), channel_id=1, source_target_pairs={{0,1},{1,0},{2,3},{3,2},{4,5},{5,4},{6,7},{7,6},{8,9},{9,8},{10,11... | collective-permute-start | bytes 466952 | tf_op jit(solution)/shard_map/ppermute | solution.py:80
  51.4 0.5 collective-permute-start.16
  52.0 2.1 %collective-permute-start.21 = (bf16[128,512]{1,0:T(8,128)(2,1)S(1)}, bf16[128,512]{1,0:T(8,128)(2,1)S(1)}, u32[]{:S(2)}, u32[]{:S(2)}) collective-permute-start(bf16[128,512]{1,0:T(8,128)(2,1)S(1)} %get-tuple-element.88), channel_id=1, source_target_pairs={{0,4},{1,5},{2,6},{3,7},{4,0},{5,1},{6,2},{7,3},{8,12},{9,13},{10,... | collective-permute-start | bytes 393224 | tf_op jit(solution)/shard_map/ppermute | solution.py:80
  54.1 1.6 %collective-permute-start.22 = (bf16[128,512]{1,0:T(8,128)(2,1)S(1)}, bf16[128,512]{1,0:T(8,128)(2,1)S(1)}, u32[]{:S(2)}, u32[]{:S(2)}) collective-permute-start(bf16[128,512]{1,0:T(8,128)(2,1)S(1)} %get-tuple-element.89), channel_id=1, source_target_pairs={{0,6},{1,7},{2,4},{3,5},{4,2},{5,3},{6,0},{7,1},{8,14},{9,15},{10,... | collective-permute-start | bytes 393224 | tf_op jit(solution)/shard_map/ppermute | solution.py:80
  55.7 0.5 collective-permute-done.17
  56.2 2.5 %collective-permute-done.15 = bf16[152,512]{1,0:T(8,128)(2,1)S(1)} collective-permute-done((bf16[152,512]{1,0:T(8,128)(2,1)S(1)}, bf16[152,512]{1,0:T(8,128)(2,1)S(1)}, u32[]{:S(2)}, u32[]{:S(2)}) %collective-permute-start.15) | collective-permute-done | bytes 155680 | tf_op jit(solution)/shard_map/ppermute | solution.py:80
  58.8 0.1 slice_add_fusion
  59.0 2.2 %collective-permute-start.18 = (bf16[44,512]{1,0:T(8,128)(2,1)S(1)}, bf16[44,512]{1,0:T(8,128)(2,1)S(1)}, u32[]{:S(2)}, u32[]{:S(2)}) collective-permute-start(bf16[44,512]{1,0:T(8,128)(2,1)S(1)} %get-tuple-element.134), channel_id=1, source_target_pairs={{0,4},{1,5},{2,6},{3,7},{4,0},{5,1},{6,2},{7,3},{8,12},{9,13},{10,... | collective-permute-start | bytes 135176 | tf_op jit(solution)/shard_map/ppermute | solution.py:80
  61.2 2.3 %collective-permute-start.20 = (bf16[44,512]{1,0:T(8,128)(2,1)S(1)}, bf16[44,512]{1,0:T(8,128)(2,1)S(1)}, u32[]{:S(2)}, u32[]{:S(2)}) collective-permute-start(bf16[44,512]{1,0:T(8,128)(2,1)S(1)} %get-tuple-element.136), channel_id=1, source_target_pairs={{0,6},{1,7},{2,4},{3,5},{4,2},{5,3},{6,0},{7,1},{8,14},{9,15},{10,... | collective-permute-start | bytes 135176 | tf_op jit(solution)/shard_map/ppermute | solution.py:80
  63.5 1.0 multiply_convert_fusion
  64.4 5.2 %collective-permute-done.18 = bf16[44,512]{1,0:T(8,128)(2,1)S(1)} collective-permute-done((bf16[44,512]{1,0:T(8,128)(2,1)S(1)}, bf16[44,512]{1,0:T(8,128)(2,1)S(1)}, u32[]{:S(2)}, u32[]{:S(2)}) %collective-permute-start.18) | collective-permute-done | bytes 45088 | tf_op jit(solution)/shard_map/ppermute | solution.py:80
  69.8 1.4 %collective-permute-start.25 = (bf16[32,512]{1,0:T(8,128)(2,1)S(1)}, bf16[32,512]{1,0:T(8,128)(2,1)S(1)}, u32[]{:S(2)}, u32[]{:S(2)}) collective-permute-start(bf16[32,512]{1,0:T(8,128)(2,1)S(1)} %fusion), channel_id=1, source_target_pairs={{0,6},{1,7},{2,4},{3,5},{4,2},{5,3},{6,0},{7,1},{8,14},{9,15},{10,... | collective-permute-start | bytes 98312 | tf_op jit(solution)/shard_map/ppermute | solution.py:80
  71.2 0.1 collective-permute-start.24
  71.4 2.9 %collective-permute-start.23 = (bf16[32,512]{1,0:T(8,128)(2,1)S(1)}, bf16[32,512]{1,0:T(8,128)(2,1)S(1)}, u32[]{:S(2)}, u32[]{:S(2)}) collective-permute-start(bf16[32,512]{1,0:T(8,128)(2,1)S(1)} %fusion), channel_id=1, source_target_pairs={{0,4},{1,5},{2,6},{3,7},{4,0},{5,1},{6,2},{7,3},{8,12},{9,13},{10,... | collective-permute-start | bytes 98312 | tf_op jit(solution)/shard_map/ppermute | solution.py:80
  74.2 0.5 collective-permute-start.26
  74.7 1.0 %collective-permute-start.27 = (bf16[128,512]{1,0:T(8,128)(2,1)S(1)}, bf16[128,512]{1,0:T(8,128)(2,1)S(1)}, u32[]{:S(2)}, u32[]{:S(2)}) collective-permute-start(bf16[128,512]{1,0:T(8,128)(2,1)S(1)} %get-tuple-element.100), channel_id=1, source_target_pairs={{0,5},{1,4},{2,7},{3,6},{4,1},{5,0},{6,3},{7,2},{8,13},{9,12},{10,... | collective-permute-start | bytes 393224 | tf_op jit(solution)/shard_map/ppermute | solution.py:80
  75.7 0.4 collective-permute-done.23
  76.2 4.3 %collective-permute-done.26.rest_3_ = bf16[128,512]{1,0:T(8,128)(2,1)S(1)} collective-permute-done((bf16[128,512]{1,0:T(8,128)(2,1)S(1)}, bf16[128,512]{1,0:T(8,128)(2,1)S(1)}, u32[]{:S(2)}, u32[]{:S(2)}) %collective-permute-start.26) | collective-permute-done | bytes 131104 | tf_op jit(solution)/shard_map/ppermute | solution.py:80
  80.5 1.9 %collective-permute-done.27.rest_4_ = bf16[128,512]{1,0:T(8,128)(2,1)S(1)} collective-permute-done((bf16[128,512]{1,0:T(8,128)(2,1)S(1)}, bf16[128,512]{1,0:T(8,128)(2,1)S(1)}, u32[]{:S(2)}, u32[]{:S(2)}) %collective-permute-start.27) | collective-permute-done | bytes 131104 | tf_op jit(solution)/shard_map/ppermute | solution.py:80
  82.5 2.5 %collective-permute-start.30 = (bf16[128,512]{1,0:T(8,128)(2,1)S(1)}, bf16[128,512]{1,0:T(8,128)(2,1)S(1)}, u32[]{:S(2)}, u32[]{:S(2)}) collective-permute-start(bf16[128,512]{1,0:T(8,128)(2,1)S(1)} %pad_maximum_fusion.5), channel_id=1, source_target_pairs={{0,17},{1,16},{2,19},{3,18},{4,21},{5,20},{6,23},{7,22},{8,25},{9,... | collective-permute-start | bytes 393224 | tf_op jit(solution)/shard_map/ppermute | solution.py:80
  84.9 0.5 collective-permute-start.29
  85.5 0.5 collective-permute-start.28
  86.0 0.3 collective-permute-start.31
  86.2 2.1 %collective-permute-start.32 = (bf16[128,512]{1,0:T(8,128)(2,1)S(1)}, bf16[128,512]{1,0:T(8,128)(2,1)S(1)}, u32[]{:S(2)}, u32[]{:S(2)}) collective-permute-start(bf16[128,512]{1,0:T(8,128)(2,1)S(1)} %get-tuple-element.103), channel_id=1, source_target_pairs={{0,7},{1,6},{2,5},{3,4},{4,3},{5,2},{6,1},{7,0},{8,15},{9,14},{10,... | collective-permute-start | bytes 393224 | tf_op jit(solution)/shard_map/ppermute | solution.py:80
  88.3 1.2 %collective-permute-done.30 = bf16[128,512]{1,0:T(8,128)(2,1)S(1)} collective-permute-done((bf16[128,512]{1,0:T(8,128)(2,1)S(1)}, bf16[128,512]{1,0:T(8,128)(2,1)S(1)}, u32[]{:S(2)}, u32[]{:S(2)}) %collective-permute-start.30) | collective-permute-done | bytes 131104 | tf_op jit(solution)/shard_map/ppermute | solution.py:80
  89.5 0.3 collective-permute-start.33
  89.8 1.2 %scatter_first.1.own_ref = f32[384,512]{1,0:T(8,128)S(1)} custom-call(s32[1,8]{1,0:T(1,128)S(1)} %copy-done.5, s32[8,128]{1,0:T(8,128)S(1)} %copy-done.4, f32[384,512]{1,0:T(8,128)S(1)} %get-tuple-element.106.gown_ref, bf16[384,512]{1,0:T(8,128)(2,1)S(1)} %get-tuple-element.107.gp_ref, bf16[512,512]{1,0:T(8,128)(2,1)S(1)} %convert_element_type.39.ws_ref, ...), custom_call_target="tpu_custom_call" | custom-call | flops 400000000 | bytes 3000000 | tf_op jit(solution)/shard_map/scatter_first/pallas_call | solution.py:426
  91.1 3.1 %collective-permute-done.28 = bf16[128,512]{1,0:T(8,128)(2,1)S(1)} collective-permute-done((bf16[128,512]{1,0:T(8,128)(2,1)S(1)}, bf16[128,512]{1,0:T(8,128)(2,1)S(1)}, u32[]{:S(2)}, u32[]{:S(2)}) %collective-permute-start.28) | collective-permute-done | bytes 131104 | tf_op jit(solution)/shard_map/ppermute | solution.py:80
  94.3 0.9 collective-permute-done.33.rest_2_
  95.3 1.7 %scatter_last.1 = bf16[384,512]{1,0:T(8,128)(2,1)} custom-call(s32[4]{0:T(128)S(1)} %copy-done.6, s32[1,8]{1,0:T(1,128)S(1)} %copy-done.5, s32[8,128]{1,0:T(8,128)S(1)} %copy-done.4, f32[384,512]{1,0:T(8,128)S(1)} %scatter_first.1.own_ref, f32[4,512]{1,0:T(4,128)S(1)} %slice_add_fusion.15.hub_grad_ref, bf16[128,512]{1,0:T(8,128)(2,1)S(1)} %collective-permute-done.31.rest_0_, ...), custom_call_target="tpu_custom_call" | custom-call | flops 200000000 | bytes 2000000 | tf_op jit(solution)/shard_map/scatter_last/pallas_call | solution.py:438
  97.0 0.2 collective-permute-done.34.y_ref
  97.1 1.6 %finish.1 = (f32[512,512]{1,0:T(8,128)}, f32[512,512]{1,0:T(8,128)}, f32[1,512]{1,0:T(1,128)}) custom-call(bf16[512,512]{1,0:T(8,128)(2,1)S(1)} %pad_maximum_fusion.x_ref, bf16[512,512]{1,0:T(8,128)(2,1)S(1)} %collective-permute-done.34.y_ref, f32[8,512]{1,0:T(8,128)S(1)} %slice_add_fusion.9.bias_in), custom_call_target="tpu_custom_call" | custom-call | flops 1000000 | bytes 3000000 | tf_op jit(solution)/shard_map/finish/pallas_call | solution.py:449
  (73 shorter events, 0.5 us)
Async XLA Ops:
  0.6 32.4 %copy-start = (bf16[384,512]{1,0:T(8,128)(2,1)S(1)}, bf16[384,512]{1,0:T(8,128)(2,1)}, u32[]{:S(2)}) copy-start(bf16[384,512]{1,0:T(8,128)(2,1)} %feat_ref.3) | copy-start | bytes 1179652
  0.6 26.6 %copy-start.9 = (f32[512,512]{1,0:T(8,128)S(1)}, f32[512,512]{1,0:T(8,128)}, u32[]{:S(2)}) copy-start(f32[512,512]{1,0:T(8,128)} %param.16) | copy-start | bytes 3145732
  0.7 32.4 %copy-start.10 = (f32[512]{0:T(512)S(1)}, f32[512]{0:T(512)}, u32[]{:S(2)}) copy-start(f32[512]{0:T(512)} %param.18) | copy-start | bytes 6148
  3.3 24.1 %copy-start.13 = (bf16[128,512]{1,0:T(8,128)(2,1)S(1)}, bf16[128,512]{1,0:T(8,128)(2,1)}, u32[]{:S(2)}) copy-start(bf16[128,512]{1,0:T(8,128)(2,1)} %get-tuple-element.76) | copy-start | bytes 393220
  3.3 26.0 %copy-start.12 = (bf16[128,512]{1,0:T(8,128)(2,1)S(1)}, bf16[128,512]{1,0:T(8,128)(2,1)}, u32[]{:S(2)}) copy-start(bf16[128,512]{1,0:T(8,128)(2,1)} %get-tuple-element.79) | copy-start | bytes 393220
  3.3 29.5 %copy-start.11 = (bf16[128,512]{1,0:T(8,128)(2,1)S(1)}, bf16[128,512]{1,0:T(8,128)(2,1)}, u32[]{:S(2)}) copy-start(bf16[128,512]{1,0:T(8,128)(2,1)} %get-tuple-element.80) | copy-start | bytes 393220
  3.3 5.5 %collective-permute-start = (bf16[4,512]{1,0:T(4,128)(2,1)}, bf16[4,512]{1,0:T(4,128)(2,1)S(1)}, u32[]{:S(2)}, u32[]{:S(2)}) collective-permute-start(bf16[4,512]{1,0:T(4,128)(2,1)} %get-tuple-element.64), channel_id=1, source_target_pairs={{0,8},{1,9},{2,10},{3,11},{4,12},{5,13},{6,14},{7,15},{8,0},{9,1},... | collective-permute-start | bytes 12296 | tf_op jit(solution)/shard_map/ppermute | solution.py:80
  3.8 13.8 %collective-permute-start.4 = (bf16[128,512]{1,0:T(8,128)(2,1)}, bf16[128,512]{1,0:T(8,128)(2,1)S(1)}, u32[]{:S(2)}, u32[]{:S(2)}) collective-permute-start(bf16[128,512]{1,0:T(8,128)(2,1)} %get-tuple-element.65), channel_id=1, source_target_pairs={{0,4},{1,5},{2,6},{3,7},{4,0},{5,1},{6,2},{7,3},{8,12},{9,13},{10,... | collective-permute-start | bytes 393224 | tf_op jit(solution)/shard_map/ppermute | solution.py:80
  7.5 13.7 %collective-permute-start.5 = (bf16[128,512]{1,0:T(8,128)(2,1)}, bf16[128,512]{1,0:T(8,128)(2,1)S(1)}, u32[]{:S(2)}, u32[]{:S(2)}) collective-permute-start(bf16[128,512]{1,0:T(8,128)(2,1)} %get-tuple-element.66), channel_id=1, source_target_pairs={{0,5},{1,4},{2,7},{3,6},{4,1},{5,0},{6,3},{7,2},{8,13},{9,12},{10,... | collective-permute-start | bytes 393224 | tf_op jit(solution)/shard_map/ppermute | solution.py:80
  9.5 4.5 %collective-permute-start.3 = (bf16[8,512]{1,0:T(8,128)(2,1)S(1)}, bf16[8,512]{1,0:T(8,128)(2,1)S(1)}, u32[]{:S(2)}, u32[]{:S(2)}) collective-permute-start(bf16[8,512]{1,0:T(8,128)(2,1)S(1)} %pad_maximum_fusion.10), channel_id=1, source_target_pairs={{0,17},{1,16},{2,19},{3,18},{4,21},{5,20},{6,23},{7,22},{8,25},{9,... | collective-permute-start | bytes 24584 | tf_op jit(solution)/shard_map/ppermute | solution.py:80
  10.9 3.7 %collective-permute-start.2 = (bf16[8,512]{1,0:T(8,128)(2,1)S(1)}, bf16[8,512]{1,0:T(8,128)(2,1)S(1)}, u32[]{:S(2)}, u32[]{:S(2)}) collective-permute-start(bf16[8,512]{1,0:T(8,128)(2,1)S(1)} %pad_maximum_fusion.10), channel_id=1, source_target_pairs={{0,16},{1,17},{2,18},{3,19},{4,20},{5,21},{6,22},{7,23},{8,24},{9,... | collective-permute-start | bytes 24584 | tf_op jit(solution)/shard_map/ppermute | solution.py:80
  11.2 3.7 %collective-permute-start.1 = (bf16[8,512]{1,0:T(8,128)(2,1)S(1)}, bf16[8,512]{1,0:T(8,128)(2,1)S(1)}, u32[]{:S(2)}, u32[]{:S(2)}) collective-permute-start(bf16[8,512]{1,0:T(8,128)(2,1)S(1)} %pad_maximum_fusion.10), channel_id=1, source_target_pairs={{0,1},{1,0},{2,3},{3,2},{4,5},{5,4},{6,7},{7,6},{8,9},{9,8},{10,11... | collective-permute-start | bytes 24584 | tf_op jit(solution)/shard_map/ppermute | solution.py:80
  21.2 6.1 %collective-permute-start.8 = (bf16[32,512]{1,0:T(8,128)(2,1)S(1)}, bf16[32,512]{1,0:T(8,128)(2,1)S(1)}, u32[]{:S(2)}, u32[]{:S(2)}) collective-permute-start(bf16[32,512]{1,0:T(8,128)(2,1)S(1)} %pad_maximum_fusion.9), channel_id=1, source_target_pairs={{0,6},{1,7},{2,4},{3,5},{4,2},{5,3},{6,0},{7,1},{8,14},{9,15},{10,... | collective-permute-start | bytes 98312 | tf_op jit(solution)/shard_map/ppermute | solution.py:80
  24.7 4.6 %collective-permute-start.7 = (bf16[32,512]{1,0:T(8,128)(2,1)S(1)}, bf16[32,512]{1,0:T(8,128)(2,1)S(1)}, u32[]{:S(2)}, u32[]{:S(2)}) collective-permute-start(bf16[32,512]{1,0:T(8,128)(2,1)S(1)} %pad_maximum_fusion.9), channel_id=1, source_target_pairs={{0,2},{1,3},{2,0},{3,1},{4,6},{5,7},{6,4},{7,5},{8,10},{9,11},{10,... | collective-permute-start | bytes 98312 | tf_op jit(solution)/shard_map/ppermute | solution.py:80
  24.7 8.1 %collective-permute-start.6 = (bf16[32,512]{1,0:T(8,128)(2,1)S(1)}, bf16[32,512]{1,0:T(8,128)(2,1)S(1)}, u32[]{:S(2)}, u32[]{:S(2)}) collective-permute-start(bf16[32,512]{1,0:T(8,128)(2,1)S(1)} %pad_maximum_fusion.9), channel_id=1, source_target_pairs={{0,4},{1,5},{2,6},{3,7},{4,0},{5,1},{6,2},{7,3},{8,12},{9,13},{10,... | collective-permute-start | bytes 98312 | tf_op jit(solution)/shard_map/ppermute | solution.py:80
  25.6 8.4 %collective-permute-start.9 = (bf16[128,512]{1,0:T(8,128)(2,1)}, bf16[128,512]{1,0:T(8,128)(2,1)S(1)}, u32[]{:S(2)}, u32[]{:S(2)}) collective-permute-start(bf16[128,512]{1,0:T(8,128)(2,1)} %get-tuple-element.74), channel_id=1, source_target_pairs={{0,1},{1,0},{2,3},{3,2},{4,5},{5,4},{6,7},{7,6},{8,9},{9,8},{10,11... | collective-permute-start | bytes 393224 | tf_op jit(solution)/shard_map/ppermute | solution.py:80
  26.1 7.9 %collective-permute-start.10 = (bf16[128,512]{1,0:T(8,128)(2,1)}, bf16[128,512]{1,0:T(8,128)(2,1)S(1)}, u32[]{:S(2)}, u32[]{:S(2)}) collective-permute-start(bf16[128,512]{1,0:T(8,128)(2,1)} %get-tuple-element.75), channel_id=1, source_target_pairs={{0,2},{1,3},{2,0},{3,1},{4,6},{5,7},{6,4},{7,5},{8,10},{9,11},{10,... | collective-permute-start | bytes 393224 | tf_op jit(solution)/shard_map/ppermute | solution.py:80
  27.3 6.1 %copy-start.3 = (bf16[384,512]{1,0:T(8,128)(2,1)S(1)}, bf16[384,512]{1,0:T(8,128)(2,1)}, u32[]{:S(2)}) copy-start(bf16[384,512]{1,0:T(8,128)(2,1)} %cot_ref.1) | copy-start | bytes 1179652
  27.3 6.1 %copy-start.1 = (f32[512,512]{1,0:T(8,128)S(1)}, f32[512,512]{1,0:T(8,128)}, u32[]{:S(2)}) copy-start(f32[512,512]{1,0:T(8,128)} %wn_ref.1) | copy-start | bytes 3145732
  27.3 6.1 %copy-start.2 = (bf16[18,128,128]{2,1,0:T(8,128)(2,1)S(1)}, bf16[18,128,128]{2,1,0:T(8,128)(2,1)}, u32[]{:S(2)}) copy-start(bf16[18,128,128]{2,1,0:T(8,128)(2,1)} %adj_ref.1) | copy-start | bytes 1769476
  27.4 7.4 %collective-permute-start.11 = (bf16[128,512]{1,0:T(8,128)(2,1)S(1)}, bf16[128,512]{1,0:T(8,128)(2,1)S(1)}, u32[]{:S(2)}, u32[]{:S(2)}) collective-permute-start(bf16[128,512]{1,0:T(8,128)(2,1)S(1)} %copy-done.13), channel_id=1, source_target_pairs={{0,3},{1,2},{2,1},{3,0},{4,7},{5,6},{6,5},{7,4},{8,11},{9,10},{10,... | collective-permute-start | bytes 393224 | tf_op jit(solution)/shard_map/ppermute | solution.py:80
  29.3 10.6 %collective-permute-start.12 = (bf16[128,512]{1,0:T(8,128)(2,1)S(1)}, bf16[128,512]{1,0:T(8,128)(2,1)S(1)}, u32[]{:S(2)}, u32[]{:S(2)}) collective-permute-start(bf16[128,512]{1,0:T(8,128)(2,1)S(1)} %copy-done.12), channel_id=1, source_target_pairs={{0,6},{1,7},{2,4},{3,5},{4,2},{5,3},{6,0},{7,1},{8,14},{9,15},{10,... | collective-permute-start | bytes 393224 | tf_op jit(solution)/shard_map/ppermute | solution.py:80
  32.8 9.5 %collective-permute-start.13 = (bf16[128,512]{1,0:T(8,128)(2,1)S(1)}, bf16[128,512]{1,0:T(8,128)(2,1)S(1)}, u32[]{:S(2)}, u32[]{:S(2)}) collective-permute-start(bf16[128,512]{1,0:T(8,128)(2,1)S(1)} %copy-done.11), channel_id=1, source_target_pairs={{0,7},{1,6},{2,5},{3,4},{4,3},{5,2},{6,1},{7,0},{8,15},{9,14},{10,... | collective-permute-start | bytes 393224 | tf_op jit(solution)/shard_map/ppermute | solution.py:80
  33.4 8.8 %copy-start.7 = (s32[3,6]{1,0:T(4,128)S(1)}, s32[3,6]{1,0:T(4,128)}, u32[]{:S(2)}) copy-start(s32[3,6]{1,0:T(4,128)} %tile_src.1) | copy-start | bytes 220
  33.4 8.8 %copy-start.8 = (bf16[128,512]{1,0:T(8,128)(2,1)S(1)}, bf16[128,512]{1,0:T(8,128)(2,1)}, u32[]{:S(2)}) copy-start(bf16[128,512]{1,0:T(8,128)(2,1)} %get-tuple-element.73.rest_0_) | copy-start | bytes 393220
  45.9 2.1 %collective-permute-start.14 = (bf16[592,512]{1,0:T(8,128)(2,1)S(1)}, bf16[592,512]{1,0:T(8,128)(2,1)S(1)}, u32[]{:S(2)}, u32[]{:S(2)}) collective-permute-start(bf16[592,512]{1,0:T(8,128)(2,1)S(1)} %get-tuple-element.82), channel_id=1, source_target_pairs={{0,8},{1,9},{2,10},{3,11},{4,12},{5,13},{6,14},{7,15},{8,0},{9,1},... | collective-permute-start | bytes 1818632 | tf_op jit(solution)/shard_map/ppermute | solution.py:80
  48.3 7.9 %collective-permute-start.17 = (bf16[152,512]{1,0:T(8,128)(2,1)S(1)}, bf16[152,512]{1,0:T(8,128)(2,1)S(1)}, u32[]{:S(2)}, u32[]{:S(2)}) collective-permute-start(bf16[152,512]{1,0:T(8,128)(2,1)S(1)} %pad_maximum_fusion.3), channel_id=1, source_target_pairs={{0,17},{1,16},{2,19},{3,18},{4,21},{5,20},{6,23},{7,22},{8,25},{9,... | collective-permute-start | bytes 466952 | tf_op jit(solution)/shard_map/ppermute | solution.py:80
  49.8 8.9 %collective-permute-start.15 = (bf16[152,512]{1,0:T(8,128)(2,1)S(1)}, bf16[152,512]{1,0:T(8,128)(2,1)S(1)}, u32[]{:S(2)}, u32[]{:S(2)}) collective-permute-start(bf16[152,512]{1,0:T(8,128)(2,1)S(1)} %get-tuple-element.137), channel_id=1, source_target_pairs={{0,1},{1,0},{2,3},{3,2},{4,5},{5,4},{6,7},{7,6},{8,9},{9,8},{10,11... | collective-permute-start | bytes 466952 | tf_op jit(solution)/shard_map/ppermute | solution.py:80
  51.4 7.3 %collective-permute-start.16 = (bf16[152,512]{1,0:T(8,128)(2,1)S(1)}, bf16[152,512]{1,0:T(8,128)(2,1)S(1)}, u32[]{:S(2)}, u32[]{:S(2)}) collective-permute-start(bf16[152,512]{1,0:T(8,128)(2,1)S(1)} %get-tuple-element.138), channel_id=1, source_target_pairs={{0,16},{1,17},{2,18},{3,19},{4,20},{5,21},{6,22},{7,23},{8,24},{9,... | collective-permute-start | bytes 466952 | tf_op jit(solution)/shard_map/ppermute | solution.py:80
  52.0 17.8 %collective-permute-start.21 = (bf16[128,512]{1,0:T(8,128)(2,1)S(1)}, bf16[128,512]{1,0:T(8,128)(2,1)S(1)}, u32[]{:S(2)}, u32[]{:S(2)}) collective-permute-start(bf16[128,512]{1,0:T(8,128)(2,1)S(1)} %get-tuple-element.88), channel_id=1, source_target_pairs={{0,4},{1,5},{2,6},{3,7},{4,0},{5,1},{6,2},{7,3},{8,12},{9,13},{10,... | collective-permute-start | bytes 393224 | tf_op jit(solution)/shard_map/ppermute | solution.py:80
  54.1 15.7 %collective-permute-start.22 = (bf16[128,512]{1,0:T(8,128)(2,1)S(1)}, bf16[128,512]{1,0:T(8,128)(2,1)S(1)}, u32[]{:S(2)}, u32[]{:S(2)}) collective-permute-start(bf16[128,512]{1,0:T(8,128)(2,1)S(1)} %get-tuple-element.89), channel_id=1, source_target_pairs={{0,6},{1,7},{2,4},{3,5},{4,2},{5,3},{6,0},{7,1},{8,14},{9,15},{10,... | collective-permute-start | bytes 393224 | tf_op jit(solution)/shard_map/ppermute | solution.py:80
  59.0 30.8 %copy-start.4 = (s32[8,128]{1,0:T(8,128)S(1)}, s32[8,128]{1,0:T(8,128)}, u32[]{:S(2)}) copy-start(s32[8,128]{1,0:T(8,128)} %rows_ref.5) | copy-start | bytes 12292
  59.0 30.8 %copy-start.5 = (s32[1,8]{1,0:T(1,128)S(1)}, s32[1,8]{1,0:T(1,128)}, u32[]{:S(2)}) copy-start(s32[1,8]{1,0:T(1,128)} %count_ref.5) | copy-start | bytes 100
  59.0 10.6 %collective-permute-start.18 = (bf16[44,512]{1,0:T(8,128)(2,1)S(1)}, bf16[44,512]{1,0:T(8,128)(2,1)S(1)}, u32[]{:S(2)}, u32[]{:S(2)}) collective-permute-start(bf16[44,512]{1,0:T(8,128)(2,1)S(1)} %get-tuple-element.134), channel_id=1, source_target_pairs={{0,4},{1,5},{2,6},{3,7},{4,0},{5,1},{6,2},{7,3},{8,12},{9,13},{10,... | collective-permute-start | bytes 135176 | tf_op jit(solution)/shard_map/ppermute | solution.py:80
  61.2 8.5 %collective-permute-start.19 = (bf16[44,512]{1,0:T(8,128)(2,1)S(1)}, bf16[44,512]{1,0:T(8,128)(2,1)S(1)}, u32[]{:S(2)}, u32[]{:S(2)}) collective-permute-start(bf16[44,512]{1,0:T(8,128)(2,1)S(1)} %get-tuple-element.135), channel_id=1, source_target_pairs={{0,2},{1,3},{2,0},{3,1},{4,6},{5,7},{6,4},{7,5},{8,10},{9,11},{10,... | collective-permute-start | bytes 135176 | tf_op jit(solution)/shard_map/ppermute | solution.py:80
  61.2 8.5 %collective-permute-start.20 = (bf16[44,512]{1,0:T(8,128)(2,1)S(1)}, bf16[44,512]{1,0:T(8,128)(2,1)S(1)}, u32[]{:S(2)}, u32[]{:S(2)}) collective-permute-start(bf16[44,512]{1,0:T(8,128)(2,1)S(1)} %get-tuple-element.136), channel_id=1, source_target_pairs={{0,6},{1,7},{2,4},{3,5},{4,2},{5,3},{6,0},{7,1},{8,14},{9,15},{10,... | collective-permute-start | bytes 135176 | tf_op jit(solution)/shard_map/ppermute | solution.py:80
  69.8 5.9 %collective-permute-start.25 = (bf16[32,512]{1,0:T(8,128)(2,1)S(1)}, bf16[32,512]{1,0:T(8,128)(2,1)S(1)}, u32[]{:S(2)}, u32[]{:S(2)}) collective-permute-start(bf16[32,512]{1,0:T(8,128)(2,1)S(1)} %fusion), channel_id=1, source_target_pairs={{0,6},{1,7},{2,4},{3,5},{4,2},{5,3},{6,0},{7,1},{8,14},{9,15},{10,... | collective-permute-start | bytes 98312 | tf_op jit(solution)/shard_map/ppermute | solution.py:80
  71.2 4.5 %collective-permute-start.24 = (bf16[32,512]{1,0:T(8,128)(2,1)S(1)}, bf16[32,512]{1,0:T(8,128)(2,1)S(1)}, u32[]{:S(2)}, u32[]{:S(2)}) collective-permute-start(bf16[32,512]{1,0:T(8,128)(2,1)S(1)} %fusion), channel_id=1, source_target_pairs={{0,2},{1,3},{2,0},{3,1},{4,6},{5,7},{6,4},{7,5},{8,10},{9,11},{10,... | collective-permute-start | bytes 98312 | tf_op jit(solution)/shard_map/ppermute | solution.py:80
  71.4 4.8 %collective-permute-start.23 = (bf16[32,512]{1,0:T(8,128)(2,1)S(1)}, bf16[32,512]{1,0:T(8,128)(2,1)S(1)}, u32[]{:S(2)}, u32[]{:S(2)}) collective-permute-start(bf16[32,512]{1,0:T(8,128)(2,1)S(1)} %fusion), channel_id=1, source_target_pairs={{0,4},{1,5},{2,6},{3,7},{4,0},{5,1},{6,2},{7,3},{8,12},{9,13},{10,... | collective-permute-start | bytes 98312 | tf_op jit(solution)/shard_map/ppermute | solution.py:80
  74.2 6.3 %collective-permute-start.26 = (bf16[128,512]{1,0:T(8,128)(2,1)S(1)}, bf16[128,512]{1,0:T(8,128)(2,1)S(1)}, u32[]{:S(2)}, u32[]{:S(2)}) collective-permute-start(bf16[128,512]{1,0:T(8,128)(2,1)S(1)} %get-tuple-element.99), channel_id=1, source_target_pairs={{0,1},{1,0},{2,3},{3,2},{4,5},{5,4},{6,7},{7,6},{8,9},{9,8},{10,11... | collective-permute-start | bytes 393224 | tf_op jit(solution)/shard_map/ppermute | solution.py:80
  74.7 7.7 %collective-permute-start.27 = (bf16[128,512]{1,0:T(8,128)(2,1)S(1)}, bf16[128,512]{1,0:T(8,128)(2,1)S(1)}, u32[]{:S(2)}, u32[]{:S(2)}) collective-permute-start(bf16[128,512]{1,0:T(8,128)(2,1)S(1)} %get-tuple-element.100), channel_id=1, source_target_pairs={{0,5},{1,4},{2,7},{3,6},{4,1},{5,0},{6,3},{7,2},{8,13},{9,12},{10,... | collective-permute-start | bytes 393224 | tf_op jit(solution)/shard_map/ppermute | solution.py:80
  82.5 7.1 %collective-permute-start.30 = (bf16[128,512]{1,0:T(8,128)(2,1)S(1)}, bf16[128,512]{1,0:T(8,128)(2,1)S(1)}, u32[]{:S(2)}, u32[]{:S(2)}) collective-permute-start(bf16[128,512]{1,0:T(8,128)(2,1)S(1)} %pad_maximum_fusion.5), channel_id=1, source_target_pairs={{0,17},{1,16},{2,19},{3,18},{4,21},{5,20},{6,23},{7,22},{8,25},{9,... | collective-permute-start | bytes 393224 | tf_op jit(solution)/shard_map/ppermute | solution.py:80
  84.9 6.1 %collective-permute-start.29 = (bf16[128,512]{1,0:T(8,128)(2,1)S(1)}, bf16[128,512]{1,0:T(8,128)(2,1)S(1)}, u32[]{:S(2)}, u32[]{:S(2)}) collective-permute-start(bf16[128,512]{1,0:T(8,128)(2,1)S(1)} %pad_maximum_fusion.5), channel_id=1, source_target_pairs={{0,16},{1,17},{2,18},{3,19},{4,20},{5,21},{6,22},{7,23},{8,24},{9,... | collective-permute-start | bytes 393224 | tf_op jit(solution)/shard_map/ppermute | solution.py:80
  85.5 8.8 %collective-permute-start.28 = (bf16[128,512]{1,0:T(8,128)(2,1)S(1)}, bf16[128,512]{1,0:T(8,128)(2,1)S(1)}, u32[]{:S(2)}, u32[]{:S(2)}) collective-permute-start(bf16[128,512]{1,0:T(8,128)(2,1)S(1)} %pad_maximum_fusion.5), channel_id=1, source_target_pairs={{0,1},{1,0},{2,3},{3,2},{4,5},{5,4},{6,7},{7,6},{8,9},{9,8},{10,11... | collective-permute-start | bytes 393224 | tf_op jit(solution)/shard_map/ppermute | solution.py:80
  86.0 8.3 %collective-permute-start.31 = (bf16[128,512]{1,0:T(8,128)(2,1)S(1)}, bf16[128,512]{1,0:T(8,128)(2,1)S(1)}, u32[]{:S(2)}, u32[]{:S(2)}) collective-permute-start(bf16[128,512]{1,0:T(8,128)(2,1)S(1)} %get-tuple-element.102), channel_id=1, source_target_pairs={{0,3},{1,2},{2,1},{3,0},{4,7},{5,6},{6,5},{7,4},{8,11},{9,10},{10,... | collective-permute-start | bytes 393224 | tf_op jit(solution)/shard_map/ppermute | solution.py:80
  86.2 8.1 %collective-permute-start.32 = (bf16[128,512]{1,0:T(8,128)(2,1)S(1)}, bf16[128,512]{1,0:T(8,128)(2,1)S(1)}, u32[]{:S(2)}, u32[]{:S(2)}) collective-permute-start(bf16[128,512]{1,0:T(8,128)(2,1)S(1)} %get-tuple-element.103), channel_id=1, source_target_pairs={{0,7},{1,6},{2,5},{3,4},{4,3},{5,2},{6,1},{7,0},{8,15},{9,14},{10,... | collective-permute-start | bytes 393224 | tf_op jit(solution)/shard_map/ppermute | solution.py:80
  89.5 5.7 %collective-permute-start.33 = (bf16[128,512]{1,0:T(8,128)(2,1)S(1)}, bf16[128,512]{1,0:T(8,128)(2,1)S(1)}, u32[]{:S(2)}, u32[]{:S(2)}) collective-permute-start(bf16[128,512]{1,0:T(8,128)(2,1)S(1)} %get-tuple-element.104), channel_id=1, source_target_pairs={{0,2},{1,3},{2,0},{3,1},{4,6},{5,7},{6,4},{7,5},{8,10},{9,11},{10,... | collective-permute-start | bytes 393224 | tf_op jit(solution)/shard_map/ppermute | solution.py:80
  89.8 5.4 %copy-start.6 = (s32[4]{0:T(128)S(1)}, s32[4]{0:T(128)}, u32[]{:S(2)}) copy-start(s32[4]{0:T(128)} %hub_ref.3) | copy-start | bytes 52
  95.2 1.9 %collective-permute-start.34 = (bf16[512,512]{1,0:T(8,128)(2,1)S(1)}, bf16[512,512]{1,0:T(8,128)(2,1)S(1)}, u32[]{:S(2)}, u32[]{:S(2)}) collective-permute-start(bf16[512,512]{1,0:T(8,128)(2,1)S(1)} %pad_maximum_fusion.x_ref), channel_id=1, source_target_pairs={{0,8},{1,9},{2,10},{3,11},{4,12},{5,13},{6,14},{7,15},{8,0},{9,1},... | collective-permute-start | bytes 1572872 | tf_op jit(solution)/shard_map/ppermute | solution.py:80

commit v4 on v3

--- a/solution.py
+++ b/solution.py
@@ -85,6 +85,29 @@
     return lax.optimization_barrier(jnp.concatenate(parts, 0))
 
 
+def relayed(n_inner):
+    return list(range(2, n_inner - 2, 2))
+
+
+def places(n_inner, tile):
+    pairs = relayed(n_inner)
+    near = 1 + len(pairs)
+    where = {0: (0, 0), 1: (near, 0), n_inner - 2: (near + 1, 0), n_inner - 1: (near + 2, 0)}
+    for k, c in enumerate(pairs):
+        where[c] = (1 + k, 0)
+        where[c + 1] = (near, (1 + k) * tile)
+    return where
+
+
+def sent_blocks(n_inner):
+    return [[0]] + [[c, c + 1] for c in relayed(n_inner)] + [[1], [n_inner - 2], [n_inner - 1]]
+
+
+def relay(pairs, one):
+    rows = one.shape[0]
+    return exchange(jnp.concatenate([one] + [p[rows:] for p in pairs], 0), (0, 1))
+
+
 def slot_onehot(rows_ref, count_ref, nrows, partners):
     slots = rows_ref.shape[1]
     sub = lax.broadcasted_iota(jnp.int32, (nrows, slots), 0)
@@ -98,7 +121,7 @@
 
 def gather_kernel(hub_ref, count_ref, feat_ref, rows_ref, hub_out_ref, *outs):
     nrows = feat_ref.shape[0]
-    slots = rows_ref.shape[1]
+    n_inner, slots = rows_ref.shape
     nhub = hub_ref.shape[0]
     i = lax.axis_index("inner")
     feat = feat_ref[...]
@@ -108,10 +131,14 @@
     for h in range(nhub):
         hot = hot + ((sub == h) & (lane == hub_ref[h])).astype(F32)
     hub_out_ref[...] = dot(hot.astype(BF), feat)[:nhub].astype(BF)
-    pick = slot_onehot(rows_ref, count_ref, nrows, [i ^ d for d in range(len(outs))])
+    blocks = sent_blocks(n_inner)
+    order = [d for some in blocks for d in some]
+    pick = slot_onehot(rows_ref, count_ref, nrows, [i ^ d for d in order])
     rows = dot(pick, feat, TN).astype(BF)
-    for d, out in enumerate(outs):
-        out[...] = rows[d * slots : (d + 1) * slots, :]
+    at = 0
+    for some, out in zip(blocks, outs):
+        out[...] = rows[at * slots : (at + len(some)) * slots, :]
+        at += len(some)
 
 
 def prepare_kernel(feat_ref, adj_ref, wn_ref, cot_ref, feat_t, adj_cat, adj_t, wn_low, wn_t, cot_wide):
@@ -132,6 +159,7 @@
 def middle_kernel(
     steps,
     hub_steps,
+    n_inner,
     tile_src,
     feat,
     feat_t,
@@ -144,9 +172,9 @@
     cot,
     *rest,
 ):
-    n_inner = (len(rest) - 11) // 2
-    recv, (pre_out, gp_out, gown, keep, give), rest = rest[:n_inner], rest[n_inner : n_inner + 5], rest[n_inner + 5 :]
-    back, (src, agg, gsrc, wacc, wperm, hubf) = rest[:n_inner], rest[n_inner:]
+    count = (len(rest) - 11) // 2
+    recv, (pre_out, gp_out, gown, keep, give), rest = rest[:count], rest[count : count + 5], rest[count + 5 :]
+    back, (src, agg, gsrc, wacc, wperm, hubf) = rest[:count], rest[count:]
     o = lax.axis_index("outer")
     i = lax.axis_index("inner")
     table = flips(steps)
@@ -158,8 +186,8 @@
     nhubs = hubx.shape[0]
     hd = nhubs // len(table)
     src[0:nblocks] = feat[...]
-    for d in range(n_inner):
-        src[nblocks + (i ^ d)] = recv[d][...]
+    for d, (k, at) in places(n_inner, tile).items():
+        src[nblocks + (i ^ d)] = recv[k][at : at + tile, :]
     order = hub_order(hub_steps, n_inner, hd, nhubs)
     src[first_hub:] = dot(order, hubx[...]).astype(BF).reshape(ntiles - first_hub, tile, width)
     for b in range(nblocks):
@@ -184,8 +212,9 @@
             for u in range(t, last):
                 s = tile_src[b, u]
                 gsrc[s] = gsrc[s] + some[(u - t) * tile : (u - t + 1) * tile, :]
-    for d in range(n_inner):
-        back[d][...] = gsrc[nblocks + (i ^ d)].astype(BF)
+    for some, out in zip(sent_blocks(n_inner), back):
+        for k, d in enumerate(some):
+            out[k * tile : (k + 1) * tile, :] = gsrc[nblocks + (i ^ d)].astype(BF)
     gown[...] = gsrc[0:nblocks].reshape(nrows, width)
     wacc[0:width, :] = dot(feat_t[...], gp)
     wacc[width : 2 * width, :] = dot(agg[...], gp, TN)
@@ -210,10 +239,11 @@
 
 def add_returned(acc, rows_ref, count_ref, blocks, returned):
     i = lax.axis_index("inner")
+    tile = rows_ref.shape[1]
     for k in range(0, len(blocks), 2):
-        some = range(k, min(k + 2, len(blocks)))
-        put = slot_onehot(rows_ref, count_ref, acc.shape[0], [i ^ blocks[u] for u in some])
-        values = [returned[u][...] for u in some]
+        some = blocks[k : k + 2]
+        put = slot_onehot(rows_ref, count_ref, acc.shape[0], [i ^ d for d, _, _ in some])
+        values = [returned[ref][at : at + tile, :] for _, ref, at in some]
         acc[...] += dot(put, values[0] if len(values) == 1 else jnp.concatenate(values, axis=0))
 
 
@@ -288,27 +318,26 @@
     def shape(*dims, dtype=BF):
         return jax.ShapeDtypeStruct(dims, dtype)
 
-    hub_own, *outgoing = pl.pallas_call(
+    blocks = sent_blocks(n_inner)
+    sizes = tuple(shape(tile * len(some), width) for some in blocks)
+    hub_own, own_rows, *outgoing, one, far_a, far_b = pl.pallas_call(
         gather_kernel,
-        out_shape=(shape(hd, width),) + (shape(tile, width),) * n_inner,
+        out_shape=(shape(hd, width),) + sizes,
         in_specs=[SM, SM, VM, VM],
-        out_specs=(VM,) * (1 + n_inner),
+        out_specs=(VM,) * (1 + len(sizes)),
         compiler_params=params(60),
         cost_estimate=cost(4 * 10**8, 3 * 10**6),
         name="gather_rows",
     )(hub_rows, send_count, features, send_rows)
-    received = [outgoing[0]] + [None] * (n_inner - 1)
-    for d in range(1, n_inner):
-        received[d] = exchange(outgoing[d], (0, d))
-    far = n_inner // 2
+    relays = relayed(n_inner)
+    pairs = [exchange(p, (0, c)) for p, c in zip(outgoing, relays)]
     hubx = hub_own
     for group in groups[:-1]:
         hubx = spread(hubx, group)
-    ahead = range(far, far + far // 2)
-    hubx, held = lax.optimization_barrier((hubx, [received[d] for d in ahead]))
-    for d, value in zip(ahead, held):
-        received[d] = value
+    hubx, pairs, far_a, far_b = lax.optimization_barrier((hubx, pairs, far_a, far_b))
+    direct = [exchange(far_a, (0, n_inner - 2)), exchange(far_b, (0, n_inner - 1))]
     hubx = spread(hubx, groups[-1])
+    received = [own_rows, *pairs, relay(pairs, one), *direct]
     feat_t, adj_cat, adj_t, neigh_low, neigh_t, cot_wide = pl.pallas_call(
         prepare_kernel,
         out_shape=(
@@ -343,7 +372,7 @@
         shape(nrows, width, dtype=F32),
         shape(half, width),
         shape(half, width),
-    ) + (shape(tile, width),) * n_inner
+    ) + sizes
     operands = (
         features.reshape(nblocks, tile, width),
         feat_t,
@@ -357,7 +386,7 @@
         *received,
     )
     pre, gp, gown, keep, give, *back = pl.pallas_call(
-        functools.partial(middle_kernel, steps, hub_steps),
+        functools.partial(middle_kernel, steps, hub_steps, n_inner),
         out_shape=out_shape,
         in_specs=[SM] + [VM] * len(operands),
         out_specs=(VM,) * len(out_shape),
@@ -368,83 +397,62 @@
     )(tile_src, *operands)
     hidden_out = (pre * jax.nn.sigmoid(pre)).astype(BF)
 
-    returned = [back[0]] + [None] * (n_inner - 1)
-    odd = list(range(far + 1, n_inner, 2))
-    first = list(range(far, n_inner, 2))
-    second = [1] + odd[: far // 4]
-    third = [3] + odd[far // 4 :]
-    fourth = [d for d in range(2, far) if d != 3]
-
-    def start(ds, after=None):
-        held = [back[d] for d in ds]
-        if after is not None:
-            after, held = lax.optimization_barrier((after, held))
-        for d, value in zip(ds, held):
-            returned[d] = exchange(value, (0, d))
-        return after
-
-    def wait(value, ds):
-        value, held = lax.optimization_barrier((value, [returned[d] for d in ds]))
-        for d, block in zip(ds, held):
-            returned[d] = block
-        return value
-
-    def reduce(parts, group, pending=()):
+    back_own, *back, back_one, back_a, back_b = back
+
+    def reduce(parts, group):
         ways = 2 ** len(group)
         seg = [p.shape[0] // ways for p in parts[:2]]
         sends = []
         for c in range(1, ways):
             rows = [p[c * n : (c + 1) * n] for p, n in zip(parts, seg)]
             sends.append(jnp.concatenate(rows + [parts[2]], 0).astype(BF))
-        if pending:
-            sends = wait(sends, pending)
         w, hub, bias = parts[0][: seg[0]], parts[1][: seg[1]], parts[2]
         for flip, send in zip(flips(group)[1:], sends):
             got = exchange(send, flip).astype(F32)
             w, hub, bias = w + got[: seg[0]], hub + got[seg[0] : seg[0] + seg[1]], bias + got[seg[0] + seg[1] :]
         return w, hub, bias
 
-    start(first)
+    tie = lax.optimization_barrier
+    pairs = [exchange(p, (0, c)) for p, c in zip(back, relays)]
     got = exchange(give, flips(groups[0])[1])
     part = keep.astype(F32) + got.astype(F32)
     parts = (part[:width], part[width : width + nhubs // 2], part[width + nhubs // 2 : width + nhubs // 2 + 8])
     for group in groups[1:-1]:
         parts = reduce(parts, group)
-    parts = start(second, parts)
+    parts, back_one = tie((parts, back_one))
+    near = relay(pairs, back_one)
     part, hub_grad, bias_sum = reduce(parts, groups[-1])
-    mine = wait(part.astype(BF), first)
-    mine, hidden_out = lax.optimization_barrier((mine, hidden_out))
-    mine = start(third, mine)
+    mine, hidden_out, back_a, back_b = tie((part.astype(BF), hidden_out, back_a, back_b))
+    direct = [exchange(back_a, (0, n_inner - 2)), exchange(back_b, (0, n_inner - 1))]
     gathered = spread(mine, groups[-1])
-    gathered = start(fourth, gathered)
-    gathered = wait(gathered, second)
+    gathered, near = tie((gathered, near))
     for group in groups[1:-1][::-1]:
         gathered = spread(gathered, group)
-    gathered = wait(gathered, third + fourth)
-
-    blocks = [0] + first + second
+    gathered, direct = tie((gathered, direct))
+
+    where = places(n_inner, tile)
+    first = [(d, k, at) for d, (k, at) in where.items() if d < n_inner - 2]
     own = pl.pallas_call(
-        functools.partial(first_scatter_kernel, blocks),
+        functools.partial(first_scatter_kernel, first),
         out_shape=shape(nrows, width, dtype=F32),
-        in_specs=[SM] + [VM] * (4 + len(blocks)),
+        in_specs=[SM] + [VM] * (6 + len(pairs)),
         out_specs=VM,
         compiler_params=params(16),
         cost_estimate=cost(4 * 10**8, 3 * 10**6),
         name="scatter_first",
-    )(send_count, send_rows, gown, gp, self_low, *[returned[d] for d in blocks])
+    )(send_count, send_rows, gown, gp, self_low, back_own, *pairs, near)
     gathered, own = lax.optimization_barrier((gathered, own))
     other = exchange(gathered, flips(groups[0])[1])
-    blocks = third + fourth
     grad_features = pl.pallas_call(
-        functools.partial(last_scatter_kernel, blocks),
+        functools.partial(last_scatter_kernel, [(n_inner - 2, 0, 0), (n_inner - 1, 1, 0)]),
         out_shape=shape(nrows, width),
-        in_specs=[SM, SM] + [VM] * (3 + len(blocks)),
+        in_specs=[SM, SM] + [VM] * 5,
         out_specs=VM,
         scratch_shapes=[pltpu.VMEM((nrows, width), F32)],
         compiler_params=params(16),
         cost_estimate=cost(2 * 10**8, 2 * 10**6),
         name="scatter_last",
-    )(hub_rows, send_count, send_rows, own, hub_grad, *[returned[d] for d in blocks])
+    )(hub_rows, send_count, send_rows, own, hub_grad, *direct)
     factor = 1.0 / float(nrows * ndevice) ** 0.5
     total_self, total_neigh, total_bias = pl.pallas_call(
         functools.partial(finish_kernel, steps, n_inner, factor),

time: 98.9 us -> 91.5 us (0.925)
  waiting for transfers between devices: 39 us -> 31.7 us
  starting transfers between devices: 44.5 us -> 43.3 us
  other arithmetic: 2.33 us -> 3.37 us
    ppermute x35 -> x31, waiting for transfers between devices: 39 us -> 31.7 us  [exchange(): lax.ppermute(x, ('outer', 'inner'), [(s, s ^ mask) for s in range(n_outer...]
    ppermute x35 -> x31, starting transfers between devices: 44.5 us -> 43.3 us  [exchange(): lax.ppermute(x, ('outer', 'inner'), [(s, s ^ mask) for s in range(n_outer...]
    concatenate x0 -> x2, other arithmetic: none -> 1.02 us  [relay(): jnp.concatenate([one] + [p[rows:] for p in pairs], 0)]
  transfers between devices with their start and end apart: 35 -> 31, of which waited for: 19 -> 17; matrix products, arithmetic and copies ran while one was open for 3% -> 4% of each run, Pallas kernels for 3% -> 4%
where the time goes in v4:
time: 91.5 us; the launch traced here: 91.3 us
  starting transfers between devices  43.3 us (47%)
  waiting for transfers between devices  31.7 us (35%)
  Pallas kernels  11.2 us (12%)
  other arithmetic  3.37 us (4%)
  between operations  1.13 us (1%)
    ppermute x31, starting transfers between devices, exchange(): lax.ppermute(x, ('outer', 'inner'), [(s, s ^ mask) for s in range(n_outer...  43.3 us
    ppermute x31, waiting for transfers between devices, exchange(): lax.ppermute(x, ('outer', 'inner'), [(s, s ^ mask) for s in range(n_outer...  31.7 us
    pallas_call x1, Pallas kernels, body(): pl.pallas_call(functools.partial(middle_kernel, steps, hub_steps, n_inner...  3.65 us
    pallas_call x1, Pallas kernels, body(): pl.pallas_call(gather_kernel, out_shape=(shape(hd, width),) + sizes, in_s...  2.68 us
  transfers between devices with their start and end apart: 31, of which 17 were waited for; matrix products, arithmetic and copies ran while one was open for 4% of the time, Pallas kernels for 4%

profile of v4, /device:TPU:0, one launch (start us, length us, event | category | flops | bytes accessed | tf_op | source)
XLA Modules:
  0.0 91.3 jit_solution(8752881985629852875)
XLA Ops:
  0.6 2.7 %gather_rows.1 = (bf16[4,512]{1,0:T(4,128)(2,1)}, bf16[128,512]{1,0:T(8,128)(2,1)}, bf16[256,512]{1,0:T(8,128)(2,1)}, bf16[256,512]{1,0:T(8,128)(2,1)}, bf16[128...) custom-call(s32[4]{0:T(128)} %hub_ref.3, s32[1,8]{1,0:T(1,128)} %count_ref.5, ...), custom_call_target="tpu_custom_call" | custom-call | flops 400000000 | bytes 3000000 | tf_op jit(solution)/shard_map/gather_rows/pallas_call | solution.py:323
  3.3 3.0 %collective-permute-start.4 = (bf16[256,512]{1,0:T(8,128)(2,1)}, bf16[256,512]{1,0:T(8,128)(2,1)S(1)}, u32[]{:S(2)}, u32[]{:S(2)}) collective-permute-start(bf16[256,512]{1,0:T(8,128)(2,1)} %get-tuple-element.54), channel_id=1, source_target_pairs={{0,2},{1,3},{2,0},{3,1},{4,6},{5,7},{6,4},{7,5},{8,10},{9,11},{10,... | collective-permute-start | bytes 786440 | tf_op jit(solution)/shard_map/ppermute | solution.py:80
  6.3 2.6 %collective-permute-start.5 = (bf16[256,512]{1,0:T(8,128)(2,1)}, bf16[256,512]{1,0:T(8,128)(2,1)S(1)}, u32[]{:S(2)}, u32[]{:S(2)}) collective-permute-start(bf16[256,512]{1,0:T(8,128)(2,1)} %get-tuple-element.55), channel_id=1, source_target_pairs={{0,4},{1,5},{2,6},{3,7},{4,0},{5,1},{6,2},{7,3},{8,12},{9,13},{10,... | collective-permute-start | bytes 786440 | tf_op jit(solution)/shard_map/ppermute | solution.py:80
  8.9 1.4 %collective-permute-done = bf16[4,512]{1,0:T(4,128)(2,1)S(1)} collective-permute-done((bf16[4,512]{1,0:T(4,128)(2,1)}, bf16[4,512]{1,0:T(4,128)(2,1)S(1)}, u32[]{:S(2)}, u32[]{:S(2)}) %collective-permute-start) | collective-permute-done | bytes 4128 | tf_op jit(solution)/shard_map/ppermute | solution.py:80
  10.3 0.7 pad_maximum_fusion.12
  11.0 2.4 %collective-permute-start.3 = (bf16[8,512]{1,0:T(8,128)(2,1)S(1)}, bf16[8,512]{1,0:T(8,128)(2,1)S(1)}, u32[]{:S(2)}, u32[]{:S(2)}) collective-permute-start(bf16[8,512]{1,0:T(8,128)(2,1)S(1)} %pad_maximum_fusion.12), channel_id=1, source_target_pairs={{0,17},{1,16},{2,19},{3,18},{4,21},{5,20},{6,23},{7,22},{8,25},{9,... | collective-permute-start | bytes 24584 | tf_op jit(solution)/shard_map/ppermute | solution.py:80
  13.4 0.5 collective-permute-start.2
  14.0 0.5 collective-permute-start.1
  14.5 1.1 %collective-permute-done.3 = bf16[8,512]{1,0:T(8,128)(2,1)S(1)} collective-permute-done((bf16[8,512]{1,0:T(8,128)(2,1)S(1)}, bf16[8,512]{1,0:T(8,128)(2,1)S(1)}, u32[]{:S(2)}, u32[]{:S(2)}) %collective-permute-start.3) | collective-permute-done | bytes 8224 | tf_op jit(solution)/shard_map/ppermute | solution.py:80
  15.6 1.5 %collective-permute-done.2 = bf16[8,512]{1,0:T(8,128)(2,1)S(1)} collective-permute-done((bf16[8,512]{1,0:T(8,128)(2,1)S(1)}, bf16[8,512]{1,0:T(8,128)(2,1)S(1)}, u32[]{:S(2)}, u32[]{:S(2)}) %collective-permute-start.2) | collective-permute-done | bytes 8224 | tf_op jit(solution)/shard_map/ppermute | solution.py:80
  17.1 0.5 collective-permute-done.1
  17.6 0.7 collective-permute-done.4.rest_1_
  18.4 2.5 %collective-permute-done.5.rest_2_ = bf16[256,512]{1,0:T(8,128)(2,1)S(1)} collective-permute-done((bf16[256,512]{1,0:T(8,128)(2,1)}, bf16[256,512]{1,0:T(8,128)(2,1)S(1)}, u32[]{:S(2)}, u32[]{:S(2)}) %collective-permute-start.5) | collective-permute-done | bytes 262176 | tf_op jit(solution)/shard_map/ppermute | solution.py:80
  20.9 2.5 %collective-permute-start.8 = (bf16[32,512]{1,0:T(8,128)(2,1)S(1)}, bf16[32,512]{1,0:T(8,128)(2,1)S(1)}, u32[]{:S(2)}, u32[]{:S(2)}) collective-permute-start(bf16[32,512]{1,0:T(8,128)(2,1)S(1)} %pad_maximum_fusion.11), channel_id=1, source_target_pairs={{0,6},{1,7},{2,4},{3,5},{4,2},{5,3},{6,0},{7,1},{8,14},{9,15},{10,... | collective-permute-start | bytes 98312 | tf_op jit(solution)/shard_map/ppermute | solution.py:80
  23.4 0.0 copy-start
  23.4 0.0 copy-start.10
  23.4 1.0 %pad_maximum_fusion.1 = bf16[384,512]{1,0:T(8,128)(2,1)S(1)} fusion(bf16[128,512]{1,0:T(8,128)(2,1)S(1)} %slice.141, bf16[128,512]{1,0:T(8,128)(2,1)S(1)} %slice.140, bf16[128,512]{1,0:T(8,128)(2,1)} %get-tuple-element.67), kind=kLoop, calls=%fused_computation.4 | loop fusion | flops 1179648 | bytes 786432 | tf_op jit(solution)/shard_map/concatenate | solution.py:108
  24.4 1.6 %collective-permute-start.9 = (bf16[384,512]{1,0:T(8,128)(2,1)S(1)}, bf16[384,512]{1,0:T(8,128)(2,1)S(1)}, u32[]{:S(2)}, u32[]{:S(2)}) collective-permute-start(bf16[384,512]{1,0:T(8,128)(2,1)S(1)} %pad_maximum_fusion.1), channel_id=1, source_target_pairs={{0,1},{1,0},{2,3},{3,2},{4,5},{5,4},{6,7},{7,6},{8,9},{9,8},{10,11... | collective-permute-start | bytes 1179656 | tf_op jit(solution)/shard_map/ppermute | solution.py:80
  26.0 0.1 convert_element_type.39.ws_ref
  26.1 0.0 copy-start.1
  26.1 0.0 copy-start.2
  26.1 0.1 collective-permute-start.7
  26.2 1.9 %collective-permute-start.6 = (bf16[32,512]{1,0:T(8,128)(2,1)S(1)}, bf16[32,512]{1,0:T(8,128)(2,1)S(1)}, u32[]{:S(2)}, u32[]{:S(2)}) collective-permute-start(bf16[32,512]{1,0:T(8,128)(2,1)S(1)} %pad_maximum_fusion.11), channel_id=1, source_target_pairs={{0,4},{1,5},{2,6},{3,7},{4,0},{5,1},{6,2},{7,3},{8,12},{9,13},{10,... | collective-permute-start | bytes 98312 | tf_op jit(solution)/shard_map/ppermute | solution.py:80
  28.1 2.5 %collective-permute-start.10 = (bf16[128,512]{1,0:T(8,128)(2,1)S(1)}, bf16[128,512]{1,0:T(8,128)(2,1)S(1)}, u32[]{:S(2)}, u32[]{:S(2)}) collective-permute-start(bf16[128,512]{1,0:T(8,128)(2,1)S(1)} %copy-done.12), channel_id=1, source_target_pairs={{0,6},{1,7},{2,4},{3,5},{4,2},{5,3},{6,0},{7,1},{8,14},{9,15},{10,... | collective-permute-start | bytes 393224 | tf_op jit(solution)/shard_map/ppermute | solution.py:80
  30.6 1.3 %collective-permute-start.11 = (bf16[128,512]{1,0:T(8,128)(2,1)S(1)}, bf16[128,512]{1,0:T(8,128)(2,1)S(1)}, u32[]{:S(2)}, u32[]{:S(2)}) collective-permute-start(bf16[128,512]{1,0:T(8,128)(2,1)S(1)} %copy-done.11), channel_id=1, source_target_pairs={{0,7},{1,6},{2,5},{3,4},{4,3},{5,2},{6,1},{7,0},{8,15},{9,14},{10,... | collective-permute-start | bytes 393224 | tf_op jit(solution)/shard_map/ppermute | solution.py:80
  31.9 0.4 convolution_add_fusion.pre0
  32.3 0.0 copy-start.8
  32.3 0.5 prepare.1
  32.9 2.1 %collective-permute-done.10.rest_4_ = bf16[128,512]{1,0:T(8,128)(2,1)S(1)} collective-permute-done((bf16[128,512]{1,0:T(8,128)(2,1)S(1)}, bf16[128,512]{1,0:T(8,128)(2,1)S(1)}, u32[]{:S(2)}, u32[]{:S(2)}) %collective-permute-start.10) | collective-permute-done | bytes 131104 | tf_op jit(solution)/shard_map/ppermute | solution.py:80
  35.0 3.4 %collective-permute-done.11.rest_5_ = bf16[128,512]{1,0:T(8,128)(2,1)S(1)} collective-permute-done((bf16[128,512]{1,0:T(8,128)(2,1)S(1)}, bf16[128,512]{1,0:T(8,128)(2,1)S(1)}, u32[]{:S(2)}, u32[]{:S(2)}) %collective-permute-start.11) | collective-permute-done | bytes 131104 | tf_op jit(solution)/shard_map/ppermute | solution.py:80
  38.4 3.6 %middle.1 = (f32[384,512]{1,0:T(8,128)S(1)}, bf16[384,512]{1,0:T(8,128)(2,1)S(1)}, f32[384,512]{1,0:T(8,128)S(1)}, bf16[592,512]{1,0:T(8,128)(2,1)S(1)}, bf16[59...) custom-call(s32[3,6]{1,0:T(4,128)S(1)} %copy-done.7, ...), custom_call_target="tpu_custom_call" | custom-call | flops 2000000000 | bytes 9000000 | tf_op jit(solution)/shard_map/middle/pallas_call | solution.py:388
  42.0 0.1 collective-permute-start.12
  42.1 1.8 %collective-permute-start.22 = (bf16[256,512]{1,0:T(8,128)(2,1)S(1)}, bf16[256,512]{1,0:T(8,128)(2,1)S(1)}, u32[]{:S(2)}, u32[]{:S(2)}) collective-permute-start(bf16[256,512]{1,0:T(8,128)(2,1)S(1)} %get-tuple-element.82), channel_id=1, source_target_pairs={{0,2},{1,3},{2,0},{3,1},{4,6},{5,7},{6,4},{7,5},{8,10},{9,11},{10,... | collective-permute-start | bytes 786440 | tf_op jit(solution)/shard_map/ppermute | solution.py:80
  43.9 0.5 collective-permute-start.23
  44.4 0.2 convert_add_fusion
  44.7 2.5 %collective-permute-start.15 = (bf16[152,512]{1,0:T(8,128)(2,1)S(1)}, bf16[152,512]{1,0:T(8,128)(2,1)S(1)}, u32[]{:S(2)}, u32[]{:S(2)}) collective-permute-start(bf16[152,512]{1,0:T(8,128)(2,1)S(1)} %pad_maximum_fusion.5), channel_id=1, source_target_pairs={{0,17},{1,16},{2,19},{3,18},{4,21},{5,20},{6,23},{7,22},{8,25},{9,... | collective-permute-start | bytes 466952 | tf_op jit(solution)/shard_map/ppermute | solution.py:80
  47.2 0.6 collective-permute-start.13
  47.8 0.5 collective-permute-start.14
  48.3 7.4 %collective-permute-done.22.rest_1_ = bf16[256,512]{1,0:T(8,128)(2,1)S(1)} collective-permute-done((bf16[256,512]{1,0:T(8,128)(2,1)S(1)}, bf16[256,512]{1,0:T(8,128)(2,1)S(1)}, u32[]{:S(2)}, u32[]{:S(2)}) %collective-permute-start.22) | collective-permute-done | bytes 262176 | tf_op jit(solution)/shard_map/ppermute | solution.py:80
  55.7 3.1 %collective-permute-done.23.rest_2_ = bf16[256,512]{1,0:T(8,128)(2,1)S(1)} collective-permute-done((bf16[256,512]{1,0:T(8,128)(2,1)S(1)}, bf16[256,512]{1,0:T(8,128)(2,1)S(1)}, u32[]{:S(2)}, u32[]{:S(2)}) %collective-permute-start.23) | collective-permute-done | bytes 262176 | tf_op jit(solution)/shard_map/ppermute | solution.py:80
  59.0 0.1 slice_add_fusion
  59.2 0.4 collective-permute-start.16
  59.6 2.1 %collective-permute-start.17 = (bf16[44,512]{1,0:T(8,128)(2,1)S(1)}, bf16[44,512]{1,0:T(8,128)(2,1)S(1)}, u32[]{:S(2)}, u32[]{:S(2)}) collective-permute-start(bf16[44,512]{1,0:T(8,128)(2,1)S(1)} %get-tuple-element.113), channel_id=1, source_target_pairs={{0,2},{1,3},{2,0},{3,1},{4,6},{5,7},{6,4},{7,5},{8,10},{9,11},{10,... | collective-permute-start | bytes 135176 | tf_op jit(solution)/shard_map/ppermute | solution.py:80
  61.7 1.9 %collective-permute-start.18 = (bf16[44,512]{1,0:T(8,128)(2,1)S(1)}, bf16[44,512]{1,0:T(8,128)(2,1)S(1)}, u32[]{:S(2)}, u32[]{:S(2)}) collective-permute-start(bf16[44,512]{1,0:T(8,128)(2,1)S(1)} %get-tuple-element.114), channel_id=1, source_target_pairs={{0,6},{1,7},{2,4},{3,5},{4,2},{5,3},{6,0},{7,1},{8,14},{9,15},{10,... | collective-permute-start | bytes 135176 | tf_op jit(solution)/shard_map/ppermute | solution.py:80
  63.7 0.0 copy-start.5
  63.7 1.4 %collective-permute-start.24 = (bf16[384,512]{1,0:T(8,128)(2,1)S(1)}, bf16[384,512]{1,0:T(8,128)(2,1)S(1)}, u32[]{:S(2)}, u32[]{:S(2)}) collective-permute-start(bf16[384,512]{1,0:T(8,128)(2,1)S(1)} %pad_maximum_fusion.2), channel_id=1, source_target_pairs={{0,1},{1,0},{2,3},{3,2},{4,5},{5,4},{6,7},{7,6},{8,9},{9,8},{10,11... | collective-permute-start | bytes 1179656 | tf_op jit(solution)/shard_map/ppermute | solution.py:80
  65.2 1.0 %multiply_convert_fusion = bf16[384,512]{1,0:T(8,128)(2,1)} fusion(f32[384,512]{1,0:T(8,128)S(1)} %get-tuple-element.76), kind=kLoop, calls=%fused_computation.2 | loop fusion | flops 983040 | bytes 1179648 | tf_op jit(solution)/shard_map/convert_element_type | solution.py:398
  66.2 1.6 %collective-permute-done.18 = bf16[44,512]{1,0:T(8,128)(2,1)S(1)} collective-permute-done((bf16[44,512]{1,0:T(8,128)(2,1)S(1)}, bf16[44,512]{1,0:T(8,128)(2,1)S(1)}, u32[]{:S(2)}, u32[]{:S(2)}) %collective-permute-start.18) | collective-permute-done | bytes 45088 | tf_op jit(solution)/shard_map/ppermute | solution.py:80
  67.8 2.0 %collective-permute-start.21 = (bf16[32,512]{1,0:T(8,128)(2,1)S(1)}, bf16[32,512]{1,0:T(8,128)(2,1)S(1)}, u32[]{:S(2)}, u32[]{:S(2)}) collective-permute-start(bf16[32,512]{1,0:T(8,128)(2,1)S(1)} %fusion), channel_id=1, source_target_pairs={{0,6},{1,7},{2,4},{3,5},{4,2},{5,3},{6,0},{7,1},{8,14},{9,15},{10,... | collective-permute-start | bytes 98312 | tf_op jit(solution)/shard_map/ppermute | solution.py:80
  69.7 2.5 %collective-permute-start.19 = (bf16[32,512]{1,0:T(8,128)(2,1)S(1)}, bf16[32,512]{1,0:T(8,128)(2,1)S(1)}, u32[]{:S(2)}, u32[]{:S(2)}) collective-permute-start(bf16[32,512]{1,0:T(8,128)(2,1)S(1)} %fusion), channel_id=1, source_target_pairs={{0,4},{1,5},{2,6},{3,7},{4,0},{5,1},{6,2},{7,3},{8,12},{9,13},{10,... | collective-permute-start | bytes 98312 | tf_op jit(solution)/shard_map/ppermute | solution.py:80
  72.2 1.3 %collective-permute-done.21 = bf16[32,512]{1,0:T(8,128)(2,1)S(1)} collective-permute-done((bf16[32,512]{1,0:T(8,128)(2,1)S(1)}, bf16[32,512]{1,0:T(8,128)(2,1)S(1)}, u32[]{:S(2)}, u32[]{:S(2)}) %collective-permute-start.21) | collective-permute-done | bytes 32800 | tf_op jit(solution)/shard_map/ppermute | solution.py:80
  73.6 0.3 collective-permute-done.20
  73.9 0.6 collective-permute-done.19
  74.6 2.3 %collective-permute-start.27 = (bf16[128,512]{1,0:T(8,128)(2,1)S(1)}, bf16[128,512]{1,0:T(8,128)(2,1)S(1)}, u32[]{:S(2)}, u32[]{:S(2)}) collective-permute-start(bf16[128,512]{1,0:T(8,128)(2,1)S(1)} %pad_maximum_fusion.7), channel_id=1, source_target_pairs={{0,17},{1,16},{2,19},{3,18},{4,21},{5,20},{6,23},{7,22},{8,25},{9,... | collective-permute-start | bytes 393224 | tf_op jit(solution)/shard_map/ppermute | solution.py:80
  76.9 0.5 collective-permute-start.26
  77.4 0.7 collective-permute-start.25
  78.1 1.9 %collective-permute-start.28 = (bf16[128,512]{1,0:T(8,128)(2,1)S(1)}, bf16[128,512]{1,0:T(8,128)(2,1)S(1)}, u32[]{:S(2)}, u32[]{:S(2)}) collective-permute-start(bf16[128,512]{1,0:T(8,128)(2,1)S(1)} %get-tuple-element.85), channel_id=1, source_target_pairs={{0,6},{1,7},{2,4},{3,5},{4,2},{5,3},{6,0},{7,1},{8,14},{9,15},{10,... | collective-permute-start | bytes 393224 | tf_op jit(solution)/shard_map/ppermute | solution.py:80
  80.0 2.6 %collective-permute-start.29 = (bf16[128,512]{1,0:T(8,128)(2,1)S(1)}, bf16[128,512]{1,0:T(8,128)(2,1)S(1)}, u32[]{:S(2)}, u32[]{:S(2)}) collective-permute-start(bf16[128,512]{1,0:T(8,128)(2,1)S(1)} %get-tuple-element.86), channel_id=1, source_target_pairs={{0,7},{1,6},{2,5},{3,4},{4,3},{5,2},{6,1},{7,0},{8,15},{9,14},{10,... | collective-permute-start | bytes 393224 | tf_op jit(solution)/shard_map/ppermute | solution.py:80
  82.7 1.2 %scatter_first.1.own_ref = f32[384,512]{1,0:T(8,128)S(1)} custom-call(s32[1,8]{1,0:T(1,128)S(1)} %copy-done.5, s32[8,128]{1,0:T(8,128)S(1)} %copy-done.4, f32[384,512]{1,0:T(8,128)S(1)} %get-tuple-element.88.gown_ref, bf16[384,512]{1,0:T(8,128)(2,1)S(1)} %get-tuple-element.89.gp_ref, bf16[512,512]{1,0:T(8,128)(2,1)S(1)} %convert_element_type.39.ws_ref, ...), custom_call_target="tpu_custom_call" | custom-call | flops 400000000 | bytes 3000000 | tf_op jit(solution)/shard_map/scatter_first/pallas_call | solution.py:435
  84.0 1.0 %collective-permute-done.28.rest_0_ = bf16[128,512]{1,0:T(8,128)(2,1)S(1)} collective-permute-done((bf16[128,512]{1,0:T(8,128)(2,1)S(1)}, bf16[128,512]{1,0:T(8,128)(2,1)S(1)}, u32[]{:S(2)}, u32[]{:S(2)}) %collective-permute-start.28) | collective-permute-done | bytes 131104 | tf_op jit(solution)/shard_map/ppermute | solution.py:80
  85.0 2.8 %collective-permute-done.29.rest_1_ = bf16[128,512]{1,0:T(8,128)(2,1)S(1)} collective-permute-done((bf16[128,512]{1,0:T(8,128)(2,1)S(1)}, bf16[128,512]{1,0:T(8,128)(2,1)S(1)}, u32[]{:S(2)}, u32[]{:S(2)}) %collective-permute-start.29) | collective-permute-done | bytes 131104 | tf_op jit(solution)/shard_map/ppermute | solution.py:80
  87.9 1.6 %scatter_last.1 = bf16[384,512]{1,0:T(8,128)(2,1)} custom-call(s32[4]{0:T(128)S(1)} %copy-done.6, s32[1,8]{1,0:T(1,128)S(1)} %copy-done.5, s32[8,128]{1,0:T(8,128)S(1)} %copy-done.4, f32[384,512]{1,0:T(8,128)S(1)} %scatter_first.1.own_ref, f32[4,512]{1,0:T(4,128)S(1)} %slice_add_fusion.15.hub_grad_ref, bf16[128,512]{1,0:T(8,128)(2,1)S(1)} %collective-permute-done.28.rest_0_, ...), custom_call_target="tpu_custom_call" | custom-call | flops 200000000 | bytes 2000000 | tf_op jit(solution)/shard_map/scatter_last/pallas_call | solution.py:446
  89.5 0.3 collective-permute-done.30.y_ref
  89.7 1.6 %finish.1 = (f32[512,512]{1,0:T(8,128)}, f32[512,512]{1,0:T(8,128)}, f32[1,512]{1,0:T(1,128)}) custom-call(bf16[512,512]{1,0:T(8,128)(2,1)S(1)} %pad_maximum_fusion.x_ref, bf16[512,512]{1,0:T(8,128)(2,1)S(1)} %collective-permute-done.30.y_ref, f32[8,512]{1,0:T(8,128)S(1)} %slice_add_fusion.9.bias_in), custom_call_target="tpu_custom_call" | custom-call | flops 1000000 | bytes 3000000 | tf_op jit(solution)/shard_map/finish/pallas_call | solution.py:457
  (69 shorter events, 0.5 us)
Async XLA Ops:
  0.6 25.4 %copy-start.9 = (f32[512,512]{1,0:T(8,128)S(1)}, f32[512,512]{1,0:T(8,128)}, u32[]{:S(2)}) copy-start(f32[512,512]{1,0:T(8,128)} %param.16) | copy-start | bytes 3145732
  3.3 15.0 %collective-permute-start.4 = (bf16[256,512]{1,0:T(8,128)(2,1)}, bf16[256,512]{1,0:T(8,128)(2,1)S(1)}, u32[]{:S(2)}, u32[]{:S(2)}) collective-permute-start(bf16[256,512]{1,0:T(8,128)(2,1)} %get-tuple-element.54), channel_id=1, source_target_pairs={{0,2},{1,3},{2,0},{3,1},{4,6},{5,7},{6,4},{7,5},{8,10},{9,11},{10,... | collective-permute-start | bytes 786440 | tf_op jit(solution)/shard_map/ppermute | solution.py:80
  6.3 14.5 %collective-permute-start.5 = (bf16[256,512]{1,0:T(8,128)(2,1)}, bf16[256,512]{1,0:T(8,128)(2,1)S(1)}, u32[]{:S(2)}, u32[]{:S(2)}) collective-permute-start(bf16[256,512]{1,0:T(8,128)(2,1)} %get-tuple-element.55), channel_id=1, source_target_pairs={{0,4},{1,5},{2,6},{3,7},{4,0},{5,1},{6,2},{7,3},{8,12},{9,13},{10,... | collective-permute-start | bytes 786440 | tf_op jit(solution)/shard_map/ppermute | solution.py:80
  8.9 1.4 %collective-permute-start = (bf16[4,512]{1,0:T(4,128)(2,1)}, bf16[4,512]{1,0:T(4,128)(2,1)S(1)}, u32[]{:S(2)}, u32[]{:S(2)}) collective-permute-start(bf16[4,512]{1,0:T(4,128)(2,1)} %get-tuple-element.53), channel_id=1, source_target_pairs={{0,8},{1,9},{2,10},{3,11},{4,12},{5,13},{6,14},{7,15},{8,0},{9,1},... | collective-permute-start | bytes 12296 | tf_op jit(solution)/shard_map/ppermute | solution.py:80
  11.0 4.5 %collective-permute-start.3 = (bf16[8,512]{1,0:T(8,128)(2,1)S(1)}, bf16[8,512]{1,0:T(8,128)(2,1)S(1)}, u32[]{:S(2)}, u32[]{:S(2)}) collective-permute-start(bf16[8,512]{1,0:T(8,128)(2,1)S(1)} %pad_maximum_fusion.12), channel_id=1, source_target_pairs={{0,17},{1,16},{2,19},{3,18},{4,21},{5,20},{6,23},{7,22},{8,25},{9,... | collective-permute-start | bytes 24584 | tf_op jit(solution)/shard_map/ppermute | solution.py:80
  13.4 3.7 %collective-permute-start.2 = (bf16[8,512]{1,0:T(8,128)(2,1)S(1)}, bf16[8,512]{1,0:T(8,128)(2,1)S(1)}, u32[]{:S(2)}, u32[]{:S(2)}) collective-permute-start(bf16[8,512]{1,0:T(8,128)(2,1)S(1)} %pad_maximum_fusion.12), channel_id=1, source_target_pairs={{0,16},{1,17},{2,18},{3,19},{4,20},{5,21},{6,22},{7,23},{8,24},{9,... | collective-permute-start | bytes 24584 | tf_op jit(solution)/shard_map/ppermute | solution.py:80
  14.0 3.7 %collective-permute-start.1 = (bf16[8,512]{1,0:T(8,128)(2,1)S(1)}, bf16[8,512]{1,0:T(8,128)(2,1)S(1)}, u32[]{:S(2)}, u32[]{:S(2)}) collective-permute-start(bf16[8,512]{1,0:T(8,128)(2,1)S(1)} %pad_maximum_fusion.12), channel_id=1, source_target_pairs={{0,1},{1,0},{2,3},{3,2},{4,5},{5,4},{6,7},{7,6},{8,9},{9,8},{10,11... | collective-permute-start | bytes 24584 | tf_op jit(solution)/shard_map/ppermute | solution.py:80
  20.9 9.7 %collective-permute-start.8 = (bf16[32,512]{1,0:T(8,128)(2,1)S(1)}, bf16[32,512]{1,0:T(8,128)(2,1)S(1)}, u32[]{:S(2)}, u32[]{:S(2)}) collective-permute-start(bf16[32,512]{1,0:T(8,128)(2,1)S(1)} %pad_maximum_fusion.11), channel_id=1, source_target_pairs={{0,6},{1,7},{2,4},{3,5},{4,2},{5,3},{6,0},{7,1},{8,14},{9,15},{10,... | collective-permute-start | bytes 98312 | tf_op jit(solution)/shard_map/ppermute | solution.py:80
  23.4 4.7 %copy-start.12 = (bf16[128,512]{1,0:T(8,128)(2,1)S(1)}, bf16[128,512]{1,0:T(8,128)(2,1)}, u32[]{:S(2)}) copy-start(bf16[128,512]{1,0:T(8,128)(2,1)} %get-tuple-element.68) | copy-start | bytes 393220
  23.4 7.2 %copy-start.11 = (bf16[128,512]{1,0:T(8,128)(2,1)S(1)}, bf16[128,512]{1,0:T(8,128)(2,1)}, u32[]{:S(2)}) copy-start(bf16[128,512]{1,0:T(8,128)(2,1)} %get-tuple-element.69) | copy-start | bytes 393220
  23.4 8.5 %copy-start = (bf16[384,512]{1,0:T(8,128)(2,1)S(1)}, bf16[384,512]{1,0:T(8,128)(2,1)}, u32[]{:S(2)}) copy-start(bf16[384,512]{1,0:T(8,128)(2,1)} %feat_ref.3) | copy-start | bytes 1179652
  23.4 8.4 %copy-start.10 = (f32[512]{0:T(512)S(1)}, f32[512]{0:T(512)}, u32[]{:S(2)}) copy-start(f32[512]{0:T(512)} %param.18) | copy-start | bytes 6148
  24.4 13.9 %collective-permute-start.9 = (bf16[384,512]{1,0:T(8,128)(2,1)S(1)}, bf16[384,512]{1,0:T(8,128)(2,1)S(1)}, u32[]{:S(2)}, u32[]{:S(2)}) collective-permute-start(bf16[384,512]{1,0:T(8,128)(2,1)S(1)} %pad_maximum_fusion.1), channel_id=1, source_target_pairs={{0,1},{1,0},{2,3},{3,2},{4,5},{5,4},{6,7},{7,6},{8,9},{9,8},{10,11... | collective-permute-start | bytes 1179656 | tf_op jit(solution)/shard_map/ppermute | solution.py:80
  26.0 6.2 %copy-start.3 = (bf16[384,512]{1,0:T(8,128)(2,1)S(1)}, bf16[384,512]{1,0:T(8,128)(2,1)}, u32[]{:S(2)}) copy-start(bf16[384,512]{1,0:T(8,128)(2,1)} %cot_ref.1) | copy-start | bytes 1179652
  26.1 6.2 %copy-start.1 = (f32[512,512]{1,0:T(8,128)S(1)}, f32[512,512]{1,0:T(8,128)}, u32[]{:S(2)}) copy-start(f32[512,512]{1,0:T(8,128)} %wn_ref.1) | copy-start | bytes 3145732
  26.1 6.2 %copy-start.2 = (bf16[18,128,128]{2,1,0:T(8,128)(2,1)S(1)}, bf16[18,128,128]{2,1,0:T(8,128)(2,1)}, u32[]{:S(2)}) copy-start(bf16[18,128,128]{2,1,0:T(8,128)(2,1)} %adj_ref.1) | copy-start | bytes 1769476
  26.1 6.7 %collective-permute-start.7 = (bf16[32,512]{1,0:T(8,128)(2,1)S(1)}, bf16[32,512]{1,0:T(8,128)(2,1)S(1)}, u32[]{:S(2)}, u32[]{:S(2)}) collective-permute-start(bf16[32,512]{1,0:T(8,128)(2,1)S(1)} %pad_maximum_fusion.11), channel_id=1, source_target_pairs={{0,2},{1,3},{2,0},{3,1},{4,6},{5,7},{6,4},{7,5},{8,10},{9,11},{10,... | collective-permute-start | bytes 98312 | tf_op jit(solution)/shard_map/ppermute | solution.py:80
  26.2 6.6 %collective-permute-start.6 = (bf16[32,512]{1,0:T(8,128)(2,1)S(1)}, bf16[32,512]{1,0:T(8,128)(2,1)S(1)}, u32[]{:S(2)}, u32[]{:S(2)}) collective-permute-start(bf16[32,512]{1,0:T(8,128)(2,1)S(1)} %pad_maximum_fusion.11), channel_id=1, source_target_pairs={{0,4},{1,5},{2,6},{3,7},{4,0},{5,1},{6,2},{7,3},{8,12},{9,13},{10,... | collective-permute-start | bytes 98312 | tf_op jit(solution)/shard_map/ppermute | solution.py:80
  28.1 6.9 %collective-permute-start.10 = (bf16[128,512]{1,0:T(8,128)(2,1)S(1)}, bf16[128,512]{1,0:T(8,128)(2,1)S(1)}, u32[]{:S(2)}, u32[]{:S(2)}) collective-permute-start(bf16[128,512]{1,0:T(8,128)(2,1)S(1)} %copy-done.12), channel_id=1, source_target_pairs={{0,6},{1,7},{2,4},{3,5},{4,2},{5,3},{6,0},{7,1},{8,14},{9,15},{10,... | collective-permute-start | bytes 393224 | tf_op jit(solution)/shard_map/ppermute | solution.py:80
  30.6 7.8 %collective-permute-start.11 = (bf16[128,512]{1,0:T(8,128)(2,1)S(1)}, bf16[128,512]{1,0:T(8,128)(2,1)S(1)}, u32[]{:S(2)}, u32[]{:S(2)}) collective-permute-start(bf16[128,512]{1,0:T(8,128)(2,1)S(1)} %copy-done.11), channel_id=1, source_target_pairs={{0,7},{1,6},{2,5},{3,4},{4,3},{5,2},{6,1},{7,0},{8,15},{9,14},{10,... | collective-permute-start | bytes 393224 | tf_op jit(solution)/shard_map/ppermute | solution.py:80
  32.3 6.1 %copy-start.7 = (s32[3,6]{1,0:T(4,128)S(1)}, s32[3,6]{1,0:T(4,128)}, u32[]{:S(2)}) copy-start(s32[3,6]{1,0:T(4,128)} %tile_src.1) | copy-start | bytes 220
  32.3 6.1 %copy-start.8 = (bf16[128,512]{1,0:T(8,128)(2,1)S(1)}, bf16[128,512]{1,0:T(8,128)(2,1)}, u32[]{:S(2)}) copy-start(bf16[128,512]{1,0:T(8,128)(2,1)} %get-tuple-element.64.rest_0_) | copy-start | bytes 393220
  42.0 2.4 %collective-permute-start.12 = (bf16[592,512]{1,0:T(8,128)(2,1)S(1)}, bf16[592,512]{1,0:T(8,128)(2,1)S(1)}, u32[]{:S(2)}, u32[]{:S(2)}) collective-permute-start(bf16[592,512]{1,0:T(8,128)(2,1)S(1)} %get-tuple-element.71), channel_id=1, source_target_pairs={{0,8},{1,9},{2,10},{3,11},{4,12},{5,13},{6,14},{7,15},{8,0},{9,1},... | collective-permute-start | bytes 1818632 | tf_op jit(solution)/shard_map/ppermute | solution.py:80
  42.1 13.6 %collective-permute-start.22 = (bf16[256,512]{1,0:T(8,128)(2,1)S(1)}, bf16[256,512]{1,0:T(8,128)(2,1)S(1)}, u32[]{:S(2)}, u32[]{:S(2)}) collective-permute-start(bf16[256,512]{1,0:T(8,128)(2,1)S(1)} %get-tuple-element.82), channel_id=1, source_target_pairs={{0,2},{1,3},{2,0},{3,1},{4,6},{5,7},{6,4},{7,5},{8,10},{9,11},{10,... | collective-permute-start | bytes 786440 | tf_op jit(solution)/shard_map/ppermute | solution.py:80
  43.9 14.9 %collective-permute-start.23 = (bf16[256,512]{1,0:T(8,128)(2,1)S(1)}, bf16[256,512]{1,0:T(8,128)(2,1)S(1)}, u32[]{:S(2)}, u32[]{:S(2)}) collective-permute-start(bf16[256,512]{1,0:T(8,128)(2,1)S(1)} %get-tuple-element.83), channel_id=1, source_target_pairs={{0,4},{1,5},{2,6},{3,7},{4,0},{5,1},{6,2},{7,3},{8,12},{9,13},{10,... | collective-permute-start | bytes 786440 | tf_op jit(solution)/shard_map/ppermute | solution.py:80
  44.7 14.1 %collective-permute-start.15 = (bf16[152,512]{1,0:T(8,128)(2,1)S(1)}, bf16[152,512]{1,0:T(8,128)(2,1)S(1)}, u32[]{:S(2)}, u32[]{:S(2)}) collective-permute-start(bf16[152,512]{1,0:T(8,128)(2,1)S(1)} %pad_maximum_fusion.5), channel_id=1, source_target_pairs={{0,17},{1,16},{2,19},{3,18},{4,21},{5,20},{6,23},{7,22},{8,25},{9,... | collective-permute-start | bytes 466952 | tf_op jit(solution)/shard_map/ppermute | solution.py:80
  47.2 11.7 %collective-permute-start.13 = (bf16[152,512]{1,0:T(8,128)(2,1)S(1)}, bf16[152,512]{1,0:T(8,128)(2,1)S(1)}, u32[]{:S(2)}, u32[]{:S(2)}) collective-permute-start(bf16[152,512]{1,0:T(8,128)(2,1)S(1)} %get-tuple-element.115), channel_id=1, source_target_pairs={{0,1},{1,0},{2,3},{3,2},{4,5},{5,4},{6,7},{7,6},{8,9},{9,8},{10,11... | collective-permute-start | bytes 466952 | tf_op jit(solution)/shard_map/ppermute | solution.py:80
  47.8 11.1 %collective-permute-start.14 = (bf16[152,512]{1,0:T(8,128)(2,1)S(1)}, bf16[152,512]{1,0:T(8,128)(2,1)S(1)}, u32[]{:S(2)}, u32[]{:S(2)}) collective-permute-start(bf16[152,512]{1,0:T(8,128)(2,1)S(1)} %get-tuple-element.116), channel_id=1, source_target_pairs={{0,16},{1,17},{2,18},{3,19},{4,20},{5,21},{6,22},{7,23},{8,24},{9,... | collective-permute-start | bytes 466952 | tf_op jit(solution)/shard_map/ppermute | solution.py:80
  59.2 6.9 %collective-permute-start.16 = (bf16[44,512]{1,0:T(8,128)(2,1)S(1)}, bf16[44,512]{1,0:T(8,128)(2,1)S(1)}, u32[]{:S(2)}, u32[]{:S(2)}) collective-permute-start(bf16[44,512]{1,0:T(8,128)(2,1)S(1)} %get-tuple-element.112), channel_id=1, source_target_pairs={{0,4},{1,5},{2,6},{3,7},{4,0},{5,1},{6,2},{7,3},{8,12},{9,13},{10,... | collective-permute-start | bytes 135176 | tf_op jit(solution)/shard_map/ppermute | solution.py:80
  59.6 6.5 %collective-permute-start.17 = (bf16[44,512]{1,0:T(8,128)(2,1)S(1)}, bf16[44,512]{1,0:T(8,128)(2,1)S(1)}, u32[]{:S(2)}, u32[]{:S(2)}) collective-permute-start(bf16[44,512]{1,0:T(8,128)(2,1)S(1)} %get-tuple-element.113), channel_id=1, source_target_pairs={{0,2},{1,3},{2,0},{3,1},{4,6},{5,7},{6,4},{7,5},{8,10},{9,11},{10,... | collective-permute-start | bytes 135176 | tf_op jit(solution)/shard_map/ppermute | solution.py:80
  61.7 6.0 %collective-permute-start.18 = (bf16[44,512]{1,0:T(8,128)(2,1)S(1)}, bf16[44,512]{1,0:T(8,128)(2,1)S(1)}, u32[]{:S(2)}, u32[]{:S(2)}) collective-permute-start(bf16[44,512]{1,0:T(8,128)(2,1)S(1)} %get-tuple-element.114), channel_id=1, source_target_pairs={{0,6},{1,7},{2,4},{3,5},{4,2},{5,3},{6,0},{7,1},{8,14},{9,15},{10,... | collective-permute-start | bytes 135176 | tf_op jit(solution)/shard_map/ppermute | solution.py:80
  63.7 19.0 %copy-start.4 = (s32[8,128]{1,0:T(8,128)S(1)}, s32[8,128]{1,0:T(8,128)}, u32[]{:S(2)}) copy-start(s32[8,128]{1,0:T(8,128)} %rows_ref.5) | copy-start | bytes 12292
  63.7 19.0 %copy-start.5 = (s32[1,8]{1,0:T(1,128)S(1)}, s32[1,8]{1,0:T(1,128)}, u32[]{:S(2)}) copy-start(s32[1,8]{1,0:T(1,128)} %count_ref.5) | copy-start | bytes 100
  63.7 10.8 %collective-permute-start.24 = (bf16[384,512]{1,0:T(8,128)(2,1)S(1)}, bf16[384,512]{1,0:T(8,128)(2,1)S(1)}, u32[]{:S(2)}, u32[]{:S(2)}) collective-permute-start(bf16[384,512]{1,0:T(8,128)(2,1)S(1)} %pad_maximum_fusion.2), channel_id=1, source_target_pairs={{0,1},{1,0},{2,3},{3,2},{4,5},{5,4},{6,7},{7,6},{8,9},{9,8},{10,11... | collective-permute-start | bytes 1179656 | tf_op jit(solution)/shard_map/ppermute | solution.py:80
  67.8 5.8 %collective-permute-start.21 = (bf16[32,512]{1,0:T(8,128)(2,1)S(1)}, bf16[32,512]{1,0:T(8,128)(2,1)S(1)}, u32[]{:S(2)}, u32[]{:S(2)}) collective-permute-start(bf16[32,512]{1,0:T(8,128)(2,1)S(1)} %fusion), channel_id=1, source_target_pairs={{0,6},{1,7},{2,4},{3,5},{4,2},{5,3},{6,0},{7,1},{8,14},{9,15},{10,... | collective-permute-start | bytes 98312 | tf_op jit(solution)/shard_map/ppermute | solution.py:80
  69.7 4.2 %collective-permute-start.20 = (bf16[32,512]{1,0:T(8,128)(2,1)S(1)}, bf16[32,512]{1,0:T(8,128)(2,1)S(1)}, u32[]{:S(2)}, u32[]{:S(2)}) collective-permute-start(bf16[32,512]{1,0:T(8,128)(2,1)S(1)} %fusion), channel_id=1, source_target_pairs={{0,2},{1,3},{2,0},{3,1},{4,6},{5,7},{6,4},{7,5},{8,10},{9,11},{10,... | collective-permute-start | bytes 98312 | tf_op jit(solution)/shard_map/ppermute | solution.py:80
  69.7 4.8 %collective-permute-start.19 = (bf16[32,512]{1,0:T(8,128)(2,1)S(1)}, bf16[32,512]{1,0:T(8,128)(2,1)S(1)}, u32[]{:S(2)}, u32[]{:S(2)}) collective-permute-start(bf16[32,512]{1,0:T(8,128)(2,1)S(1)} %fusion), channel_id=1, source_target_pairs={{0,4},{1,5},{2,6},{3,7},{4,0},{5,1},{6,2},{7,3},{8,12},{9,13},{10,... | collective-permute-start | bytes 98312 | tf_op jit(solution)/shard_map/ppermute | solution.py:80
  74.6 9.4 %collective-permute-start.27 = (bf16[128,512]{1,0:T(8,128)(2,1)S(1)}, bf16[128,512]{1,0:T(8,128)(2,1)S(1)}, u32[]{:S(2)}, u32[]{:S(2)}) collective-permute-start(bf16[128,512]{1,0:T(8,128)(2,1)S(1)} %pad_maximum_fusion.7), channel_id=1, source_target_pairs={{0,17},{1,16},{2,19},{3,18},{4,21},{5,20},{6,23},{7,22},{8,25},{9,... | collective-permute-start | bytes 393224 | tf_op jit(solution)/shard_map/ppermute | solution.py:80
  76.9 7.1 %collective-permute-start.26 = (bf16[128,512]{1,0:T(8,128)(2,1)S(1)}, bf16[128,512]{1,0:T(8,128)(2,1)S(1)}, u32[]{:S(2)}, u32[]{:S(2)}) collective-permute-start(bf16[128,512]{1,0:T(8,128)(2,1)S(1)} %pad_maximum_fusion.7), channel_id=1, source_target_pairs={{0,16},{1,17},{2,18},{3,19},{4,20},{5,21},{6,22},{7,23},{8,24},{9,... | collective-permute-start | bytes 393224 | tf_op jit(solution)/shard_map/ppermute | solution.py:80
  77.4 6.6 %collective-permute-start.25 = (bf16[128,512]{1,0:T(8,128)(2,1)S(1)}, bf16[128,512]{1,0:T(8,128)(2,1)S(1)}, u32[]{:S(2)}, u32[]{:S(2)}) collective-permute-start(bf16[128,512]{1,0:T(8,128)(2,1)S(1)} %pad_maximum_fusion.7), channel_id=1, source_target_pairs={{0,1},{1,0},{2,3},{3,2},{4,5},{5,4},{6,7},{7,6},{8,9},{9,8},{10,11... | collective-permute-start | bytes 393224 | tf_op jit(solution)/shard_map/ppermute | solution.py:80
  78.1 6.9 %collective-permute-start.28 = (bf16[128,512]{1,0:T(8,128)(2,1)S(1)}, bf16[128,512]{1,0:T(8,128)(2,1)S(1)}, u32[]{:S(2)}, u32[]{:S(2)}) collective-permute-start(bf16[128,512]{1,0:T(8,128)(2,1)S(1)} %get-tuple-element.85), channel_id=1, source_target_pairs={{0,6},{1,7},{2,4},{3,5},{4,2},{5,3},{6,0},{7,1},{8,14},{9,15},{10,... | collective-permute-start | bytes 393224 | tf_op jit(solution)/shard_map/ppermute | solution.py:80
  80.0 7.8 %collective-permute-start.29 = (bf16[128,512]{1,0:T(8,128)(2,1)S(1)}, bf16[128,512]{1,0:T(8,128)(2,1)S(1)}, u32[]{:S(2)}, u32[]{:S(2)}) collective-permute-start(bf16[128,512]{1,0:T(8,128)(2,1)S(1)} %get-tuple-element.86), channel_id=1, source_target_pairs={{0,7},{1,6},{2,5},{3,4},{4,3},{5,2},{6,1},{7,0},{8,15},{9,14},{10,... | collective-permute-start | bytes 393224 | tf_op jit(solution)/shard_map/ppermute | solution.py:80
  82.7 5.2 %copy-start.6 = (s32[4]{0:T(128)S(1)}, s32[4]{0:T(128)}, u32[]{:S(2)}) copy-start(s32[4]{0:T(128)} %hub_ref.3) | copy-start | bytes 52
  87.8 1.9 %collective-permute-start.30 = (bf16[512,512]{1,0:T(8,128)(2,1)S(1)}, bf16[512,512]{1,0:T(8,128)(2,1)S(1)}, u32[]{:S(2)}, u32[]{:S(2)}) collective-permute-start(bf16[512,512]{1,0:T(8,128)(2,1)S(1)} %pad_maximum_fusion.x_ref), channel_id=1, source_target_pairs={{0,8},{1,9},{2,10},{3,11},{4,12},{5,13},{6,14},{7,15},{8,0},{9,1},... | collective-permute-start | bytes 1572872 | tf_op jit(solution)/shard_map/ppermute | solution.py:80

commit v5 on v4

--- a/solution.py
+++ b/solution.py
@@ -312,7 +312,8 @@
     ntiles = nblocks + n_inner + nhubs // tile
     groups = tree_groups(n_outer, n_inner)
     steps = sum(groups, [])
-    hub_steps = sum(groups[::-1], [])
+    hub_groups = groups[:-1] + [[step] for step in groups[-1]]
+    hub_steps = sum(hub_groups[::-1], [])
     wrows = 2 * width // ndevice
 
     def shape(*dims, dtype=BF):
@@ -334,9 +335,10 @@
     hubx = hub_own
     for group in groups[:-1]:
         hubx = spread(hubx, group)
-    hubx, pairs, far_a, far_b = lax.optimization_barrier((hubx, pairs, far_a, far_b))
+    hubx, pairs[0], far_a, far_b = lax.optimization_barrier((hubx, pairs[0], far_a, far_b))
     direct = [exchange(far_a, (0, n_inner - 2)), exchange(far_b, (0, n_inner - 1))]
-    hubx = spread(hubx, groups[-1])
+    for group in hub_groups[-2:]:
+        hubx = spread(hubx, group)
     received = [own_rows, *pairs, relay(pairs, one), *direct]
     feat_t, adj_cat, adj_t, neigh_low, neigh_t, cot_wide = pl.pallas_call(
         prepare_kernel,

time: 91.5 us -> 88.2 us (0.964)
  starting transfers between devices: 43.3 us -> 41.1 us
  other arithmetic: 3.37 us -> 2.4 us
    ppermute x31 -> x30, starting transfers between devices: 43.3 us -> 41.1 us  [exchange(): lax.ppermute(x, ('outer', 'inner'), [(s, s ^ mask) for s in range(n_outer...]
    concatenate x2, other arithmetic: 1.02 us -> 0.05 us  [relay(): jnp.concatenate([one] + [p[rows:] for p in pairs], 0)]
    ppermute x31 -> x30, waiting for transfers between devices: 31.7 us -> 31.7 us  [exchange(): lax.ppermute(x, ('outer', 'inner'), [(s, s ^ mask) for s in range(n_outer...]
  transfers between devices with their start and end apart: 31 -> 30, of which waited for: 17 -> 15; matrix products, arithmetic and copies ran while one was open for 4% -> 3% of each run, Pallas kernels for 4% -> 4%
where the time goes in v5:
time: 88.2 us; the launch traced here: 88.1 us
  starting transfers between devices  41.1 us (47%)
  waiting for transfers between devices  31.7 us (36%)
  Pallas kernels  11.2 us (13%)
  other arithmetic  2.4 us (3%)
  between operations  1.12 us (1%)
    ppermute x30, starting transfers between devices, exchange(): lax.ppermute(x, ('outer', 'inner'), [(s, s ^ mask) for s in range(n_outer...  41.1 us
    ppermute x30, waiting for transfers between devices, exchange(): lax.ppermute(x, ('outer', 'inner'), [(s, s ^ mask) for s in range(n_outer...  31.7 us
    pallas_call x1, Pallas kernels, body(): pl.pallas_call(functools.partial(middle_kernel, steps, hub_steps, n_inner...  3.64 us
    pallas_call x1, Pallas kernels, body(): pl.pallas_call(gather_kernel, out_shape=(shape(hd, width),) + sizes, in_s...  2.68 us
  transfers between devices with their start and end apart: 30, of which 15 were waited for; matrix products, arithmetic and copies ran while one was open for 3% of the time, Pallas kernels for 4%

profile of v5, /device:TPU:0, one launch (start us, length us, event | category | flops | bytes accessed | tf_op | source)
XLA Modules:
  0.0 88.1 jit_solution(6474849330430381280)
XLA Ops:
  0.6 2.7 %gather_rows.1 = (bf16[4,512]{1,0:T(4,128)(2,1)}, bf16[128,512]{1,0:T(8,128)(2,1)}, bf16[256,512]{1,0:T(8,128)(2,1)}, bf16[256,512]{1,0:T(8,128)(2,1)}, bf16[128...) custom-call(s32[4]{0:T(128)} %hub_ref.3, s32[1,8]{1,0:T(1,128)} %count_ref.5, ...), custom_call_target="tpu_custom_call" | custom-call | flops 400000000 | bytes 3000000 | tf_op jit(solution)/shard_map/gather_rows/pallas_call | solution.py:324
  3.3 3.1 %collective-permute-start.4 = (bf16[256,512]{1,0:T(8,128)(2,1)}, bf16[256,512]{1,0:T(8,128)(2,1)S(1)}, u32[]{:S(2)}, u32[]{:S(2)}) collective-permute-start(bf16[256,512]{1,0:T(8,128)(2,1)} %get-tuple-element.53), channel_id=1, source_target_pairs={{0,2},{1,3},{2,0},{3,1},{4,6},{5,7},{6,4},{7,5},{8,10},{9,11},{10,... | collective-permute-start | bytes 786440 | tf_op jit(solution)/shard_map/ppermute | solution.py:80
  6.4 2.6 %collective-permute-start.7 = (bf16[256,512]{1,0:T(8,128)(2,1)}, bf16[256,512]{1,0:T(8,128)(2,1)S(1)}, u32[]{:S(2)}, u32[]{:S(2)}) collective-permute-start(bf16[256,512]{1,0:T(8,128)(2,1)} %get-tuple-element.64), channel_id=1, source_target_pairs={{0,4},{1,5},{2,6},{3,7},{4,0},{5,1},{6,2},{7,3},{8,12},{9,13},{10,... | collective-permute-start | bytes 786440 | tf_op jit(solution)/shard_map/ppermute | solution.py:80
  9.0 1.4 %collective-permute-done = bf16[4,512]{1,0:T(4,128)(2,1)S(1)} collective-permute-done((bf16[4,512]{1,0:T(4,128)(2,1)}, bf16[4,512]{1,0:T(4,128)(2,1)S(1)}, u32[]{:S(2)}, u32[]{:S(2)}) %collective-permute-start) | collective-permute-done | bytes 4128 | tf_op jit(solution)/shard_map/ppermute | solution.py:80
  10.4 0.7 pad_maximum_fusion.13
  11.1 0.0 copy-start.11
  11.1 2.5 %collective-permute-start.3 = (bf16[8,512]{1,0:T(8,128)(2,1)S(1)}, bf16[8,512]{1,0:T(8,128)(2,1)S(1)}, u32[]{:S(2)}, u32[]{:S(2)}) collective-permute-start(bf16[8,512]{1,0:T(8,128)(2,1)S(1)} %pad_maximum_fusion.13), channel_id=1, source_target_pairs={{0,17},{1,16},{2,19},{3,18},{4,21},{5,20},{6,23},{7,22},{8,25},{9,... | collective-permute-start | bytes 24584 | tf_op jit(solution)/shard_map/ppermute | solution.py:80
  13.6 0.5 collective-permute-start.2
  14.1 0.5 collective-permute-start.1
  14.7 0.1 convert_element_type.39.ws_ref
  14.7 1.0 %collective-permute-done.3 = bf16[8,512]{1,0:T(8,128)(2,1)S(1)} collective-permute-done((bf16[8,512]{1,0:T(8,128)(2,1)S(1)}, bf16[8,512]{1,0:T(8,128)(2,1)S(1)}, u32[]{:S(2)}, u32[]{:S(2)}) %collective-permute-start.3) | collective-permute-done | bytes 8224 | tf_op jit(solution)/shard_map/ppermute | solution.py:80
  15.7 1.5 %collective-permute-done.2 = bf16[8,512]{1,0:T(8,128)(2,1)S(1)} collective-permute-done((bf16[8,512]{1,0:T(8,128)(2,1)S(1)}, bf16[8,512]{1,0:T(8,128)(2,1)S(1)}, u32[]{:S(2)}, u32[]{:S(2)}) %collective-permute-start.2) | collective-permute-done | bytes 8224 | tf_op jit(solution)/shard_map/ppermute | solution.py:80
  17.3 0.5 collective-permute-done.1
  17.8 0.6 collective-permute-done.4.rest_1_
  18.4 0.0 collective-permute-start.5
  18.5 2.7 %collective-permute-start.9 = (bf16[128,512]{1,0:T(8,128)(2,1)S(1)}, bf16[128,512]{1,0:T(8,128)(2,1)S(1)}, u32[]{:S(2)}, u32[]{:S(2)}) collective-permute-start(bf16[128,512]{1,0:T(8,128)(2,1)S(1)} %copy-done.13), channel_id=1, source_target_pairs={{0,6},{1,7},{2,4},{3,5},{4,2},{5,3},{6,0},{7,1},{8,14},{9,15},{10,... | collective-permute-start | bytes 393224 | tf_op jit(solution)/shard_map/ppermute | solution.py:80
  21.2 2.3 %collective-permute-start.10 = (bf16[128,512]{1,0:T(8,128)(2,1)S(1)}, bf16[128,512]{1,0:T(8,128)(2,1)S(1)}, u32[]{:S(2)}, u32[]{:S(2)}) collective-permute-start(bf16[128,512]{1,0:T(8,128)(2,1)S(1)} %copy-done.12), channel_id=1, source_target_pairs={{0,7},{1,6},{2,5},{3,4},{4,3},{5,2},{6,1},{7,0},{8,15},{9,14},{10,... | collective-permute-start | bytes 393224 | tf_op jit(solution)/shard_map/ppermute | solution.py:80
  23.5 0.0 collective-permute-done.7.rest_2_
  23.5 0.0 copy-start.1
  23.5 0.0 copy-start.2
  23.5 0.0 copy-start.3
  23.6 0.4 collective-permute-start.8
  24.0 0.0 collective-permute-done.5
  24.0 1.5 %collective-permute-start.6 = (bf16[64,512]{1,0:T(8,128)(2,1)S(1)}, bf16[64,512]{1,0:T(8,128)(2,1)S(1)}, u32[]{:S(2)}, u32[]{:S(2)}) collective-permute-start(bf16[64,512]{1,0:T(8,128)(2,1)S(1)} %pad_maximum_fusion.11), channel_id=1, source_target_pairs={{0,4},{1,5},{2,6},{3,7},{4,0},{5,1},{6,2},{7,3},{8,12},{9,13},{10,... | collective-permute-start | bytes 196616 | tf_op jit(solution)/shard_map/ppermute | solution.py:80
  25.5 0.4 convolution_add_fusion.pre0
  25.9 0.0 copy-start.7
  25.9 0.0 copy-start.8
  25.9 0.5 prepare.1
  26.4 9.2 %collective-permute-done.6 = bf16[64,512]{1,0:T(8,128)(2,1)S(1)} collective-permute-done((bf16[64,512]{1,0:T(8,128)(2,1)S(1)}, bf16[64,512]{1,0:T(8,128)(2,1)S(1)}, u32[]{:S(2)}, u32[]{:S(2)}) %collective-permute-start.6) | collective-permute-done | bytes 65568 | tf_op jit(solution)/shard_map/ppermute | solution.py:80
  35.7 0.2 collective-permute-done.8.rest_3_
  35.9 3.6 %middle.1 = (f32[384,512]{1,0:T(8,128)S(1)}, bf16[384,512]{1,0:T(8,128)(2,1)S(1)}, f32[384,512]{1,0:T(8,128)S(1)}, bf16[592,512]{1,0:T(8,128)(2,1)S(1)}, bf16[59...) custom-call(s32[3,6]{1,0:T(4,128)S(1)} %copy-done.7, ...), custom_call_target="tpu_custom_call" | custom-call | flops 2000000000 | bytes 9000000 | tf_op jit(solution)/shard_map/middle/pallas_call | solution.py:390
  39.5 0.1 collective-permute-start.11
  39.6 0.5 collective-permute-start.21
  40.1 2.6 %collective-permute-start.22 = (bf16[256,512]{1,0:T(8,128)(2,1)S(1)}, bf16[256,512]{1,0:T(8,128)(2,1)S(1)}, u32[]{:S(2)}, u32[]{:S(2)}) collective-permute-start(bf16[256,512]{1,0:T(8,128)(2,1)S(1)} %get-tuple-element.81), channel_id=1, source_target_pairs={{0,4},{1,5},{2,6},{3,7},{4,0},{5,1},{6,2},{7,3},{8,12},{9,13},{10,... | collective-permute-start | bytes 786440 | tf_op jit(solution)/shard_map/ppermute | solution.py:80
  42.7 0.2 convert_add_fusion
  43.0 2.3 %collective-permute-start.14 = (bf16[152,512]{1,0:T(8,128)(2,1)S(1)}, bf16[152,512]{1,0:T(8,128)(2,1)S(1)}, u32[]{:S(2)}, u32[]{:S(2)}) collective-permute-start(bf16[152,512]{1,0:T(8,128)(2,1)S(1)} %pad_maximum_fusion.5), channel_id=1, source_target_pairs={{0,17},{1,16},{2,19},{3,18},{4,21},{5,20},{6,23},{7,22},{8,25},{9,... | collective-permute-start | bytes 466952 | tf_op jit(solution)/shard_map/ppermute | solution.py:80
  45.3 0.8 collective-permute-start.12
  46.1 0.5 collective-permute-start.13
  46.7 7.2 %collective-permute-done.21.rest_1_ = bf16[256,512]{1,0:T(8,128)(2,1)S(1)} collective-permute-done((bf16[256,512]{1,0:T(8,128)(2,1)S(1)}, bf16[256,512]{1,0:T(8,128)(2,1)S(1)}, u32[]{:S(2)}, u32[]{:S(2)}) %collective-permute-start.21) | collective-permute-done | bytes 262176 | tf_op jit(solution)/shard_map/ppermute | solution.py:80
  53.9 1.1 %collective-permute-done.22.rest_2_ = bf16[256,512]{1,0:T(8,128)(2,1)S(1)} collective-permute-done((bf16[256,512]{1,0:T(8,128)(2,1)S(1)}, bf16[256,512]{1,0:T(8,128)(2,1)S(1)}, u32[]{:S(2)}, u32[]{:S(2)}) %collective-permute-start.22) | collective-permute-done | bytes 262176 | tf_op jit(solution)/shard_map/ppermute | solution.py:80
  55.2 0.1 slice_add_fusion
  55.4 0.4 collective-permute-start.15
  55.8 2.8 %collective-permute-start.16 = (bf16[44,512]{1,0:T(8,128)(2,1)S(1)}, bf16[44,512]{1,0:T(8,128)(2,1)S(1)}, u32[]{:S(2)}, u32[]{:S(2)}) collective-permute-start(bf16[44,512]{1,0:T(8,128)(2,1)S(1)} %get-tuple-element.111), channel_id=1, source_target_pairs={{0,2},{1,3},{2,0},{3,1},{4,6},{5,7},{6,4},{7,5},{8,10},{9,11},{10,... | collective-permute-start | bytes 135176 | tf_op jit(solution)/shard_map/ppermute | solution.py:80
  58.6 1.3 %collective-permute-start.17 = (bf16[44,512]{1,0:T(8,128)(2,1)S(1)}, bf16[44,512]{1,0:T(8,128)(2,1)S(1)}, u32[]{:S(2)}, u32[]{:S(2)}) collective-permute-start(bf16[44,512]{1,0:T(8,128)(2,1)S(1)} %get-tuple-element.112), channel_id=1, source_target_pairs={{0,6},{1,7},{2,4},{3,5},{4,2},{5,3},{6,0},{7,1},{8,14},{9,15},{10,... | collective-permute-start | bytes 135176 | tf_op jit(solution)/shard_map/ppermute | solution.py:80
  59.9 0.0 copy-start.4
  59.9 0.0 copy-start.5
  59.9 1.3 %collective-permute-start.23 = (bf16[384,512]{1,0:T(8,128)(2,1)S(1)}, bf16[384,512]{1,0:T(8,128)(2,1)S(1)}, u32[]{:S(2)}, u32[]{:S(2)}) collective-permute-start(bf16[384,512]{1,0:T(8,128)(2,1)S(1)} %pad_maximum_fusion.2), channel_id=1, source_target_pairs={{0,1},{1,0},{2,3},{3,2},{4,5},{5,4},{6,7},{7,6},{8,9},{9,8},{10,11... | collective-permute-start | bytes 1179656 | tf_op jit(solution)/shard_map/ppermute | solution.py:80
  61.2 1.0 %multiply_convert_fusion = bf16[384,512]{1,0:T(8,128)(2,1)} fusion(f32[384,512]{1,0:T(8,128)S(1)} %get-tuple-element.74), kind=kLoop, calls=%fused_computation.2 | loop fusion | flops 983040 | bytes 1179648 | tf_op jit(solution)/shard_map/convert_element_type | solution.py:400
  62.2 2.3 %collective-permute-done.17 = bf16[44,512]{1,0:T(8,128)(2,1)S(1)} collective-permute-done((bf16[44,512]{1,0:T(8,128)(2,1)S(1)}, bf16[44,512]{1,0:T(8,128)(2,1)S(1)}, u32[]{:S(2)}, u32[]{:S(2)}) %collective-permute-start.17) | collective-permute-done | bytes 45088 | tf_op jit(solution)/shard_map/ppermute | solution.py:80
  64.5 1.4 %collective-permute-start.20 = (bf16[32,512]{1,0:T(8,128)(2,1)S(1)}, bf16[32,512]{1,0:T(8,128)(2,1)S(1)}, u32[]{:S(2)}, u32[]{:S(2)}) collective-permute-start(bf16[32,512]{1,0:T(8,128)(2,1)S(1)} %fusion), channel_id=1, source_target_pairs={{0,6},{1,7},{2,4},{3,5},{4,2},{5,3},{6,0},{7,1},{8,14},{9,15},{10,... | collective-permute-start | bytes 98312 | tf_op jit(solution)/shard_map/ppermute | solution.py:80
  66.0 3.0 %collective-permute-start.18 = (bf16[32,512]{1,0:T(8,128)(2,1)S(1)}, bf16[32,512]{1,0:T(8,128)(2,1)S(1)}, u32[]{:S(2)}, u32[]{:S(2)}) collective-permute-start(bf16[32,512]{1,0:T(8,128)(2,1)S(1)} %fusion), channel_id=1, source_target_pairs={{0,4},{1,5},{2,6},{3,7},{4,0},{5,1},{6,2},{7,3},{8,12},{9,13},{10,... | collective-permute-start | bytes 98312 | tf_op jit(solution)/shard_map/ppermute | solution.py:80
  69.0 1.3 %collective-permute-done.20 = bf16[32,512]{1,0:T(8,128)(2,1)S(1)} collective-permute-done((bf16[32,512]{1,0:T(8,128)(2,1)S(1)}, bf16[32,512]{1,0:T(8,128)(2,1)S(1)}, u32[]{:S(2)}, u32[]{:S(2)}) %collective-permute-start.20) | collective-permute-done | bytes 32800 | tf_op jit(solution)/shard_map/ppermute | solution.py:80
  70.3 0.6 collective-permute-done.18
  70.9 2.1 %collective-permute-start.26 = (bf16[128,512]{1,0:T(8,128)(2,1)S(1)}, bf16[128,512]{1,0:T(8,128)(2,1)S(1)}, u32[]{:S(2)}, u32[]{:S(2)}) collective-permute-start(bf16[128,512]{1,0:T(8,128)(2,1)S(1)} %pad_maximum_fusion.7), channel_id=1, source_target_pairs={{0,17},{1,16},{2,19},{3,18},{4,21},{5,20},{6,23},{7,22},{8,25},{9,... | collective-permute-start | bytes 393224 | tf_op jit(solution)/shard_map/ppermute | solution.py:80
  73.0 0.5 collective-permute-start.25
  73.6 0.9 collective-permute-start.24
  74.5 2.4 %collective-permute-start.27 = (bf16[128,512]{1,0:T(8,128)(2,1)S(1)}, bf16[128,512]{1,0:T(8,128)(2,1)S(1)}, u32[]{:S(2)}, u32[]{:S(2)}) collective-permute-start(bf16[128,512]{1,0:T(8,128)(2,1)S(1)} %get-tuple-element.83), channel_id=1, source_target_pairs={{0,6},{1,7},{2,4},{3,5},{4,2},{5,3},{6,0},{7,1},{8,14},{9,15},{10,... | collective-permute-start | bytes 393224 | tf_op jit(solution)/shard_map/ppermute | solution.py:80
  76.8 2.0 %collective-permute-start.28 = (bf16[128,512]{1,0:T(8,128)(2,1)S(1)}, bf16[128,512]{1,0:T(8,128)(2,1)S(1)}, u32[]{:S(2)}, u32[]{:S(2)}) collective-permute-start(bf16[128,512]{1,0:T(8,128)(2,1)S(1)} %get-tuple-element.84), channel_id=1, source_target_pairs={{0,7},{1,6},{2,5},{3,4},{4,3},{5,2},{6,1},{7,0},{8,15},{9,14},{10,... | collective-permute-start | bytes 393224 | tf_op jit(solution)/shard_map/ppermute | solution.py:80
  78.9 1.2 %scatter_first.1.own_ref = f32[384,512]{1,0:T(8,128)S(1)} custom-call(s32[1,8]{1,0:T(1,128)S(1)} %copy-done.5, s32[8,128]{1,0:T(8,128)S(1)} %copy-done.4, f32[384,512]{1,0:T(8,128)S(1)} %get-tuple-element.86.gown_ref, bf16[384,512]{1,0:T(8,128)(2,1)S(1)} %get-tuple-element.87.gp_ref, bf16[512,512]{1,0:T(8,128)(2,1)S(1)} %convert_element_type.39.ws_ref, ...), custom_call_target="tpu_custom_call" | custom-call | flops 400000000 | bytes 3000000 | tf_op jit(solution)/shard_map/scatter_first/pallas_call | solution.py:437
  80.2 1.1 %collective-permute-done.27.rest_0_ = bf16[128,512]{1,0:T(8,128)(2,1)S(1)} collective-permute-done((bf16[128,512]{1,0:T(8,128)(2,1)S(1)}, bf16[128,512]{1,0:T(8,128)(2,1)S(1)}, u32[]{:S(2)}, u32[]{:S(2)}) %collective-permute-start.27) | collective-permute-done | bytes 131104 | tf_op jit(solution)/shard_map/ppermute | solution.py:80
  81.3 3.3 %collective-permute-done.28.rest_1_ = bf16[128,512]{1,0:T(8,128)(2,1)S(1)} collective-permute-done((bf16[128,512]{1,0:T(8,128)(2,1)S(1)}, bf16[128,512]{1,0:T(8,128)(2,1)S(1)}, u32[]{:S(2)}, u32[]{:S(2)}) %collective-permute-start.28) | collective-permute-done | bytes 131104 | tf_op jit(solution)/shard_map/ppermute | solution.py:80
  84.6 1.6 %scatter_last.1 = bf16[384,512]{1,0:T(8,128)(2,1)} custom-call(s32[4]{0:T(128)S(1)} %copy-done.6, s32[1,8]{1,0:T(1,128)S(1)} %copy-done.5, s32[8,128]{1,0:T(8,128)S(1)} %copy-done.4, f32[384,512]{1,0:T(8,128)S(1)} %scatter_first.1.own_ref, f32[4,512]{1,0:T(4,128)S(1)} %slice_add_fusion.15.hub_grad_ref, bf16[128,512]{1,0:T(8,128)(2,1)S(1)} %collective-permute-done.27.rest_0_, ...), custom_call_target="tpu_custom_call" | custom-call | flops 200000000 | bytes 2000000 | tf_op jit(solution)/shard_map/scatter_last/pallas_call | solution.py:448
  86.2 0.3 collective-permute-done.29.y_ref
  86.5 1.6 %finish.1 = (f32[512,512]{1,0:T(8,128)}, f32[512,512]{1,0:T(8,128)}, f32[1,512]{1,0:T(1,128)}) custom-call(bf16[512,512]{1,0:T(8,128)(2,1)S(1)} %pad_maximum_fusion.x_ref, bf16[512,512]{1,0:T(8,128)(2,1)S(1)} %collective-permute-done.29.y_ref, f32[8,512]{1,0:T(8,128)S(1)} %slice_add_fusion.9.bias_in), custom_call_target="tpu_custom_call" | custom-call | flops 1000000 | bytes 3000000 | tf_op jit(solution)/shard_map/finish/pallas_call | solution.py:459
  (70 shorter events, 0.5 us)
Async XLA Ops:
  0.6 14.0 %copy-start.9 = (f32[512,512]{1,0:T(8,128)S(1)}, f32[512,512]{1,0:T(8,128)}, u32[]{:S(2)}) copy-start(f32[512,512]{1,0:T(8,128)} %param.16) | copy-start | bytes 3145732
  3.3 15.1 %copy-start.13 = (bf16[128,512]{1,0:T(8,128)(2,1)S(1)}, bf16[128,512]{1,0:T(8,128)(2,1)}, u32[]{:S(2)}) copy-start(bf16[128,512]{1,0:T(8,128)(2,1)} %get-tuple-element.66) | copy-start | bytes 393220
  3.3 17.9 %copy-start.12 = (bf16[128,512]{1,0:T(8,128)(2,1)S(1)}, bf16[128,512]{1,0:T(8,128)(2,1)}, u32[]{:S(2)}) copy-start(bf16[128,512]{1,0:T(8,128)(2,1)} %get-tuple-element.67) | copy-start | bytes 393220
  3.3 20.2 %copy-start.10 = (bf16[128,512]{1,0:T(8,128)(2,1)S(1)}, bf16[128,512]{1,0:T(8,128)(2,1)}, u32[]{:S(2)}) copy-start(bf16[128,512]{1,0:T(8,128)(2,1)} %get-tuple-element.65) | copy-start | bytes 393220
  3.3 15.1 %collective-permute-start.4 = (bf16[256,512]{1,0:T(8,128)(2,1)}, bf16[256,512]{1,0:T(8,128)(2,1)S(1)}, u32[]{:S(2)}, u32[]{:S(2)}) collective-permute-start(bf16[256,512]{1,0:T(8,128)(2,1)} %get-tuple-element.53), channel_id=1, source_target_pairs={{0,2},{1,3},{2,0},{3,1},{4,6},{5,7},{6,4},{7,5},{8,10},{9,11},{10,... | collective-permute-start | bytes 786440 | tf_op jit(solution)/shard_map/ppermute | solution.py:80
  6.4 17.1 %collective-permute-start.7 = (bf16[256,512]{1,0:T(8,128)(2,1)}, bf16[256,512]{1,0:T(8,128)(2,1)S(1)}, u32[]{:S(2)}, u32[]{:S(2)}) collective-permute-start(bf16[256,512]{1,0:T(8,128)(2,1)} %get-tuple-element.64), channel_id=1, source_target_pairs={{0,4},{1,5},{2,6},{3,7},{4,0},{5,1},{6,2},{7,3},{8,12},{9,13},{10,... | collective-permute-start | bytes 786440 | tf_op jit(solution)/shard_map/ppermute | solution.py:80
  9.0 1.4 %collective-permute-start = (bf16[4,512]{1,0:T(4,128)(2,1)}, bf16[4,512]{1,0:T(4,128)(2,1)S(1)}, u32[]{:S(2)}, u32[]{:S(2)}) collective-permute-start(bf16[4,512]{1,0:T(4,128)(2,1)} %get-tuple-element.52), channel_id=1, source_target_pairs={{0,8},{1,9},{2,10},{3,11},{4,12},{5,13},{6,14},{7,15},{8,0},{9,1},... | collective-permute-start | bytes 12296 | tf_op jit(solution)/shard_map/ppermute | solution.py:80
  11.1 14.4 %copy-start = (bf16[384,512]{1,0:T(8,128)(2,1)S(1)}, bf16[384,512]{1,0:T(8,128)(2,1)}, u32[]{:S(2)}) copy-start(bf16[384,512]{1,0:T(8,128)(2,1)} %feat_ref.3) | copy-start | bytes 1179652
  11.1 14.4 %copy-start.11 = (f32[512]{0:T(512)S(1)}, f32[512]{0:T(512)}, u32[]{:S(2)}) copy-start(f32[512]{0:T(512)} %param.18) | copy-start | bytes 6148
  11.1 4.6 %collective-permute-start.3 = (bf16[8,512]{1,0:T(8,128)(2,1)S(1)}, bf16[8,512]{1,0:T(8,128)(2,1)S(1)}, u32[]{:S(2)}, u32[]{:S(2)}) collective-permute-start(bf16[8,512]{1,0:T(8,128)(2,1)S(1)} %pad_maximum_fusion.13), channel_id=1, source_target_pairs={{0,17},{1,16},{2,19},{3,18},{4,21},{5,20},{6,23},{7,22},{8,25},{9,... | collective-permute-start | bytes 24584 | tf_op jit(solution)/shard_map/ppermute | solution.py:80
  13.6 3.7 %collective-permute-start.2 = (bf16[8,512]{1,0:T(8,128)(2,1)S(1)}, bf16[8,512]{1,0:T(8,128)(2,1)S(1)}, u32[]{:S(2)}, u32[]{:S(2)}) collective-permute-start(bf16[8,512]{1,0:T(8,128)(2,1)S(1)} %pad_maximum_fusion.13), channel_id=1, source_target_pairs={{0,16},{1,17},{2,18},{3,19},{4,20},{5,21},{6,22},{7,23},{8,24},{9,... | collective-permute-start | bytes 24584 | tf_op jit(solution)/shard_map/ppermute | solution.py:80
  14.1 3.7 %collective-permute-start.1 = (bf16[8,512]{1,0:T(8,128)(2,1)S(1)}, bf16[8,512]{1,0:T(8,128)(2,1)S(1)}, u32[]{:S(2)}, u32[]{:S(2)}) collective-permute-start(bf16[8,512]{1,0:T(8,128)(2,1)S(1)} %pad_maximum_fusion.13), channel_id=1, source_target_pairs={{0,1},{1,0},{2,3},{3,2},{4,5},{5,4},{6,7},{7,6},{8,9},{9,8},{10,11... | collective-permute-start | bytes 24584 | tf_op jit(solution)/shard_map/ppermute | solution.py:80
  18.4 5.5 %collective-permute-start.5 = (bf16[32,512]{1,0:T(8,128)(2,1)S(1)}, bf16[32,512]{1,0:T(8,128)(2,1)S(1)}, u32[]{:S(2)}, u32[]{:S(2)}) collective-permute-start(bf16[32,512]{1,0:T(8,128)(2,1)S(1)} %pad_maximum_fusion.12), channel_id=1, source_target_pairs={{0,2},{1,3},{2,0},{3,1},{4,6},{5,7},{6,4},{7,5},{8,10},{9,11},{10,... | collective-permute-start | bytes 98312 | tf_op jit(solution)/shard_map/ppermute | solution.py:80
  18.5 17.2 %collective-permute-start.9 = (bf16[128,512]{1,0:T(8,128)(2,1)S(1)}, bf16[128,512]{1,0:T(8,128)(2,1)S(1)}, u32[]{:S(2)}, u32[]{:S(2)}) collective-permute-start(bf16[128,512]{1,0:T(8,128)(2,1)S(1)} %copy-done.13), channel_id=1, source_target_pairs={{0,6},{1,7},{2,4},{3,5},{4,2},{5,3},{6,0},{7,1},{8,14},{9,15},{10,... | collective-permute-start | bytes 393224 | tf_op jit(solution)/shard_map/ppermute | solution.py:80
  21.2 14.5 %collective-permute-start.10 = (bf16[128,512]{1,0:T(8,128)(2,1)S(1)}, bf16[128,512]{1,0:T(8,128)(2,1)S(1)}, u32[]{:S(2)}, u32[]{:S(2)}) collective-permute-start(bf16[128,512]{1,0:T(8,128)(2,1)S(1)} %copy-done.12), channel_id=1, source_target_pairs={{0,7},{1,6},{2,5},{3,4},{4,3},{5,2},{6,1},{7,0},{8,15},{9,14},{10,... | collective-permute-start | bytes 393224 | tf_op jit(solution)/shard_map/ppermute | solution.py:80
  23.5 2.3 %copy-start.1 = (f32[512,512]{1,0:T(8,128)S(1)}, f32[512,512]{1,0:T(8,128)}, u32[]{:S(2)}) copy-start(f32[512,512]{1,0:T(8,128)} %wn_ref.1) | copy-start | bytes 3145732
  23.5 2.3 %copy-start.2 = (bf16[18,128,128]{2,1,0:T(8,128)(2,1)S(1)}, bf16[18,128,128]{2,1,0:T(8,128)(2,1)}, u32[]{:S(2)}) copy-start(bf16[18,128,128]{2,1,0:T(8,128)(2,1)} %adj_ref.1) | copy-start | bytes 1769476
  23.5 2.3 %copy-start.3 = (bf16[384,512]{1,0:T(8,128)(2,1)S(1)}, bf16[384,512]{1,0:T(8,128)(2,1)}, u32[]{:S(2)}) copy-start(bf16[384,512]{1,0:T(8,128)(2,1)} %cot_ref.1) | copy-start | bytes 1179652
  23.6 12.3 %collective-permute-start.8 = (bf16[384,512]{1,0:T(8,128)(2,1)S(1)}, bf16[384,512]{1,0:T(8,128)(2,1)S(1)}, u32[]{:S(2)}, u32[]{:S(2)}) collective-permute-start(bf16[384,512]{1,0:T(8,128)(2,1)S(1)} %pad_maximum_fusion.1), channel_id=1, source_target_pairs={{0,1},{1,0},{2,3},{3,2},{4,5},{5,4},{6,7},{7,6},{8,9},{9,8},{10,11... | collective-permute-start | bytes 1179656 | tf_op jit(solution)/shard_map/ppermute | solution.py:80
  24.0 11.6 %collective-permute-start.6 = (bf16[64,512]{1,0:T(8,128)(2,1)S(1)}, bf16[64,512]{1,0:T(8,128)(2,1)S(1)}, u32[]{:S(2)}, u32[]{:S(2)}) collective-permute-start(bf16[64,512]{1,0:T(8,128)(2,1)S(1)} %pad_maximum_fusion.11), channel_id=1, source_target_pairs={{0,4},{1,5},{2,6},{3,7},{4,0},{5,1},{6,2},{7,3},{8,12},{9,13},{10,... | collective-permute-start | bytes 196616 | tf_op jit(solution)/shard_map/ppermute | solution.py:80
  25.9 10.0 %copy-start.7 = (s32[3,6]{1,0:T(4,128)S(1)}, s32[3,6]{1,0:T(4,128)}, u32[]{:S(2)}) copy-start(s32[3,6]{1,0:T(4,128)} %tile_src.1) | copy-start | bytes 220
  25.9 10.0 %copy-start.8 = (bf16[128,512]{1,0:T(8,128)(2,1)S(1)}, bf16[128,512]{1,0:T(8,128)(2,1)}, u32[]{:S(2)}) copy-start(bf16[128,512]{1,0:T(8,128)(2,1)} %get-tuple-element.62.rest_0_) | copy-start | bytes 393220
  39.5 3.2 %collective-permute-start.11 = (bf16[592,512]{1,0:T(8,128)(2,1)S(1)}, bf16[592,512]{1,0:T(8,128)(2,1)S(1)}, u32[]{:S(2)}, u32[]{:S(2)}) collective-permute-start(bf16[592,512]{1,0:T(8,128)(2,1)S(1)} %get-tuple-element.69), channel_id=1, source_target_pairs={{0,8},{1,9},{2,10},{3,11},{4,12},{5,13},{6,14},{7,15},{8,0},{9,1},... | collective-permute-start | bytes 1818632 | tf_op jit(solution)/shard_map/ppermute | solution.py:80
  39.6 14.3 %collective-permute-start.21 = (bf16[256,512]{1,0:T(8,128)(2,1)S(1)}, bf16[256,512]{1,0:T(8,128)(2,1)S(1)}, u32[]{:S(2)}, u32[]{:S(2)}) collective-permute-start(bf16[256,512]{1,0:T(8,128)(2,1)S(1)} %get-tuple-element.80), channel_id=1, source_target_pairs={{0,2},{1,3},{2,0},{3,1},{4,6},{5,7},{6,4},{7,5},{8,10},{9,11},{10,... | collective-permute-start | bytes 786440 | tf_op jit(solution)/shard_map/ppermute | solution.py:80
  40.1 14.9 %collective-permute-start.22 = (bf16[256,512]{1,0:T(8,128)(2,1)S(1)}, bf16[256,512]{1,0:T(8,128)(2,1)S(1)}, u32[]{:S(2)}, u32[]{:S(2)}) collective-permute-start(bf16[256,512]{1,0:T(8,128)(2,1)S(1)} %get-tuple-element.81), channel_id=1, source_target_pairs={{0,4},{1,5},{2,6},{3,7},{4,0},{5,1},{6,2},{7,3},{8,12},{9,13},{10,... | collective-permute-start | bytes 786440 | tf_op jit(solution)/shard_map/ppermute | solution.py:80
  43.0 12.0 %collective-permute-start.14 = (bf16[152,512]{1,0:T(8,128)(2,1)S(1)}, bf16[152,512]{1,0:T(8,128)(2,1)S(1)}, u32[]{:S(2)}, u32[]{:S(2)}) collective-permute-start(bf16[152,512]{1,0:T(8,128)(2,1)S(1)} %pad_maximum_fusion.5), channel_id=1, source_target_pairs={{0,17},{1,16},{2,19},{3,18},{4,21},{5,20},{6,23},{7,22},{8,25},{9,... | collective-permute-start | bytes 466952 | tf_op jit(solution)/shard_map/ppermute | solution.py:80
  45.3 9.8 %collective-permute-start.12 = (bf16[152,512]{1,0:T(8,128)(2,1)S(1)}, bf16[152,512]{1,0:T(8,128)(2,1)S(1)}, u32[]{:S(2)}, u32[]{:S(2)}) collective-permute-start(bf16[152,512]{1,0:T(8,128)(2,1)S(1)} %get-tuple-element.113), channel_id=1, source_target_pairs={{0,1},{1,0},{2,3},{3,2},{4,5},{5,4},{6,7},{7,6},{8,9},{9,8},{10,11... | collective-permute-start | bytes 466952 | tf_op jit(solution)/shard_map/ppermute | solution.py:80
  46.1 9.0 %collective-permute-start.13 = (bf16[152,512]{1,0:T(8,128)(2,1)S(1)}, bf16[152,512]{1,0:T(8,128)(2,1)S(1)}, u32[]{:S(2)}, u32[]{:S(2)}) collective-permute-start(bf16[152,512]{1,0:T(8,128)(2,1)S(1)} %get-tuple-element.114), channel_id=1, source_target_pairs={{0,16},{1,17},{2,18},{3,19},{4,20},{5,21},{6,22},{7,23},{8,24},{9,... | collective-permute-start | bytes 466952 | tf_op jit(solution)/shard_map/ppermute | solution.py:80
  55.4 6.8 %collective-permute-start.15 = (bf16[44,512]{1,0:T(8,128)(2,1)S(1)}, bf16[44,512]{1,0:T(8,128)(2,1)S(1)}, u32[]{:S(2)}, u32[]{:S(2)}) collective-permute-start(bf16[44,512]{1,0:T(8,128)(2,1)S(1)} %get-tuple-element.110), channel_id=1, source_target_pairs={{0,4},{1,5},{2,6},{3,7},{4,0},{5,1},{6,2},{7,3},{8,12},{9,13},{10,... | collective-permute-start | bytes 135176 | tf_op jit(solution)/shard_map/ppermute | solution.py:80
  55.8 6.4 %collective-permute-start.16 = (bf16[44,512]{1,0:T(8,128)(2,1)S(1)}, bf16[44,512]{1,0:T(8,128)(2,1)S(1)}, u32[]{:S(2)}, u32[]{:S(2)}) collective-permute-start(bf16[44,512]{1,0:T(8,128)(2,1)S(1)} %get-tuple-element.111), channel_id=1, source_target_pairs={{0,2},{1,3},{2,0},{3,1},{4,6},{5,7},{6,4},{7,5},{8,10},{9,11},{10,... | collective-permute-start | bytes 135176 | tf_op jit(solution)/shard_map/ppermute | solution.py:80
  58.6 5.9 %collective-permute-start.17 = (bf16[44,512]{1,0:T(8,128)(2,1)S(1)}, bf16[44,512]{1,0:T(8,128)(2,1)S(1)}, u32[]{:S(2)}, u32[]{:S(2)}) collective-permute-start(bf16[44,512]{1,0:T(8,128)(2,1)S(1)} %get-tuple-element.112), channel_id=1, source_target_pairs={{0,6},{1,7},{2,4},{3,5},{4,2},{5,3},{6,0},{7,1},{8,14},{9,15},{10,... | collective-permute-start | bytes 135176 | tf_op jit(solution)/shard_map/ppermute | solution.py:80
  59.9 19.0 %copy-start.4 = (s32[8,128]{1,0:T(8,128)S(1)}, s32[8,128]{1,0:T(8,128)}, u32[]{:S(2)}) copy-start(s32[8,128]{1,0:T(8,128)} %rows_ref.5) | copy-start | bytes 12292
  59.9 18.9 %copy-start.5 = (s32[1,8]{1,0:T(1,128)S(1)}, s32[1,8]{1,0:T(1,128)}, u32[]{:S(2)}) copy-start(s32[1,8]{1,0:T(1,128)} %count_ref.5) | copy-start | bytes 100
  59.9 11.0 %collective-permute-start.23 = (bf16[384,512]{1,0:T(8,128)(2,1)S(1)}, bf16[384,512]{1,0:T(8,128)(2,1)S(1)}, u32[]{:S(2)}, u32[]{:S(2)}) collective-permute-start(bf16[384,512]{1,0:T(8,128)(2,1)S(1)} %pad_maximum_fusion.2), channel_id=1, source_target_pairs={{0,1},{1,0},{2,3},{3,2},{4,5},{5,4},{6,7},{7,6},{8,9},{9,8},{10,11... | collective-permute-start | bytes 1179656 | tf_op jit(solution)/shard_map/ppermute | solution.py:80
  64.5 5.8 %collective-permute-start.20 = (bf16[32,512]{1,0:T(8,128)(2,1)S(1)}, bf16[32,512]{1,0:T(8,128)(2,1)S(1)}, u32[]{:S(2)}, u32[]{:S(2)}) collective-permute-start(bf16[32,512]{1,0:T(8,128)(2,1)S(1)} %fusion), channel_id=1, source_target_pairs={{0,6},{1,7},{2,4},{3,5},{4,2},{5,3},{6,0},{7,1},{8,14},{9,15},{10,... | collective-permute-start | bytes 98312 | tf_op jit(solution)/shard_map/ppermute | solution.py:80
  66.0 4.4 %collective-permute-start.19 = (bf16[32,512]{1,0:T(8,128)(2,1)S(1)}, bf16[32,512]{1,0:T(8,128)(2,1)S(1)}, u32[]{:S(2)}, u32[]{:S(2)}) collective-permute-start(bf16[32,512]{1,0:T(8,128)(2,1)S(1)} %fusion), channel_id=1, source_target_pairs={{0,2},{1,3},{2,0},{3,1},{4,6},{5,7},{6,4},{7,5},{8,10},{9,11},{10,... | collective-permute-start | bytes 98312 | tf_op jit(solution)/shard_map/ppermute | solution.py:80
  66.0 4.9 %collective-permute-start.18 = (bf16[32,512]{1,0:T(8,128)(2,1)S(1)}, bf16[32,512]{1,0:T(8,128)(2,1)S(1)}, u32[]{:S(2)}, u32[]{:S(2)}) collective-permute-start(bf16[32,512]{1,0:T(8,128)(2,1)S(1)} %fusion), channel_id=1, source_target_pairs={{0,4},{1,5},{2,6},{3,7},{4,0},{5,1},{6,2},{7,3},{8,12},{9,13},{10,... | collective-permute-start | bytes 98312 | tf_op jit(solution)/shard_map/ppermute | solution.py:80
  70.9 9.2 %collective-permute-start.26 = (bf16[128,512]{1,0:T(8,128)(2,1)S(1)}, bf16[128,512]{1,0:T(8,128)(2,1)S(1)}, u32[]{:S(2)}, u32[]{:S(2)}) collective-permute-start(bf16[128,512]{1,0:T(8,128)(2,1)S(1)} %pad_maximum_fusion.7), channel_id=1, source_target_pairs={{0,17},{1,16},{2,19},{3,18},{4,21},{5,20},{6,23},{7,22},{8,25},{9,... | collective-permute-start | bytes 393224 | tf_op jit(solution)/shard_map/ppermute | solution.py:80
  73.0 7.1 %collective-permute-start.25 = (bf16[128,512]{1,0:T(8,128)(2,1)S(1)}, bf16[128,512]{1,0:T(8,128)(2,1)S(1)}, u32[]{:S(2)}, u32[]{:S(2)}) collective-permute-start(bf16[128,512]{1,0:T(8,128)(2,1)S(1)} %pad_maximum_fusion.7), channel_id=1, source_target_pairs={{0,16},{1,17},{2,18},{3,19},{4,20},{5,21},{6,22},{7,23},{8,24},{9,... | collective-permute-start | bytes 393224 | tf_op jit(solution)/shard_map/ppermute | solution.py:80
  73.6 6.6 %collective-permute-start.24 = (bf16[128,512]{1,0:T(8,128)(2,1)S(1)}, bf16[128,512]{1,0:T(8,128)(2,1)S(1)}, u32[]{:S(2)}, u32[]{:S(2)}) collective-permute-start(bf16[128,512]{1,0:T(8,128)(2,1)S(1)} %pad_maximum_fusion.7), channel_id=1, source_target_pairs={{0,1},{1,0},{2,3},{3,2},{4,5},{5,4},{6,7},{7,6},{8,9},{9,8},{10,11... | collective-permute-start | bytes 393224 | tf_op jit(solution)/shard_map/ppermute | solution.py:80
  74.5 6.9 %collective-permute-start.27 = (bf16[128,512]{1,0:T(8,128)(2,1)S(1)}, bf16[128,512]{1,0:T(8,128)(2,1)S(1)}, u32[]{:S(2)}, u32[]{:S(2)}) collective-permute-start(bf16[128,512]{1,0:T(8,128)(2,1)S(1)} %get-tuple-element.83), channel_id=1, source_target_pairs={{0,6},{1,7},{2,4},{3,5},{4,2},{5,3},{6,0},{7,1},{8,14},{9,15},{10,... | collective-permute-start | bytes 393224 | tf_op jit(solution)/shard_map/ppermute | solution.py:80
  76.8 7.8 %collective-permute-start.28 = (bf16[128,512]{1,0:T(8,128)(2,1)S(1)}, bf16[128,512]{1,0:T(8,128)(2,1)S(1)}, u32[]{:S(2)}, u32[]{:S(2)}) collective-permute-start(bf16[128,512]{1,0:T(8,128)(2,1)S(1)} %get-tuple-element.84), channel_id=1, source_target_pairs={{0,7},{1,6},{2,5},{3,4},{4,3},{5,2},{6,1},{7,0},{8,15},{9,14},{10,... | collective-permute-start | bytes 393224 | tf_op jit(solution)/shard_map/ppermute | solution.py:80
  78.9 5.7 %copy-start.6 = (s32[4]{0:T(128)S(1)}, s32[4]{0:T(128)}, u32[]{:S(2)}) copy-start(s32[4]{0:T(128)} %hub_ref.3) | copy-start | bytes 52
  84.6 1.9 %collective-permute-start.29 = (bf16[512,512]{1,0:T(8,128)(2,1)S(1)}, bf16[512,512]{1,0:T(8,128)(2,1)S(1)}, u32[]{:S(2)}, u32[]{:S(2)}) collective-permute-start(bf16[512,512]{1,0:T(8,128)(2,1)S(1)} %pad_maximum_fusion.x_ref), channel_id=1, source_target_pairs={{0,8},{1,9},{2,10},{3,11},{4,12},{5,13},{6,14},{7,15},{8,0},{9,1},... | collective-permute-start | bytes 1572872 | tf_op jit(solution)/shard_map/ppermute | solution.py:80

commit v6 on v5

--- a/solution.py
+++ b/solution.py
@@ -86,7 +86,7 @@
 
 
 def relayed(n_inner):
-    return list(range(2, n_inner - 2, 2))
+    return list(range(n_inner - 4, 0, -2))
 
 
 def places(n_inner, tile):
@@ -335,7 +335,7 @@
     hubx = hub_own
     for group in groups[:-1]:
         hubx = spread(hubx, group)
-    hubx, pairs[0], far_a, far_b = lax.optimization_barrier((hubx, pairs[0], far_a, far_b))
+    pairs[-1], far_a, far_b = lax.optimization_barrier((pairs[-1], far_a, far_b))
     direct = [exchange(far_a, (0, n_inner - 2)), exchange(far_b, (0, n_inner - 1))]
     for group in hub_groups[-2:]:
         hubx = spread(hubx, group)

time: 88.2 us -> 87.6 us (level)
  waiting for transfers between devices: 31.7 us -> 28.6 us
  starting transfers between devices: 41.1 us -> 43.2 us
    ppermute x30, waiting for transfers between devices: 31.7 us -> 28.6 us  [exchange(): lax.ppermute(x, ('outer', 'inner'), [(s, s ^ mask) for s in range(n_outer...]
    ppermute x30, starting transfers between devices: 41.1 us -> 43.2 us  [exchange(): lax.ppermute(x, ('outer', 'inner'), [(s, s ^ mask) for s in range(n_outer...]
  transfers between devices with their start and end apart: 30 -> 30, of which waited for: 15 -> 16; matrix products, arithmetic and copies ran while one was open for 3% -> 3% of each run, Pallas kernels for 4% -> 4%
where the time goes in v6:
time: 87.6 us; the launch traced here: 87.2 us
  starting transfers between devices  43.2 us (49%)
  waiting for transfers between devices  28.6 us (33%)
  Pallas kernels  11.2 us (13%)
  other arithmetic  2.4 us (3%)
  between operations  1.16 us (1%)
    ppermute x30, starting transfers between devices, exchange(): lax.ppermute(x, ('outer', 'inner'), [(s, s ^ mask) for s in range(n_outer...  43.2 us
    ppermute x30, waiting for transfers between devices, exchange(): lax.ppermute(x, ('outer', 'inner'), [(s, s ^ mask) for s in range(n_outer...  28.6 us
    pallas_call x1, Pallas kernels, body(): pl.pallas_call(functools.partial(middle_kernel, steps, hub_steps, n_inner...  3.65 us
    pallas_call x1, Pallas kernels, body(): pl.pallas_call(gather_kernel, out_shape=(shape(hd, width),) + sizes, in_s...  2.68 us
  transfers between devices with their start and end apart: 30, of which 16 were waited for; matrix products, arithmetic and copies ran while one was open for 3% of the time, Pallas kernels for 4%

profile of v6, /device:TPU:0, one launch (start us, length us, event | category | flops | bytes accessed | tf_op | source)
XLA Modules:
  0.0 87.2 jit_solution(7702250782472360081)
XLA Ops:
  0.6 2.7 %gather_rows.1 = (bf16[4,512]{1,0:T(4,128)(2,1)}, bf16[128,512]{1,0:T(8,128)(2,1)}, bf16[256,512]{1,0:T(8,128)(2,1)}, bf16[256,512]{1,0:T(8,128)(2,1)}, bf16[128...) custom-call(s32[4]{0:T(128)} %hub_ref.3, s32[1,8]{1,0:T(1,128)} %count_ref.5, ...), custom_call_target="tpu_custom_call" | custom-call | flops 400000000 | bytes 3000000 | tf_op jit(solution)/shard_map/gather_rows/pallas_call | solution.py:324
  3.3 3.0 %collective-permute-start.7 = (bf16[256,512]{1,0:T(8,128)(2,1)}, bf16[256,512]{1,0:T(8,128)(2,1)S(1)}, u32[]{:S(2)}, u32[]{:S(2)}) collective-permute-start(bf16[256,512]{1,0:T(8,128)(2,1)} %get-tuple-element.59), channel_id=1, source_target_pairs={{0,2},{1,3},{2,0},{3,1},{4,6},{5,7},{6,4},{7,5},{8,10},{9,11},{10,... | collective-permute-start | bytes 786440 | tf_op jit(solution)/shard_map/ppermute | solution.py:80
  6.3 2.6 %collective-permute-start.6 = (bf16[256,512]{1,0:T(8,128)(2,1)}, bf16[256,512]{1,0:T(8,128)(2,1)S(1)}, u32[]{:S(2)}, u32[]{:S(2)}) collective-permute-start(bf16[256,512]{1,0:T(8,128)(2,1)} %get-tuple-element.58), channel_id=1, source_target_pairs={{0,4},{1,5},{2,6},{3,7},{4,0},{5,1},{6,2},{7,3},{8,12},{9,13},{10,... | collective-permute-start | bytes 786440 | tf_op jit(solution)/shard_map/ppermute | solution.py:80
  8.9 0.0 collective-permute-start
  8.9 1.4 %collective-permute-done = bf16[4,512]{1,0:T(4,128)(2,1)S(1)} collective-permute-done((bf16[4,512]{1,0:T(4,128)(2,1)}, bf16[4,512]{1,0:T(4,128)(2,1)S(1)}, u32[]{:S(2)}, u32[]{:S(2)}) %collective-permute-start) | collective-permute-done | bytes 4128 | tf_op jit(solution)/shard_map/ppermute | solution.py:80
  10.3 0.7 pad_maximum_fusion.13
  11.0 0.0 copy-start
  11.0 0.0 copy-start.11
  11.0 2.5 %collective-permute-start.3 = (bf16[8,512]{1,0:T(8,128)(2,1)S(1)}, bf16[8,512]{1,0:T(8,128)(2,1)S(1)}, u32[]{:S(2)}, u32[]{:S(2)}) collective-permute-start(bf16[8,512]{1,0:T(8,128)(2,1)S(1)} %pad_maximum_fusion.13), channel_id=1, source_target_pairs={{0,17},{1,16},{2,19},{3,18},{4,21},{5,20},{6,23},{7,22},{8,25},{9,... | collective-permute-start | bytes 24584 | tf_op jit(solution)/shard_map/ppermute | solution.py:80
  13.6 0.5 collective-permute-start.2
  14.1 0.5 collective-permute-start.1
  14.6 0.1 convert_element_type.39.ws_ref
  14.7 1.0 %collective-permute-done.3 = bf16[8,512]{1,0:T(8,128)(2,1)S(1)} collective-permute-done((bf16[8,512]{1,0:T(8,128)(2,1)S(1)}, bf16[8,512]{1,0:T(8,128)(2,1)S(1)}, u32[]{:S(2)}, u32[]{:S(2)}) %collective-permute-start.3) | collective-permute-done | bytes 8224 | tf_op jit(solution)/shard_map/ppermute | solution.py:80
  15.7 1.5 %collective-permute-done.2 = bf16[8,512]{1,0:T(8,128)(2,1)S(1)} collective-permute-done((bf16[8,512]{1,0:T(8,128)(2,1)S(1)}, bf16[8,512]{1,0:T(8,128)(2,1)S(1)}, u32[]{:S(2)}, u32[]{:S(2)}) %collective-permute-start.2) | collective-permute-done | bytes 8224 | tf_op jit(solution)/shard_map/ppermute | solution.py:80
  17.2 0.5 collective-permute-done.1
  17.7 0.4 collective-permute-start.4
  18.2 0.2 collective-permute-done.7.rest_2_
  18.4 1.5 %collective-permute-done.6.rest_1_ = bf16[256,512]{1,0:T(8,128)(2,1)S(1)} collective-permute-done((bf16[256,512]{1,0:T(8,128)(2,1)}, bf16[256,512]{1,0:T(8,128)(2,1)S(1)}, u32[]{:S(2)}, u32[]{:S(2)}) %collective-permute-start.6) | collective-permute-done | bytes 262176 | tf_op jit(solution)/shard_map/ppermute | solution.py:80
  19.9 0.0 copy-start.1
  19.9 0.0 copy-start.2
  20.0 0.0 copy-start.3
  20.0 1.6 %collective-permute-start.8 = (bf16[384,512]{1,0:T(8,128)(2,1)S(1)}, bf16[384,512]{1,0:T(8,128)(2,1)S(1)}, u32[]{:S(2)}, u32[]{:S(2)}) collective-permute-start(bf16[384,512]{1,0:T(8,128)(2,1)S(1)} %pad_maximum_fusion.1), channel_id=1, source_target_pairs={{0,1},{1,0},{2,3},{3,2},{4,5},{5,4},{6,7},{7,6},{8,9},{9,8},{10,11... | collective-permute-start | bytes 1179656 | tf_op jit(solution)/shard_map/ppermute | solution.py:80
  21.6 0.1 collective-permute-done.4
  21.7 1.6 %collective-permute-start.5 = (bf16[64,512]{1,0:T(8,128)(2,1)S(1)}, bf16[64,512]{1,0:T(8,128)(2,1)S(1)}, u32[]{:S(2)}, u32[]{:S(2)}) collective-permute-start(bf16[64,512]{1,0:T(8,128)(2,1)S(1)} %pad_maximum_fusion.11), channel_id=1, source_target_pairs={{0,4},{1,5},{2,6},{3,7},{4,0},{5,1},{6,2},{7,3},{8,12},{9,13},{10,... | collective-permute-start | bytes 196616 | tf_op jit(solution)/shard_map/ppermute | solution.py:80
  23.3 2.5 %collective-permute-start.9 = (bf16[128,512]{1,0:T(8,128)(2,1)S(1)}, bf16[128,512]{1,0:T(8,128)(2,1)S(1)}, u32[]{:S(2)}, u32[]{:S(2)}) collective-permute-start(bf16[128,512]{1,0:T(8,128)(2,1)S(1)} %copy-done.13), channel_id=1, source_target_pairs={{0,6},{1,7},{2,4},{3,5},{4,2},{5,3},{6,0},{7,1},{8,14},{9,15},{10,... | collective-permute-start | bytes 393224 | tf_op jit(solution)/shard_map/ppermute | solution.py:80
  25.8 1.3 %collective-permute-start.10 = (bf16[128,512]{1,0:T(8,128)(2,1)S(1)}, bf16[128,512]{1,0:T(8,128)(2,1)S(1)}, u32[]{:S(2)}, u32[]{:S(2)}) collective-permute-start(bf16[128,512]{1,0:T(8,128)(2,1)S(1)} %copy-done.12), channel_id=1, source_target_pairs={{0,7},{1,6},{2,5},{3,4},{4,3},{5,2},{6,1},{7,0},{8,15},{9,14},{10,... | collective-permute-start | bytes 393224 | tf_op jit(solution)/shard_map/ppermute | solution.py:80
  27.1 0.4 convolution_add_fusion.pre0
  27.5 0.0 copy-start.7
  27.5 0.0 copy-start.8
  27.5 0.5 prepare.1
  28.0 5.6 %collective-permute-done.5 = bf16[64,512]{1,0:T(8,128)(2,1)S(1)} collective-permute-done((bf16[64,512]{1,0:T(8,128)(2,1)S(1)}, bf16[64,512]{1,0:T(8,128)(2,1)S(1)}, u32[]{:S(2)}, u32[]{:S(2)}) %collective-permute-start.5) | collective-permute-done | bytes 65568 | tf_op jit(solution)/shard_map/ppermute | solution.py:80
  33.6 3.7 %middle.1 = (f32[384,512]{1,0:T(8,128)S(1)}, bf16[384,512]{1,0:T(8,128)(2,1)S(1)}, f32[384,512]{1,0:T(8,128)S(1)}, bf16[592,512]{1,0:T(8,128)(2,1)S(1)}, bf16[59...) custom-call(s32[3,6]{1,0:T(4,128)S(1)} %copy-done.7, ...), custom_call_target="tpu_custom_call" | custom-call | flops 2000000000 | bytes 9000000 | tf_op jit(solution)/shard_map/middle/pallas_call | solution.py:390
  37.3 0.1 collective-permute-start.11
  37.4 5.0 %collective-permute-start.21 = (bf16[256,512]{1,0:T(8,128)(2,1)S(1)}, bf16[256,512]{1,0:T(8,128)(2,1)S(1)}, u32[]{:S(2)}, u32[]{:S(2)}) collective-permute-start(bf16[256,512]{1,0:T(8,128)(2,1)S(1)} %get-tuple-element.78), channel_id=1, source_target_pairs={{0,4},{1,5},{2,6},{3,7},{4,0},{5,1},{6,2},{7,3},{8,12},{9,13},{10,... | collective-permute-start | bytes 786440 | tf_op jit(solution)/shard_map/ppermute | solution.py:80
  42.3 0.2 convert_add_fusion
  42.6 2.1 %collective-permute-start.14 = (bf16[152,512]{1,0:T(8,128)(2,1)S(1)}, bf16[152,512]{1,0:T(8,128)(2,1)S(1)}, u32[]{:S(2)}, u32[]{:S(2)}) collective-permute-start(bf16[152,512]{1,0:T(8,128)(2,1)S(1)} %pad_maximum_fusion.5), channel_id=1, source_target_pairs={{0,17},{1,16},{2,19},{3,18},{4,21},{5,20},{6,23},{7,22},{8,25},{9,... | collective-permute-start | bytes 466952 | tf_op jit(solution)/shard_map/ppermute | solution.py:80
  44.8 1.0 %collective-permute-start.12 = (bf16[152,512]{1,0:T(8,128)(2,1)S(1)}, bf16[152,512]{1,0:T(8,128)(2,1)S(1)}, u32[]{:S(2)}, u32[]{:S(2)}) collective-permute-start(bf16[152,512]{1,0:T(8,128)(2,1)S(1)} %get-tuple-element.111), channel_id=1, source_target_pairs={{0,1},{1,0},{2,3},{3,2},{4,5},{5,4},{6,7},{7,6},{8,9},{9,8},{10,11... | collective-permute-start | bytes 466952 | tf_op jit(solution)/shard_map/ppermute | solution.py:80
  45.8 0.5 collective-permute-start.13
  46.3 8.5 %collective-permute-done.21.rest_1_ = bf16[256,512]{1,0:T(8,128)(2,1)S(1)} collective-permute-done((bf16[256,512]{1,0:T(8,128)(2,1)S(1)}, bf16[256,512]{1,0:T(8,128)(2,1)S(1)}, u32[]{:S(2)}, u32[]{:S(2)}) %collective-permute-start.21) | collective-permute-done | bytes 262176 | tf_op jit(solution)/shard_map/ppermute | solution.py:80
  55.0 0.1 slice_add_fusion
  55.3 2.3 %collective-permute-start.15 = (bf16[44,512]{1,0:T(8,128)(2,1)S(1)}, bf16[44,512]{1,0:T(8,128)(2,1)S(1)}, u32[]{:S(2)}, u32[]{:S(2)}) collective-permute-start(bf16[44,512]{1,0:T(8,128)(2,1)S(1)} %get-tuple-element.108), channel_id=1, source_target_pairs={{0,4},{1,5},{2,6},{3,7},{4,0},{5,1},{6,2},{7,3},{8,12},{9,13},{10,... | collective-permute-start | bytes 135176 | tf_op jit(solution)/shard_map/ppermute | solution.py:80
  57.5 0.3 collective-permute-start.16
  57.8 1.9 %collective-permute-start.17 = (bf16[44,512]{1,0:T(8,128)(2,1)S(1)}, bf16[44,512]{1,0:T(8,128)(2,1)S(1)}, u32[]{:S(2)}, u32[]{:S(2)}) collective-permute-start(bf16[44,512]{1,0:T(8,128)(2,1)S(1)} %get-tuple-element.110), channel_id=1, source_target_pairs={{0,6},{1,7},{2,4},{3,5},{4,2},{5,3},{6,0},{7,1},{8,14},{9,15},{10,... | collective-permute-start | bytes 135176 | tf_op jit(solution)/shard_map/ppermute | solution.py:80
  59.7 0.0 copy-start.4
  59.7 0.0 copy-start.5
  59.8 1.2 %collective-permute-start.23 = (bf16[384,512]{1,0:T(8,128)(2,1)S(1)}, bf16[384,512]{1,0:T(8,128)(2,1)S(1)}, u32[]{:S(2)}, u32[]{:S(2)}) collective-permute-start(bf16[384,512]{1,0:T(8,128)(2,1)S(1)} %pad_maximum_fusion.2), channel_id=1, source_target_pairs={{0,1},{1,0},{2,3},{3,2},{4,5},{5,4},{6,7},{7,6},{8,9},{9,8},{10,11... | collective-permute-start | bytes 1179656 | tf_op jit(solution)/shard_map/ppermute | solution.py:80
  60.9 1.0 %multiply_convert_fusion = bf16[384,512]{1,0:T(8,128)(2,1)} fusion(f32[384,512]{1,0:T(8,128)S(1)} %get-tuple-element.72), kind=kLoop, calls=%fused_computation.2 | loop fusion | flops 983040 | bytes 1179648 | tf_op jit(solution)/shard_map/convert_element_type | solution.py:400
  61.9 1.7 %collective-permute-done.17 = bf16[44,512]{1,0:T(8,128)(2,1)S(1)} collective-permute-done((bf16[44,512]{1,0:T(8,128)(2,1)S(1)}, bf16[44,512]{1,0:T(8,128)(2,1)S(1)}, u32[]{:S(2)}, u32[]{:S(2)}) %collective-permute-start.17) | collective-permute-done | bytes 45088 | tf_op jit(solution)/shard_map/ppermute | solution.py:80
  63.7 2.0 %collective-permute-start.20 = (bf16[32,512]{1,0:T(8,128)(2,1)S(1)}, bf16[32,512]{1,0:T(8,128)(2,1)S(1)}, u32[]{:S(2)}, u32[]{:S(2)}) collective-permute-start(bf16[32,512]{1,0:T(8,128)(2,1)S(1)} %fusion), channel_id=1, source_target_pairs={{0,6},{1,7},{2,4},{3,5},{4,2},{5,3},{6,0},{7,1},{8,14},{9,15},{10,... | collective-permute-start | bytes 98312 | tf_op jit(solution)/shard_map/ppermute | solution.py:80
  65.7 2.4 %collective-permute-start.18 = (bf16[32,512]{1,0:T(8,128)(2,1)S(1)}, bf16[32,512]{1,0:T(8,128)(2,1)S(1)}, u32[]{:S(2)}, u32[]{:S(2)}) collective-permute-start(bf16[32,512]{1,0:T(8,128)(2,1)S(1)} %fusion), channel_id=1, source_target_pairs={{0,4},{1,5},{2,6},{3,7},{4,0},{5,1},{6,2},{7,3},{8,12},{9,13},{10,... | collective-permute-start | bytes 98312 | tf_op jit(solution)/shard_map/ppermute | solution.py:80
  68.1 1.3 %collective-permute-done.20 = bf16[32,512]{1,0:T(8,128)(2,1)S(1)} collective-permute-done((bf16[32,512]{1,0:T(8,128)(2,1)S(1)}, bf16[32,512]{1,0:T(8,128)(2,1)S(1)}, u32[]{:S(2)}, u32[]{:S(2)}) %collective-permute-start.20) | collective-permute-done | bytes 32800 | tf_op jit(solution)/shard_map/ppermute | solution.py:80
  69.5 0.3 collective-permute-done.19
  69.8 0.7 collective-permute-done.18
  70.5 2.1 %collective-permute-start.26 = (bf16[128,512]{1,0:T(8,128)(2,1)S(1)}, bf16[128,512]{1,0:T(8,128)(2,1)S(1)}, u32[]{:S(2)}, u32[]{:S(2)}) collective-permute-start(bf16[128,512]{1,0:T(8,128)(2,1)S(1)} %pad_maximum_fusion.7), channel_id=1, source_target_pairs={{0,17},{1,16},{2,19},{3,18},{4,21},{5,20},{6,23},{7,22},{8,25},{9,... | collective-permute-start | bytes 393224 | tf_op jit(solution)/shard_map/ppermute | solution.py:80
  72.6 0.5 collective-permute-start.25
  73.2 0.9 %collective-permute-start.24 = (bf16[128,512]{1,0:T(8,128)(2,1)S(1)}, bf16[128,512]{1,0:T(8,128)(2,1)S(1)}, u32[]{:S(2)}, u32[]{:S(2)}) collective-permute-start(bf16[128,512]{1,0:T(8,128)(2,1)S(1)} %pad_maximum_fusion.7), channel_id=1, source_target_pairs={{0,1},{1,0},{2,3},{3,2},{4,5},{5,4},{6,7},{7,6},{8,9},{9,8},{10,11... | collective-permute-start | bytes 393224 | tf_op jit(solution)/shard_map/ppermute | solution.py:80
  74.1 1.9 %collective-permute-start.27 = (bf16[128,512]{1,0:T(8,128)(2,1)S(1)}, bf16[128,512]{1,0:T(8,128)(2,1)S(1)}, u32[]{:S(2)}, u32[]{:S(2)}) collective-permute-start(bf16[128,512]{1,0:T(8,128)(2,1)S(1)} %get-tuple-element.81), channel_id=1, source_target_pairs={{0,6},{1,7},{2,4},{3,5},{4,2},{5,3},{6,0},{7,1},{8,14},{9,15},{10,... | collective-permute-start | bytes 393224 | tf_op jit(solution)/shard_map/ppermute | solution.py:80
  76.0 2.5 %collective-permute-start.28 = (bf16[128,512]{1,0:T(8,128)(2,1)S(1)}, bf16[128,512]{1,0:T(8,128)(2,1)S(1)}, u32[]{:S(2)}, u32[]{:S(2)}) collective-permute-start(bf16[128,512]{1,0:T(8,128)(2,1)S(1)} %get-tuple-element.82), channel_id=1, source_target_pairs={{0,7},{1,6},{2,5},{3,4},{4,3},{5,2},{6,1},{7,0},{8,15},{9,14},{10,... | collective-permute-start | bytes 393224 | tf_op jit(solution)/shard_map/ppermute | solution.py:80
  78.5 1.2 %scatter_first.1.own_ref = f32[384,512]{1,0:T(8,128)S(1)} custom-call(s32[1,8]{1,0:T(1,128)S(1)} %copy-done.5, s32[8,128]{1,0:T(8,128)S(1)} %copy-done.4, f32[384,512]{1,0:T(8,128)S(1)} %get-tuple-element.84.gown_ref, bf16[384,512]{1,0:T(8,128)(2,1)S(1)} %get-tuple-element.85.gp_ref, bf16[512,512]{1,0:T(8,128)(2,1)S(1)} %convert_element_type.39.ws_ref, ...), custom_call_target="tpu_custom_call" | custom-call | flops 400000000 | bytes 3000000 | tf_op jit(solution)/shard_map/scatter_first/pallas_call | solution.py:437
  79.8 1.2 %collective-permute-done.27.rest_0_ = bf16[128,512]{1,0:T(8,128)(2,1)S(1)} collective-permute-done((bf16[128,512]{1,0:T(8,128)(2,1)S(1)}, bf16[128,512]{1,0:T(8,128)(2,1)S(1)}, u32[]{:S(2)}, u32[]{:S(2)}) %collective-permute-start.27) | collective-permute-done | bytes 131104 | tf_op jit(solution)/shard_map/ppermute | solution.py:80
  81.0 2.8 %collective-permute-done.28.rest_1_ = bf16[128,512]{1,0:T(8,128)(2,1)S(1)} collective-permute-done((bf16[128,512]{1,0:T(8,128)(2,1)S(1)}, bf16[128,512]{1,0:T(8,128)(2,1)S(1)}, u32[]{:S(2)}, u32[]{:S(2)}) %collective-permute-start.28) | collective-permute-done | bytes 131104 | tf_op jit(solution)/shard_map/ppermute | solution.py:80
  83.8 1.6 %scatter_last.1 = bf16[384,512]{1,0:T(8,128)(2,1)} custom-call(s32[4]{0:T(128)S(1)} %copy-done.6, s32[1,8]{1,0:T(1,128)S(1)} %copy-done.5, s32[8,128]{1,0:T(8,128)S(1)} %copy-done.4, f32[384,512]{1,0:T(8,128)S(1)} %scatter_first.1.own_ref, f32[4,512]{1,0:T(4,128)S(1)} %slice_add_fusion.15.hub_grad_ref, bf16[128,512]{1,0:T(8,128)(2,1)S(1)} %collective-permute-done.27.rest_0_, ...), custom_call_target="tpu_custom_call" | custom-call | flops 200000000 | bytes 2000000 | tf_op jit(solution)/shard_map/scatter_last/pallas_call | solution.py:448
  85.4 0.3 collective-permute-done.29.y_ref
  85.7 1.6 %finish.1 = (f32[512,512]{1,0:T(8,128)}, f32[512,512]{1,0:T(8,128)}, f32[1,512]{1,0:T(1,128)}) custom-call(bf16[512,512]{1,0:T(8,128)(2,1)S(1)} %pad_maximum_fusion.x_ref, bf16[512,512]{1,0:T(8,128)(2,1)S(1)} %collective-permute-done.29.y_ref, f32[8,512]{1,0:T(8,128)S(1)} %slice_add_fusion.9.bias_in), custom_call_target="tpu_custom_call" | custom-call | flops 1000000 | bytes 3000000 | tf_op jit(solution)/shard_map/finish/pallas_call | solution.py:459
  (70 shorter events, 0.5 us)
Async XLA Ops:
  0.6 14.0 %copy-start.9 = (f32[512,512]{1,0:T(8,128)S(1)}, f32[512,512]{1,0:T(8,128)}, u32[]{:S(2)}) copy-start(f32[512,512]{1,0:T(8,128)} %param.16) | copy-start | bytes 3145732
  3.3 16.6 %copy-start.10 = (bf16[128,512]{1,0:T(8,128)(2,1)S(1)}, bf16[128,512]{1,0:T(8,128)(2,1)}, u32[]{:S(2)}) copy-start(bf16[128,512]{1,0:T(8,128)(2,1)} %get-tuple-element.63) | copy-start | bytes 393220
  3.3 15.0 %collective-permute-start.7 = (bf16[256,512]{1,0:T(8,128)(2,1)}, bf16[256,512]{1,0:T(8,128)(2,1)S(1)}, u32[]{:S(2)}, u32[]{:S(2)}) collective-permute-start(bf16[256,512]{1,0:T(8,128)(2,1)} %get-tuple-element.59), channel_id=1, source_target_pairs={{0,2},{1,3},{2,0},{3,1},{4,6},{5,7},{6,4},{7,5},{8,10},{9,11},{10,... | collective-permute-start | bytes 786440 | tf_op jit(solution)/shard_map/ppermute | solution.py:80
  6.3 13.6 %collective-permute-start.6 = (bf16[256,512]{1,0:T(8,128)(2,1)}, bf16[256,512]{1,0:T(8,128)(2,1)S(1)}, u32[]{:S(2)}, u32[]{:S(2)}) collective-permute-start(bf16[256,512]{1,0:T(8,128)(2,1)} %get-tuple-element.58), channel_id=1, source_target_pairs={{0,4},{1,5},{2,6},{3,7},{4,0},{5,1},{6,2},{7,3},{8,12},{9,13},{10,... | collective-permute-start | bytes 786440 | tf_op jit(solution)/shard_map/ppermute | solution.py:80
  8.9 1.4 %collective-permute-start = (bf16[4,512]{1,0:T(4,128)(2,1)}, bf16[4,512]{1,0:T(4,128)(2,1)S(1)}, u32[]{:S(2)}, u32[]{:S(2)}) collective-permute-start(bf16[4,512]{1,0:T(4,128)(2,1)} %get-tuple-element.51), channel_id=1, source_target_pairs={{0,8},{1,9},{2,10},{3,11},{4,12},{5,13},{6,14},{7,15},{8,0},{9,1},... | collective-permute-start | bytes 12296 | tf_op jit(solution)/shard_map/ppermute | solution.py:80
  11.0 12.3 %copy-start.13 = (bf16[128,512]{1,0:T(8,128)(2,1)S(1)}, bf16[128,512]{1,0:T(8,128)(2,1)}, u32[]{:S(2)}) copy-start(bf16[128,512]{1,0:T(8,128)(2,1)} %get-tuple-element.64) | copy-start | bytes 393220
  11.0 14.7 %copy-start.12 = (bf16[128,512]{1,0:T(8,128)(2,1)S(1)}, bf16[128,512]{1,0:T(8,128)(2,1)}, u32[]{:S(2)}) copy-start(bf16[128,512]{1,0:T(8,128)(2,1)} %get-tuple-element.65) | copy-start | bytes 393220
  11.0 16.0 %copy-start = (bf16[384,512]{1,0:T(8,128)(2,1)S(1)}, bf16[384,512]{1,0:T(8,128)(2,1)}, u32[]{:S(2)}) copy-start(bf16[384,512]{1,0:T(8,128)(2,1)} %feat_ref.3) | copy-start | bytes 1179652
  11.0 16.0 %copy-start.11 = (f32[512]{0:T(512)S(1)}, f32[512]{0:T(512)}, u32[]{:S(2)}) copy-start(f32[512]{0:T(512)} %param.18) | copy-start | bytes 6148
  11.0 4.6 %collective-permute-start.3 = (bf16[8,512]{1,0:T(8,128)(2,1)S(1)}, bf16[8,512]{1,0:T(8,128)(2,1)S(1)}, u32[]{:S(2)}, u32[]{:S(2)}) collective-permute-start(bf16[8,512]{1,0:T(8,128)(2,1)S(1)} %pad_maximum_fusion.13), channel_id=1, source_target_pairs={{0,17},{1,16},{2,19},{3,18},{4,21},{5,20},{6,23},{7,22},{8,25},{9,... | collective-permute-start | bytes 24584 | tf_op jit(solution)/shard_map/ppermute | solution.py:80
  13.6 3.7 %collective-permute-start.2 = (bf16[8,512]{1,0:T(8,128)(2,1)S(1)}, bf16[8,512]{1,0:T(8,128)(2,1)S(1)}, u32[]{:S(2)}, u32[]{:S(2)}) collective-permute-start(bf16[8,512]{1,0:T(8,128)(2,1)S(1)} %pad_maximum_fusion.13), channel_id=1, source_target_pairs={{0,16},{1,17},{2,18},{3,19},{4,20},{5,21},{6,22},{7,23},{8,24},{9,... | collective-permute-start | bytes 24584 | tf_op jit(solution)/shard_map/ppermute | solution.py:80
  14.1 3.7 %collective-permute-start.1 = (bf16[8,512]{1,0:T(8,128)(2,1)S(1)}, bf16[8,512]{1,0:T(8,128)(2,1)S(1)}, u32[]{:S(2)}, u32[]{:S(2)}) collective-permute-start(bf16[8,512]{1,0:T(8,128)(2,1)S(1)} %pad_maximum_fusion.13), channel_id=1, source_target_pairs={{0,1},{1,0},{2,3},{3,2},{4,5},{5,4},{6,7},{7,6},{8,9},{9,8},{10,11... | collective-permute-start | bytes 24584 | tf_op jit(solution)/shard_map/ppermute | solution.py:80
  17.7 3.9 %collective-permute-start.4 = (bf16[32,512]{1,0:T(8,128)(2,1)S(1)}, bf16[32,512]{1,0:T(8,128)(2,1)S(1)}, u32[]{:S(2)}, u32[]{:S(2)}) collective-permute-start(bf16[32,512]{1,0:T(8,128)(2,1)S(1)} %pad_maximum_fusion.12), channel_id=1, source_target_pairs={{0,2},{1,3},{2,0},{3,1},{4,6},{5,7},{6,4},{7,5},{8,10},{9,11},{10,... | collective-permute-start | bytes 98312 | tf_op jit(solution)/shard_map/ppermute | solution.py:80
  19.9 7.5 %copy-start.1 = (f32[512,512]{1,0:T(8,128)S(1)}, f32[512,512]{1,0:T(8,128)}, u32[]{:S(2)}) copy-start(f32[512,512]{1,0:T(8,128)} %wn_ref.1) | copy-start | bytes 3145732
  19.9 7.5 %copy-start.2 = (bf16[18,128,128]{2,1,0:T(8,128)(2,1)S(1)}, bf16[18,128,128]{2,1,0:T(8,128)(2,1)}, u32[]{:S(2)}) copy-start(bf16[18,128,128]{2,1,0:T(8,128)(2,1)} %adj_ref.1) | copy-start | bytes 1769476
  20.0 7.5 %copy-start.3 = (bf16[384,512]{1,0:T(8,128)(2,1)S(1)}, bf16[384,512]{1,0:T(8,128)(2,1)}, u32[]{:S(2)}) copy-start(bf16[384,512]{1,0:T(8,128)(2,1)} %cot_ref.1) | copy-start | bytes 1179652
  20.0 13.6 %collective-permute-start.8 = (bf16[384,512]{1,0:T(8,128)(2,1)S(1)}, bf16[384,512]{1,0:T(8,128)(2,1)S(1)}, u32[]{:S(2)}, u32[]{:S(2)}) collective-permute-start(bf16[384,512]{1,0:T(8,128)(2,1)S(1)} %pad_maximum_fusion.1), channel_id=1, source_target_pairs={{0,1},{1,0},{2,3},{3,2},{4,5},{5,4},{6,7},{7,6},{8,9},{9,8},{10,11... | collective-permute-start | bytes 1179656 | tf_op jit(solution)/shard_map/ppermute | solution.py:80
  21.7 11.9 %collective-permute-start.5 = (bf16[64,512]{1,0:T(8,128)(2,1)S(1)}, bf16[64,512]{1,0:T(8,128)(2,1)S(1)}, u32[]{:S(2)}, u32[]{:S(2)}) collective-permute-start(bf16[64,512]{1,0:T(8,128)(2,1)S(1)} %pad_maximum_fusion.11), channel_id=1, source_target_pairs={{0,4},{1,5},{2,6},{3,7},{4,0},{5,1},{6,2},{7,3},{8,12},{9,13},{10,... | collective-permute-start | bytes 196616 | tf_op jit(solution)/shard_map/ppermute | solution.py:80
  23.3 10.3 %collective-permute-start.9 = (bf16[128,512]{1,0:T(8,128)(2,1)S(1)}, bf16[128,512]{1,0:T(8,128)(2,1)S(1)}, u32[]{:S(2)}, u32[]{:S(2)}) collective-permute-start(bf16[128,512]{1,0:T(8,128)(2,1)S(1)} %copy-done.13), channel_id=1, source_target_pairs={{0,6},{1,7},{2,4},{3,5},{4,2},{5,3},{6,0},{7,1},{8,14},{9,15},{10,... | collective-permute-start | bytes 393224 | tf_op jit(solution)/shard_map/ppermute | solution.py:80
  25.8 7.8 %collective-permute-start.10 = (bf16[128,512]{1,0:T(8,128)(2,1)S(1)}, bf16[128,512]{1,0:T(8,128)(2,1)S(1)}, u32[]{:S(2)}, u32[]{:S(2)}) collective-permute-start(bf16[128,512]{1,0:T(8,128)(2,1)S(1)} %copy-done.12), channel_id=1, source_target_pairs={{0,7},{1,6},{2,5},{3,4},{4,3},{5,2},{6,1},{7,0},{8,15},{9,14},{10,... | collective-permute-start | bytes 393224 | tf_op jit(solution)/shard_map/ppermute | solution.py:80
  27.5 6.1 %copy-start.7 = (s32[3,6]{1,0:T(4,128)S(1)}, s32[3,6]{1,0:T(4,128)}, u32[]{:S(2)}) copy-start(s32[3,6]{1,0:T(4,128)} %tile_src.1) | copy-start | bytes 220
  27.5 6.1 %copy-start.8 = (bf16[128,512]{1,0:T(8,128)(2,1)S(1)}, bf16[128,512]{1,0:T(8,128)(2,1)}, u32[]{:S(2)}) copy-start(bf16[128,512]{1,0:T(8,128)(2,1)} %get-tuple-element.57.rest_0_) | copy-start | bytes 393220
  37.3 5.0 %collective-permute-start.11 = (bf16[592,512]{1,0:T(8,128)(2,1)S(1)}, bf16[592,512]{1,0:T(8,128)(2,1)S(1)}, u32[]{:S(2)}, u32[]{:S(2)}) collective-permute-start(bf16[592,512]{1,0:T(8,128)(2,1)S(1)} %get-tuple-element.67), channel_id=1, source_target_pairs={{0,8},{1,9},{2,10},{3,11},{4,12},{5,13},{6,14},{7,15},{8,0},{9,1},... | collective-permute-start | bytes 1818632 | tf_op jit(solution)/shard_map/ppermute | solution.py:80
  37.4 17.5 %collective-permute-start.21 = (bf16[256,512]{1,0:T(8,128)(2,1)S(1)}, bf16[256,512]{1,0:T(8,128)(2,1)S(1)}, u32[]{:S(2)}, u32[]{:S(2)}) collective-permute-start(bf16[256,512]{1,0:T(8,128)(2,1)S(1)} %get-tuple-element.78), channel_id=1, source_target_pairs={{0,4},{1,5},{2,6},{3,7},{4,0},{5,1},{6,2},{7,3},{8,12},{9,13},{10,... | collective-permute-start | bytes 786440 | tf_op jit(solution)/shard_map/ppermute | solution.py:80
  42.3 12.5 %collective-permute-start.22 = (bf16[256,512]{1,0:T(8,128)(2,1)S(1)}, bf16[256,512]{1,0:T(8,128)(2,1)S(1)}, u32[]{:S(2)}, u32[]{:S(2)}) collective-permute-start(bf16[256,512]{1,0:T(8,128)(2,1)S(1)} %get-tuple-element.79), channel_id=1, source_target_pairs={{0,2},{1,3},{2,0},{3,1},{4,6},{5,7},{6,4},{7,5},{8,10},{9,11},{10,... | collective-permute-start | bytes 786440 | tf_op jit(solution)/shard_map/ppermute | solution.py:80
  42.6 12.2 %collective-permute-start.14 = (bf16[152,512]{1,0:T(8,128)(2,1)S(1)}, bf16[152,512]{1,0:T(8,128)(2,1)S(1)}, u32[]{:S(2)}, u32[]{:S(2)}) collective-permute-start(bf16[152,512]{1,0:T(8,128)(2,1)S(1)} %pad_maximum_fusion.5), channel_id=1, source_target_pairs={{0,17},{1,16},{2,19},{3,18},{4,21},{5,20},{6,23},{7,22},{8,25},{9,... | collective-permute-start | bytes 466952 | tf_op jit(solution)/shard_map/ppermute | solution.py:80
  44.8 10.1 %collective-permute-start.12 = (bf16[152,512]{1,0:T(8,128)(2,1)S(1)}, bf16[152,512]{1,0:T(8,128)(2,1)S(1)}, u32[]{:S(2)}, u32[]{:S(2)}) collective-permute-start(bf16[152,512]{1,0:T(8,128)(2,1)S(1)} %get-tuple-element.111), channel_id=1, source_target_pairs={{0,1},{1,0},{2,3},{3,2},{4,5},{5,4},{6,7},{7,6},{8,9},{9,8},{10,11... | collective-permute-start | bytes 466952 | tf_op jit(solution)/shard_map/ppermute | solution.py:80
  45.8 9.2 %collective-permute-start.13 = (bf16[152,512]{1,0:T(8,128)(2,1)S(1)}, bf16[152,512]{1,0:T(8,128)(2,1)S(1)}, u32[]{:S(2)}, u32[]{:S(2)}) collective-permute-start(bf16[152,512]{1,0:T(8,128)(2,1)S(1)} %get-tuple-element.112), channel_id=1, source_target_pairs={{0,16},{1,17},{2,18},{3,19},{4,20},{5,21},{6,22},{7,23},{8,24},{9,... | collective-permute-start | bytes 466952 | tf_op jit(solution)/shard_map/ppermute | solution.py:80
  55.3 6.6 %collective-permute-start.15 = (bf16[44,512]{1,0:T(8,128)(2,1)S(1)}, bf16[44,512]{1,0:T(8,128)(2,1)S(1)}, u32[]{:S(2)}, u32[]{:S(2)}) collective-permute-start(bf16[44,512]{1,0:T(8,128)(2,1)S(1)} %get-tuple-element.108), channel_id=1, source_target_pairs={{0,4},{1,5},{2,6},{3,7},{4,0},{5,1},{6,2},{7,3},{8,12},{9,13},{10,... | collective-permute-start | bytes 135176 | tf_op jit(solution)/shard_map/ppermute | solution.py:80
  57.5 4.4 %collective-permute-start.16 = (bf16[44,512]{1,0:T(8,128)(2,1)S(1)}, bf16[44,512]{1,0:T(8,128)(2,1)S(1)}, u32[]{:S(2)}, u32[]{:S(2)}) collective-permute-start(bf16[44,512]{1,0:T(8,128)(2,1)S(1)} %get-tuple-element.109), channel_id=1, source_target_pairs={{0,2},{1,3},{2,0},{3,1},{4,6},{5,7},{6,4},{7,5},{8,10},{9,11},{10,... | collective-permute-start | bytes 135176 | tf_op jit(solution)/shard_map/ppermute | solution.py:80
  57.8 5.9 %collective-permute-start.17 = (bf16[44,512]{1,0:T(8,128)(2,1)S(1)}, bf16[44,512]{1,0:T(8,128)(2,1)S(1)}, u32[]{:S(2)}, u32[]{:S(2)}) collective-permute-start(bf16[44,512]{1,0:T(8,128)(2,1)S(1)} %get-tuple-element.110), channel_id=1, source_target_pairs={{0,6},{1,7},{2,4},{3,5},{4,2},{5,3},{6,0},{7,1},{8,14},{9,15},{10,... | collective-permute-start | bytes 135176 | tf_op jit(solution)/shard_map/ppermute | solution.py:80
  59.7 18.7 %copy-start.4 = (s32[8,128]{1,0:T(8,128)S(1)}, s32[8,128]{1,0:T(8,128)}, u32[]{:S(2)}) copy-start(s32[8,128]{1,0:T(8,128)} %rows_ref.5) | copy-start | bytes 12292
  59.7 18.7 %copy-start.5 = (s32[1,8]{1,0:T(1,128)S(1)}, s32[1,8]{1,0:T(1,128)}, u32[]{:S(2)}) copy-start(s32[1,8]{1,0:T(1,128)} %count_ref.5) | copy-start | bytes 100
  59.8 10.8 %collective-permute-start.23 = (bf16[384,512]{1,0:T(8,128)(2,1)S(1)}, bf16[384,512]{1,0:T(8,128)(2,1)S(1)}, u32[]{:S(2)}, u32[]{:S(2)}) collective-permute-start(bf16[384,512]{1,0:T(8,128)(2,1)S(1)} %pad_maximum_fusion.2), channel_id=1, source_target_pairs={{0,1},{1,0},{2,3},{3,2},{4,5},{5,4},{6,7},{7,6},{8,9},{9,8},{10,11... | collective-permute-start | bytes 1179656 | tf_op jit(solution)/shard_map/ppermute | solution.py:80
  63.7 5.8 %collective-permute-start.20 = (bf16[32,512]{1,0:T(8,128)(2,1)S(1)}, bf16[32,512]{1,0:T(8,128)(2,1)S(1)}, u32[]{:S(2)}, u32[]{:S(2)}) collective-permute-start(bf16[32,512]{1,0:T(8,128)(2,1)S(1)} %fusion), channel_id=1, source_target_pairs={{0,6},{1,7},{2,4},{3,5},{4,2},{5,3},{6,0},{7,1},{8,14},{9,15},{10,... | collective-permute-start | bytes 98312 | tf_op jit(solution)/shard_map/ppermute | solution.py:80
  65.7 4.1 %collective-permute-start.19 = (bf16[32,512]{1,0:T(8,128)(2,1)S(1)}, bf16[32,512]{1,0:T(8,128)(2,1)S(1)}, u32[]{:S(2)}, u32[]{:S(2)}) collective-permute-start(bf16[32,512]{1,0:T(8,128)(2,1)S(1)} %fusion), channel_id=1, source_target_pairs={{0,2},{1,3},{2,0},{3,1},{4,6},{5,7},{6,4},{7,5},{8,10},{9,11},{10,... | collective-permute-start | bytes 98312 | tf_op jit(solution)/shard_map/ppermute | solution.py:80
  65.7 4.8 %collective-permute-start.18 = (bf16[32,512]{1,0:T(8,128)(2,1)S(1)}, bf16[32,512]{1,0:T(8,128)(2,1)S(1)}, u32[]{:S(2)}, u32[]{:S(2)}) collective-permute-start(bf16[32,512]{1,0:T(8,128)(2,1)S(1)} %fusion), channel_id=1, source_target_pairs={{0,4},{1,5},{2,6},{3,7},{4,0},{5,1},{6,2},{7,3},{8,12},{9,13},{10,... | collective-permute-start | bytes 98312 | tf_op jit(solution)/shard_map/ppermute | solution.py:80
  70.5 9.2 %collective-permute-start.26 = (bf16[128,512]{1,0:T(8,128)(2,1)S(1)}, bf16[128,512]{1,0:T(8,128)(2,1)S(1)}, u32[]{:S(2)}, u32[]{:S(2)}) collective-permute-start(bf16[128,512]{1,0:T(8,128)(2,1)S(1)} %pad_maximum_fusion.7), channel_id=1, source_target_pairs={{0,17},{1,16},{2,19},{3,18},{4,21},{5,20},{6,23},{7,22},{8,25},{9,... | collective-permute-start | bytes 393224 | tf_op jit(solution)/shard_map/ppermute | solution.py:80
  72.6 7.1 %collective-permute-start.25 = (bf16[128,512]{1,0:T(8,128)(2,1)S(1)}, bf16[128,512]{1,0:T(8,128)(2,1)S(1)}, u32[]{:S(2)}, u32[]{:S(2)}) collective-permute-start(bf16[128,512]{1,0:T(8,128)(2,1)S(1)} %pad_maximum_fusion.7), channel_id=1, source_target_pairs={{0,16},{1,17},{2,18},{3,19},{4,20},{5,21},{6,22},{7,23},{8,24},{9,... | collective-permute-start | bytes 393224 | tf_op jit(solution)/shard_map/ppermute | solution.py:80
  73.2 6.6 %collective-permute-start.24 = (bf16[128,512]{1,0:T(8,128)(2,1)S(1)}, bf16[128,512]{1,0:T(8,128)(2,1)S(1)}, u32[]{:S(2)}, u32[]{:S(2)}) collective-permute-start(bf16[128,512]{1,0:T(8,128)(2,1)S(1)} %pad_maximum_fusion.7), channel_id=1, source_target_pairs={{0,1},{1,0},{2,3},{3,2},{4,5},{5,4},{6,7},{7,6},{8,9},{9,8},{10,11... | collective-permute-start | bytes 393224 | tf_op jit(solution)/shard_map/ppermute | solution.py:80
  74.1 6.9 %collective-permute-start.27 = (bf16[128,512]{1,0:T(8,128)(2,1)S(1)}, bf16[128,512]{1,0:T(8,128)(2,1)S(1)}, u32[]{:S(2)}, u32[]{:S(2)}) collective-permute-start(bf16[128,512]{1,0:T(8,128)(2,1)S(1)} %get-tuple-element.81), channel_id=1, source_target_pairs={{0,6},{1,7},{2,4},{3,5},{4,2},{5,3},{6,0},{7,1},{8,14},{9,15},{10,... | collective-permute-start | bytes 393224 | tf_op jit(solution)/shard_map/ppermute | solution.py:80
  76.0 7.8 %collective-permute-start.28 = (bf16[128,512]{1,0:T(8,128)(2,1)S(1)}, bf16[128,512]{1,0:T(8,128)(2,1)S(1)}, u32[]{:S(2)}, u32[]{:S(2)}) collective-permute-start(bf16[128,512]{1,0:T(8,128)(2,1)S(1)} %get-tuple-element.82), channel_id=1, source_target_pairs={{0,7},{1,6},{2,5},{3,4},{4,3},{5,2},{6,1},{7,0},{8,15},{9,14},{10,... | collective-permute-start | bytes 393224 | tf_op jit(solution)/shard_map/ppermute | solution.py:80
  78.5 5.3 %copy-start.6 = (s32[4]{0:T(128)S(1)}, s32[4]{0:T(128)}, u32[]{:S(2)}) copy-start(s32[4]{0:T(128)} %hub_ref.3) | copy-start | bytes 52
  83.7 1.9 %collective-permute-start.29 = (bf16[512,512]{1,0:T(8,128)(2,1)S(1)}, bf16[512,512]{1,0:T(8,128)(2,1)S(1)}, u32[]{:S(2)}, u32[]{:S(2)}) collective-permute-start(bf16[512,512]{1,0:T(8,128)(2,1)S(1)} %pad_maximum_fusion.x_ref), channel_id=1, source_target_pairs={{0,8},{1,9},{2,10},{3,11},{4,12},{5,13},{6,14},{7,15},{8,0},{9,1},... | collective-permute-start | bytes 1572872 | tf_op jit(solution)/shard_map/ppermute | solution.py:80
